TPU v7x, 32 devices: a whole 2x2x4 slice. The times are simulated.
32 devices in a mesh: dp: 8 (over y, x, core), ep: 4 (over z).
Axes of the slice: x: 2, y: 2, z: 4, core: 2. Of those that a mesh axis runs over, the one named last changes fastest.
Arguments:
- frames: float32 [2, 8192, 512], P(None, ('dp', 'ep')), may hold values from -6 to 6
- embedding: float32 [2, 8192, 512], P(None, ('dp', 'ep')), may hold values from -6 to 6
- cotangent: float32 [2, 8192, 512], P(None, ('dp', 'ep')), may hold values from -6 to 6
- expert_ids: int32 [2, 2, 8192, 1], P(None, None, ('dp', 'ep')), may hold values from 0 to 3; in each aligned block of 256 rows (0 to 255, 256 to 511, ..., all dimensions but the last counted through in order) at most 128 rows name the same one
- lengths: int32 [2, 8], replicated, may hold values from 256 to 1024, as said below
- norm_gain: float32 [5, 512], replicated, may hold values from 0.5 to 1.5
- norm_bias: float32 [5, 512], replicated, may hold values from -1.8 to 1.8
- router: float32 [2, 512, 4], replicated, may hold values from -0.125 to 0.125
- attention_in: bfloat16 [512, 1536], replicated, may hold values from -0.25 to 0.25
- attention_out: bfloat16 [512, 512], replicated, may hold values from -1 to 1
- slopes: float32 [8], replicated, may hold values from 0.0005 to 0.1
- conv_point: bfloat16 [512, 1024], replicated, may hold values from -0.25 to 0.25
- conv_depth: float32 [15, 512], replicated, may hold values from -1.5 to 1.5
- batch_gain: float32 [512], replicated, may hold values from 0.5 to 1.5
- batch_bias: float32 [512], replicated, may hold values from -1.8 to 1.8
- conv_out: bfloat16 [512, 512], replicated, may hold values from -0.25 to 0.25
- expert_in: bfloat16 [2, 4, 512, 2048], P(None, 'ep'), may hold values from -0.25 to 0.25
- expert_out: bfloat16 [2, 4, 2048, 512], P(None, 'ep'), may hold values from -1.5 to 1.5
Outputs:
- output: float32 [2, 8192, 512], P(None, ('dp', 'ep'))
- frames_grad: float32 [2, 8192, 512], P(None, ('dp', 'ep'))
- norm_gain_grad: float32 [5, 512], replicated
- norm_bias_grad: float32 [5, 512], replicated
- router_grad: float32 [2, 512, 4], replicated
- attention_in_grad: float32 [512, 1536], replicated
- attention_out_grad: float32 [512, 512], replicated
- slopes_grad: float32 [8], replicated
- conv_point_grad: float32 [512, 1024], replicated
- conv_depth_grad: float32 [15, 512], replicated
- batch_gain_grad: float32 [512], replicated
- batch_bias_grad: float32 [512], replicated
- conv_out_grad: float32 [512, 512], replicated
- expert_in_grad: float32 [2, 4, 512, 2048], P(None, 'ep')
- expert_out_grad: float32 [2, 4, 2048, 512], P(None, 'ep')
Inputs may be any that keep to these rules, and one draw needn't show every extreme that they name: `expert_ids`: in every aligned block of 256 rows (the frames of one device for one block and micro-batch) no expert is named more than 128 times, a bound that some block reaches. `lengths`: in every micro-batch one utterance, drawn from the seed, is valid in all its frames.
All inputs are finite; a program needn't handle non-finite values.
Results may differ from a plain program's by a relative error of at most 0.0003.
Values sent between devices are 32-bit elements; how exact they have to be, the bound alone decides.
No kernel may reach another device: no remote copies, remote signals or barrier semaphores. Data moves between devices by JAX's collectives and lax.ppermute only.
A program may use at most 384 MiB of HBM per device.

v0:
```python
import math

import jax
import jax.numpy as jnp
from jax import lax
from jax.sharding import PartitionSpec as P

HIGH = lax.Precision.HIGHEST
EPS = 1e-05
MASKED = -1e30


def padded_2(shard, sides, width):
    for axis, dim in sides:
        count, length = (lax.axis_size(axis), shard.shape[dim])
        up = [(i, (i + 1) % count) for i in range(count - 1)]
        down = [(j, i) for i, j in up]
        last = lax.slice_in_dim(shard, length - width, length, axis=dim)
        leading = lax.slice_in_dim(shard, 0, width, axis=dim)
        before = lax.ppermute(last, axis, up)
        after = lax.ppermute(leading, axis, down)
        shard = jnp.concatenate([before, shard, after], axis=dim)
    return shard


def product(left, right):
    return jnp.matmul(left, right, precision=HIGH)


def norm_rows(values, gain, shift):
    center = values - jnp.mean(values, axis=-1, keepdims=True)
    spread = jnp.mean(center * center, axis=-1, keepdims=True)
    return center * lax.rsqrt(spread + EPS) * gain + shift


def swish_slope(values):
    squash = jax.nn.sigmoid(values)
    return squash * (1.0 + values * (1.0 - squash))


def dispatch_table(ids, experts, capacity):
    counted = (ids[:, None] == jnp.arange(experts, dtype=jnp.int32)[None, :]).astype(jnp.int32)
    rank = jnp.sum((jnp.cumsum(counted, axis=0, dtype=jnp.int32) - 1) * counted, axis=1)
    slot = ids * capacity + rank
    table = (jnp.arange(experts * capacity, dtype=jnp.int32)[:, None] == slot[None, :]).astype(
        jnp.float32
    )
    return (counted.astype(jnp.float32), table)


def mixture_forward(hidden, embed_rows, ids, gain, shift, router, weight_in, weight_out, capacity):
    experts = router.shape[1]
    width = hidden.shape[1]
    onehot, table = dispatch_table(ids, experts, capacity)

    def mixture_front(source, gain_now, shift_now, router_now):
        normed = norm_rows(source, gain_now, shift_now)
        probs = jax.nn.softmax(product(normed + embed_rows, router_now), axis=-1)
        return (normed, jnp.sum(probs * onehot, axis=-1))

    (normed, gate), front_pull = jax.vjp(mixture_front, hidden, gain, shift, router)
    send = product(table, normed).reshape(experts, capacity, width)
    received = lax.all_to_all(send, "ep", split_axis=0, concat_axis=0, tiled=True)
    pre = product(received, weight_in)
    result, pre, received = (product(jax.nn.silu(pre), weight_out), pre, received)
    back = lax.all_to_all(result, "ep", split_axis=0, concat_axis=0, tiled=True)
    mixed = jnp.einsum("sr,sd->rd", table, back.reshape(experts * capacity, width), precision=HIGH)
    new = hidden + 0.5 * gate[:, None] * mixed
    return (new, (front_pull, table, gate, mixed, pre, received))


def mixture_backward(grad, saved, weight_in, weight_out, experts, capacity):
    front_pull, table, gate, mixed, pre, received = saved
    width = grad.shape[1]
    grad_mixed = 0.5 * gate[:, None] * grad
    grad_gate = 0.5 * jnp.sum(grad * mixed, axis=1)
    grad_back = product(table, grad_mixed).reshape(experts, capacity, width)
    grad_result = lax.all_to_all(grad_back, "ep", split_axis=0, concat_axis=0, tiled=True)
    activated = jax.nn.silu(pre)
    outer_grad = jnp.einsum("scf,scd->fd", activated, grad_result, precision=HIGH)
    grad_active = jnp.einsum("scd,fd->scf", grad_result, weight_out, precision=HIGH)
    grad_pre = grad_active * swish_slope(pre)
    inner_grad = jnp.einsum("scd,scf->df", received, grad_pre, precision=HIGH)
    grad_received = jnp.einsum("scf,df->scd", grad_pre, weight_in, precision=HIGH)
    grad_send = lax.all_to_all(grad_received, "ep", split_axis=0, concat_axis=0, tiled=True)
    grad_normed = jnp.einsum(
        "sr,sd->rd", table, grad_send.reshape(experts * capacity, width), precision=HIGH
    )
    grad_hidden, gain_grad, shift_grad, router_grad = front_pull((grad_normed, grad_gate))
    return (grad + grad_hidden, gain_grad, shift_grad, router_grad, inner_grad, outer_grad)


def attention_scores(query, keys, slopes, place, length, heads):
    rows = query.shape[0]
    total_keys = keys.shape[0]
    head_size = query.shape[1] // heads
    query_heads = query.reshape(rows, heads, head_size)
    key_heads = keys.reshape(total_keys, heads, head_size)
    key_place = jnp.arange(total_keys, dtype=jnp.int32)
    distance = jnp.abs(place[:, None] - key_place[None, :]).astype(jnp.float32)
    raw = (
        jnp.einsum("qhc,khc->hqk", query_heads, key_heads, precision=HIGH) / math.sqrt(head_size)
        - slopes[:, None, None] * distance[None]
    )
    return (jnp.where((key_place < length)[None, None, :], raw, MASKED), distance)


def attention_forward(hidden, gain, shift, weight_in, weight_out, slopes, place, length, heads):
    rows, width = hidden.shape

    def attention_front(source, gain_now, shift_now, weight_now):
        return product(norm_rows(source, gain_now, shift_now), weight_now)

    packed, front_pull = jax.vjp(attention_front, hidden, gain, shift, weight_in)
    query = packed[:, :width]
    keys, values = (
        lax.all_gather(packed[:, width : 2 * width], "ep", axis=0, tiled=True),
        lax.all_gather(packed[:, 2 * width :], "ep", axis=0, tiled=True),
    )
    scores, distance = attention_scores(query, keys, slopes, place, length, heads)
    highest = jnp.max(scores, axis=2, keepdims=True)
    raised = jnp.exp(scores - highest)
    total = jnp.sum(raised, axis=2, keepdims=True)
    probs = raised / total
    logsum = highest + jnp.log(total)
    value_heads = values.reshape(keys.shape[0], heads, width // heads)
    mixed = jnp.einsum("hqk,khc->qhc", probs, value_heads, precision=HIGH).reshape(rows, width)
    new = hidden + product(mixed, weight_out)
    return (new, (front_pull, query, keys, values, logsum, mixed))


def attention_backward(grad, saved, weight_out, slopes, place, length, heads):
    front_pull, query, keys, values, logsum, mixed = saved
    rows, width = query.shape
    head_size = width // heads
    total_keys = keys.shape[0]
    mixing_grad = product(mixed.T, grad)
    grad_mixed = product(grad, weight_out.T)
    scores, distance = attention_scores(query, keys, slopes, place, length, heads)
    probs = jnp.exp(scores - logsum)
    grad_heads = grad_mixed.reshape(rows, heads, head_size)
    mixed_heads = mixed.reshape(rows, heads, head_size)
    value_heads = values.reshape(total_keys, heads, head_size)
    key_heads = keys.reshape(total_keys, heads, head_size)
    query_heads = query.reshape(rows, heads, head_size)
    grad_values = jnp.einsum("hqk,qhc->khc", probs, grad_heads, precision=HIGH).reshape(
        total_keys, width
    )
    grad_probs = jnp.einsum("qhc,khc->hqk", grad_heads, value_heads, precision=HIGH)
    row_dot = jnp.sum(grad_heads * mixed_heads, axis=2).T
    grad_scores = probs * (grad_probs - row_dot[:, :, None])
    slope_grad = -jnp.sum(grad_scores * distance[None], axis=(1, 2))
    grad_query = (
        jnp.einsum("hqk,khc->qhc", grad_scores, key_heads, precision=HIGH) / math.sqrt(head_size)
    ).reshape(rows, width)
    grad_keys = (
        jnp.einsum("hqk,qhc->khc", grad_scores, query_heads, precision=HIGH) / math.sqrt(head_size)
    ).reshape(total_keys, width)
    grad_key, grad_value = (
        lax.psum_scatter(grad_keys, "ep", scatter_dimension=0, tiled=True),
        lax.psum_scatter(grad_values, "ep", scatter_dimension=0, tiled=True),
    )
    grad_packed = jnp.concatenate([grad_query, grad_key, grad_value], axis=1)
    grad_hidden, gain_grad, shift_grad, packed_grad = front_pull(grad_packed)
    return (grad + grad_hidden, gain_grad, shift_grad, packed_grad, mixing_grad, slope_grad)


def conv_forward(hidden, valid_f, gain, shift, point, depth):
    rows, width = hidden.shape

    def conv_front(source, gain_now, shift_now, point_now):
        both = product(norm_rows(source, gain_now, shift_now), point_now)
        return both[:, :width] * jax.nn.sigmoid(both[:, width:]) * valid_f

    gated, front_pull = jax.vjp(conv_front, hidden, gain, shift, point)
    half = depth.shape[0] // 2
    padded = padded_2(gated, (("ep", 0),), half)
    total = depth[0] * padded[0:rows]
    for offset in range(1, depth.shape[0]):
        total = total + depth[offset] * padded[offset : offset + rows]
    return (total, padded, front_pull)


def conv_backward(grad_conv, padded, front_pull, depth):
    rows = grad_conv.shape[0]
    kernel = depth.shape[0]
    half = kernel // 2
    grad_pad = padded_2(grad_conv, (("ep", 0),), half)
    grad_gated = depth[0] * grad_pad[2 * half : 2 * half + rows]
    for offset in range(1, kernel):
        grad_gated = (
            grad_gated + depth[offset] * grad_pad[2 * half - offset : 2 * half - offset + rows]
        )
    depth_grad = jnp.stack(
        [jnp.sum(grad_conv * padded[offset : offset + rows], axis=0) for offset in range(kernel)]
    )
    grad_hidden, gain_grad, shift_grad, point_grad = front_pull(grad_gated)
    return (grad_hidden, gain_grad, shift_grad, point_grad, depth_grad)


def body(
    frames,
    embedding,
    cotangent,
    expert_ids,
    lengths,
    norm_gain,
    norm_bias,
    router,
    attention_in,
    attention_out,
    slopes,
    conv_point,
    conv_depth,
    batch_gain,
    batch_bias,
    conv_out,
    expert_in,
    expert_out,
):
    packed_weight = attention_in.astype(jnp.float32)
    mixing_weight = attention_out.astype(jnp.float32)
    point_weight = conv_point.astype(jnp.float32)
    project_weight = conv_out.astype(jnp.float32)
    inner_weight = expert_in.astype(jnp.float32)
    outer_weight = expert_out.astype(jnp.float32)
    micro, rows, width = frames.shape
    experts = router.shape[2]
    heads = slopes.shape[0]
    capacity = 2 * rows // experts
    place = lax.axis_index("ep") * rows + jnp.arange(rows, dtype=jnp.int32)
    group = lax.axis_index("dp")
    outputs = []
    frame_grads = []
    dense_sum = None
    expert_sum = None
    batch_sum = None
    for step in range(micro):
        length = lengths[step, group]
        count = jnp.sum(lengths[step]).astype(jnp.float32)
        valid_f = (place < length).astype(jnp.float32)[:, None]
        first, kept_first = mixture_forward(
            frames[step],
            embedding[step],
            expert_ids[0, step, :, 0],
            norm_gain[0],
            norm_bias[0],
            router[0],
            inner_weight[0, 0],
            outer_weight[0, 0],
            capacity,
        )
        second, kept_attention = attention_forward(
            first,
            norm_gain[1],
            norm_bias[1],
            packed_weight,
            mixing_weight,
            slopes,
            place,
            length,
            heads,
        )
        conv, padded, conv_pull = conv_forward(
            second, valid_f, norm_gain[2], norm_bias[2], point_weight, conv_depth
        )
        stat_sum, square_sum = lax.psum(
            (jnp.sum(conv * valid_f, axis=0), jnp.sum(conv * conv * valid_f, axis=0)), ("dp", "ep")
        )
        centre = stat_sum / count
        inverse_dev = lax.rsqrt(square_sum / count - centre * centre + EPS)
        scaled = (conv - centre) * inverse_dev
        shaped = scaled * batch_gain + batch_bias
        swished = jax.nn.silu(shaped)
        third = second + product(swished, project_weight)
        fourth, kept_second = mixture_forward(
            third,
            embedding[step],
            expert_ids[1, step, :, 0],
            norm_gain[3],
            norm_bias[3],
            router[1],
            inner_weight[1, 0],
            outer_weight[1, 0],
            capacity,
        )

        def final(source, gain_now, shift_now):
            return norm_rows(source, gain_now, shift_now) * valid_f

        result, final_pull = jax.vjp(final, fourth, norm_gain[4], norm_bias[4])
        outputs.append(result)
        grad_fourth, gain_four, shift_four = final_pull(cotangent[step])
        grad_third, gain_three, shift_three, router_one, inner_one, outer_one = mixture_backward(
            grad_fourth, kept_second, inner_weight[1, 0], outer_weight[1, 0], experts, capacity
        )
        project_grad = product(swished.T, grad_third)
        grad_shaped = product(grad_third, project_weight.T) * swish_slope(shaped)
        shift_total, gain_total = lax.psum(
            (jnp.sum(grad_shaped, axis=0), jnp.sum(grad_shaped * scaled, axis=0)), ("dp", "ep")
        )
        grad_conv = (
            batch_gain
            * inverse_dev
            * (grad_shaped - valid_f * (shift_total + scaled * gain_total) / count)
        )
        grad_hidden, gain_two, shift_two, point_grad, depth_grad = conv_backward(
            grad_conv, padded, conv_pull, conv_depth
        )
        grad_second = grad_third + grad_hidden
        grad_first, gain_one, shift_one, packed_grad, mixing_grad, slope_grad = attention_backward(
            grad_second, kept_attention, mixing_weight, slopes, place, length, heads
        )
        grad_frames, gain_zero, shift_zero, router_zero, inner_zero, outer_zero = mixture_backward(
            grad_first, kept_first, inner_weight[0, 0], outer_weight[0, 0], experts, capacity
        )
        frame_grads.append(grad_frames)
        gain_grad = jnp.stack([gain_zero, gain_one, gain_two, gain_three, gain_four])
        shift_grad = jnp.stack([shift_zero, shift_one, shift_two, shift_three, shift_four])
        router_grad = jnp.stack([router_zero, router_one])
        inner_grad = jnp.stack([inner_zero, inner_one])[:, None]
        outer_grad = jnp.stack([outer_zero, outer_one])[:, None]
        (
            gain_grad,
            shift_grad,
            router_grad,
            packed_grad,
            mixing_grad,
            slope_grad,
            point_grad,
            depth_grad,
            project_grad,
        ) = lax.psum(
            (
                gain_grad,
                shift_grad,
                router_grad,
                packed_grad,
                mixing_grad,
                slope_grad,
                point_grad,
                depth_grad,
                project_grad,
            ),
            ("dp", "ep"),
        )
        inner_grad, outer_grad = lax.psum((inner_grad, outer_grad), "dp")
        dense_now = (
            gain_grad,
            shift_grad,
            router_grad,
            packed_grad,
            mixing_grad,
            slope_grad,
            point_grad,
            depth_grad,
            project_grad,
        )
        expert_now = (inner_grad, outer_grad)
        batch_now = (gain_total, shift_total)
        if step == 0:
            dense_sum, expert_sum, batch_sum = (dense_now, expert_now, batch_now)
        else:
            dense_sum = jax.tree.map(jnp.add, dense_sum, dense_now)
            expert_sum = jax.tree.map(jnp.add, expert_sum, expert_now)
            batch_sum = jax.tree.map(jnp.add, batch_sum, batch_now)
    (
        gain_grad,
        shift_grad,
        router_grad,
        packed_grad,
        mixing_grad,
        slope_grad,
        point_grad,
        depth_grad,
        project_grad,
    ) = dense_sum
    inner_grad, outer_grad = expert_sum
    return (
        jnp.stack(outputs),
        jnp.stack(frame_grads),
        gain_grad,
        shift_grad,
        router_grad,
        packed_grad,
        mixing_grad,
        slope_grad,
        point_grad,
        depth_grad,
        batch_sum[0],
        batch_sum[1],
        project_grad,
        inner_grad,
        outer_grad,
    )


def solution(mesh):
    placed = (
        P(None, ("dp", "ep"), None),
        P(None, ("dp", "ep"), None),
        P(None, ("dp", "ep"), None),
        P(None, None, ("dp", "ep"), None),
        P(),
        P(),
        P(),
        P(),
        P(),
        P(),
        P(),
        P(),
        P(),
        P(),
        P(),
        P(),
        P(None, "ep", None, None),
        P(None, "ep", None, None),
    )
    return jax.shard_map(
        body,
        mesh=mesh,
        in_specs=placed,
        out_specs=(
            P(None, ("dp", "ep"), None),
            P(None, ("dp", "ep"), None),
            P(),
            P(),
            P(),
            P(),
            P(),
            P(),
            P(),
            P(),
            P(),
            P(),
            P(),
            P(None, "ep", None, None),
            P(None, "ep", None, None),
        ),
        check_vma=False,
    )
```

profile of v0, /device:TPU:0, one launch (start us, length us, event | category | flops | bytes accessed | tf_op | source)
XLA Modules:
  0.0 1595.5 jit_solution(3335051829315095628)
XLA Ops:
  27.1 22.4 %all-to-all-done.4 = f32[4,128,512]{2,1,0:T(8,128)} async-done(((f32[4,128,512]{2,1,0:T(8,128)}), f32[4,128,512]{2,1,0:T(8,128)}, u32[]{:S(2)}, u32[]{:S(2)}) %all-to-all-start.4) | async-done | bytes 1048608 | tf_op jit(solution)/shard_map/all_to_all | solution.py:63
  66.3 12.7 all-to-all-done
  96.1 12.7 all-to-all-done.5
  119.5 18.8 %all-to-all-done.1 = f32[4,128,512]{2,1,0:T(8,128)} async-done(((f32[4,128,512]{2,1,0:T(8,128)}), f32[4,128,512]{2,1,0:T(8,128)}, u32[]{:S(2)}, u32[]{:S(2)}) %all-to-all-start.1) | async-done | bytes 1048608 | tf_op jit(solution)/shard_map/all_to_all | solution.py:66
  160.5 29.0 %all-gather.11.cloned.1.call-done = f32[1024,512]{1,0:T(8,128)} async-done(((f32[256,512]{1,0:T(8,128)}), f32[1024,512]{1,0:T(8,128)}) %all-gather.11.cloned.1.call-update) | async-done | bytes 2097168 | tf_op jit(solution)/shard_map/all_gather | solution.py:117
  207.8 28.5 %all-gather.9.cloned.1.call-done = f32[1024,512]{1,0:T(8,128)} async-done(((f32[256,512]{1,0:T(8,128)}), f32[1024,512]{1,0:T(8,128)}) %all-gather.9.cloned.1.call-update) | async-done | bytes 2097168 | tf_op jit(solution)/shard_map/all_gather | solution.py:118
  239.3 11.1 fusion.4
  257.4 26.0 %all-gather.7.cloned.1.call-done = f32[1024,512]{1,0:T(8,128)} async-done(((f32[256,512]{1,0:T(8,128)}), f32[1024,512]{1,0:T(8,128)}) %all-gather.7.cloned.1.call-update) | async-done | bytes 2097168 | tf_op jit(solution)/shard_map/all_gather | solution.py:117
  301.9 28.2 %all-gather.5.cloned.1.call-done = f32[1024,512]{1,0:T(8,128)} async-done(((f32[256,512]{1,0:T(8,128)}), f32[1024,512]{1,0:T(8,128)}) %all-gather.5.cloned.1.call-update) | async-done | bytes 2097168 | tf_op jit(solution)/shard_map/all_gather | solution.py:118
  333.0 11.1 fusion.6
  357.1 40.4 %all-reduce.6 = (f32[512]{0:T(512)S(1)}, f32[512]{0:T(512)S(1)}, f32[512]{0:T(512)S(1)}, f32[512]{0:T(512)S(1)}) all-reduce(f32[512]{0:T(512)S(1)} %get-tuple-element.110, f32[512]{0:T(512)S(1)} %get-tuple-element.109, f32[512]{0:T(512)S(1)} %get-tuple-element.108, ...), channel_id=1, replica_groups=mesh['dp'=8,'ep'=4] {'dp','ep'}, use_global_device_ids=true, to_apply=%region_47.48 | all-reduce | flops 2048 | bytes 16384 | tf_op jit(solution)/shard_map/psum | solution.py:267
  411.1 20.6 %all-to-all-done.2 = f32[4,128,512]{2,1,0:T(8,128)} async-done(((f32[4,128,512]{2,1,0:T(8,128)}), f32[4,128,512]{2,1,0:T(8,128)}, u32[]{:S(2)}, u32[]{:S(2)}) %all-to-all-start.2) | async-done | bytes 1048608 | tf_op jit(solution)/shard_map/all_to_all | solution.py:63
  480.4 11.0 all-to-all-done.3
  499.7 21.3 %all-to-all-done.7 = f32[4,128,512]{2,1,0:T(8,128)} async-done(((f32[4,128,512]{2,1,0:T(8,128)}), f32[4,128,512]{2,1,0:T(8,128)}, u32[]{:S(2)}, u32[]{:S(2)}) %all-to-all-start.7) | async-done | bytes 1048608 | tf_op jit(solution)/shard_map/all_to_all | solution.py:66
  537.4 22.5 %all-to-all-done.12 = f32[4,128,512]{2,1,0:T(8,128)} async-done(((f32[4,128,512]{2,1,0:T(8,128)}), f32[4,128,512]{2,1,0:T(8,128)}, u32[]{:S(2)}, u32[]{:S(2)}) %all-to-all-start.12) | async-done | bytes 1048608 | tf_op jit(solution)/shard_map/all_to_all | solution.py:78
  578.0 11.6 all-to-all-done.8
  630.5 18.4 %all-to-all-done.9 = f32[4,128,512]{2,1,0:T(8,128)} async-done(((f32[4,128,512]{2,1,0:T(8,128)}), f32[4,128,512]{2,1,0:T(8,128)}, u32[]{:S(2)}, u32[]{:S(2)}) %all-to-all-start.9) | async-done | bytes 1048608 | tf_op jit(solution)/shard_map/all_to_all | solution.py:85
  658.0 37.7 %all-reduce.5 = (f32[512]{0:T(512)S(1)}, f32[512]{0:T(512)S(1)}, f32[512]{0:T(512)S(1)}, f32[512]{0:T(512)S(1)}) all-reduce(f32[512]{0:T(512)S(1)} %get-tuple-element.122, f32[512]{0:T(512)S(1)} %get-tuple-element.121, f32[512]{0:T(512)S(1)} %get-tuple-element.120, ...), channel_id=1, replica_groups=mesh['dp'=8,'ep'=4] {'dp','ep'}, use_global_device_ids=true, to_apply=%region_88.89 | all-reduce | flops 2048 | bytes 16384 | tf_op jit(solution)/shard_map/psum | solution.py:299
  732.7 16.0 %subtract_multiply_fusion = f32[8,256,1024]{2,1,0:T(8,128)S(1)} fusion(f32[8,256,1024]{2,1,0:T(8,128)} %copy-done.2, f32[8,256]{1,0:T(8,128)S(1)} %bitcast.653, f32[8,256]{1,0:T(8,128)S(1)} %log_add_fusion, f32[256,8,64]{0,2,1:T(8,128)} %bitcast.508, f32[1024,8,64]{0,2,1:T(8,128)} %bitcast.504), kind=kOutput, calls=%fused_computation.10 | convolution fusion | flops 1616904192 | bytes 19415040 | tf_op jit(solution)/shard_map/qhc,khc->hqk/dot_general | solution.py:149
  759.4 10.9 fusion.10
  774.0 11.4 convolution_bitcast_fusion.2
  785.5 12.4 multiply_reduce_fusion.1
  807.9 10.4 convolution_bitcast_fusion.6
  818.3 17.2 %convolution_bitcast_fusion = f32[1,2048,512]{2,1,0:T(8,128)} fusion(f32[4,128,512]{2,1,0:T(8,128)} %all-to-all-done.12, f32[4,128,2048]{2,1,0:T(8,128)S(1)} %copy-done.85), kind=kOutput, calls=%fused_computation.43 | convolution fusion | flops 6446645248 | bytes 9437184 | tf_op jit(solution)/shard_map/scf,scd->fd/dot_general | solution.py:80
  851.7 11.7 convolution_multiply_fusion.4
  877.5 37.1 %reduce-scatter.5.cloned.1.call-done = f32[256,512]{0,1:T(8,128)} async-done(((f32[1024,512]{0,1:T(8,128)}), f32[256,512]{0,1:T(8,128)}) %reduce-scatter.5.cloned.1.call-update) | async-done | bytes 524304 | tf_op jit(solution)/shard_map/reduce_scatter | solution.py:160
  939.2 14.5 all-to-all-done.14
  971.0 11.4 all-to-all-done.10
  999.8 12.2 all-to-all-done.15
  1114.4 53.2 %all-reduce.13.cloned.1.call-done = (f32[5,512]{1,0:T(8,128)}, f32[5,512]{1,0:T(8,128)}, f32[2,512,4]{1,2,0:T(4,128)}, f32[8]{0:T(128)}, f32[15,512]{1,0:T(8,128)}) async-done(((f32[5,512]{1,0:T(8,128)}, f32[5,512]{1,0:T(8,128)}, f32[2,512,4]{1,2,0:T(4,128)}, f32[8]{0:T(128)}, f32[15,512]{1,0:T(8,128)}), (f32[5,512]{1,0:T(8,128)}, f32[5,512]{1,0:T(8,128)}, f32[2,512,4]{1,2,0:T(4,128)}, f32[8]{0:T(128)}, ...) | async-done | bytes 67632 | tf_op jit(solution)/shard_map/psum | solution.py:333
  1167.7 176.3 %all-reduce.15.cloned.1.call-done = (f32[512,1536]{1,0:T(8,128)}, f32[512,512]{1,0:T(8,128)}, f32[512,1024]{1,0:T(8,128)}, f32[512,512]{1,0:T(8,128)}) async-done(((f32[512,1536]{1,0:T(8,128)}, f32[512,512]{1,0:T(8,128)}, f32[512,1024]{1,0:T(8,128)}, f32[512,512]{1,0:T(8,128)}), (f32[512,1536]{1,0:T(8,128)}, f32[512,512]{1,0:T(8,128)}, f32[512,1024]{1,0:T(8,128)}, ...) | async-done | bytes 7340048 | tf_op jit(solution)/shard_map/psum | solution.py:333
  1343.9 223.0 %all-reduce.17.cloned.1.call-done = (f32[2,1,512,2048]{3,2,0,1:T(8,128)}, f32[2,1,2048,512]{3,2,0,1:T(8,128)}) async-done(((f32[2,1,512,2048]{3,2,0,1:T(8,128)}, f32[2,1,2048,512]{3,2,0,1:T(8,128)}), (f32[2,1,512,2048]{3,2,0,1:T(8,128)}, f32[2,1,2048,512]{3,2,0,1:T(8,128)})) %all-reduce.17.cloned.1.call-update) | async-done | bytes 16777232 | tf_op jit(solution)/shard_map/psum | solution.py:347
  (723 shorter events, 575.3 us)
Async XLA Ops:
  17.3 32.1 %all-to-all-start.4 = ((f32[4,128,512]{2,1,0:T(8,128)}), f32[4,128,512]{2,1,0:T(8,128)}, u32[]{:S(2)}, u32[]{:S(2)}) async-start(f32[4,128,512]{2,1,0:T(8,128)} %fusion.195), calls=%async_computation.4 | async-start | bytes 2097152 | tf_op jit(solution)/shard_map/all_to_all | solution.py:63
  49.5 29.5 %all-to-all-start = ((f32[4,128,512]{2,1,0:T(8,128)}), f32[4,128,512]{2,1,0:T(8,128)}, u32[]{:S(2)}, u32[]{:S(2)}) async-start(f32[4,128,512]{2,1,0:T(8,128)} %fusion.200), calls=%async_computation | async-start | bytes 2097152 | tf_op jit(solution)/shard_map/all_to_all | solution.py:63
  79.0 29.7 %all-to-all-start.5 = ((f32[4,128,512]{2,1,0:T(8,128)}), f32[4,128,512]{2,1,0:T(8,128)}, u32[]{:S(2)}, u32[]{:S(2)}) async-start(f32[4,128,512]{2,1,0:T(8,128)} %fusion.38), calls=%async_computation.5 | async-start | bytes 2097152 | tf_op jit(solution)/shard_map/all_to_all | solution.py:66
  108.7 29.5 %all-to-all-start.1 = ((f32[4,128,512]{2,1,0:T(8,128)}), f32[4,128,512]{2,1,0:T(8,128)}, u32[]{:S(2)}, u32[]{:S(2)}) async-start(f32[4,128,512]{2,1,0:T(8,128)} %fusion.40), calls=%async_computation.1 | async-start | bytes 2097152 | tf_op jit(solution)/shard_map/all_to_all | solution.py:66
  113.0 76.5 %all-gather.11.cloned.1.call-start = ((), (), s32[]{:S(2)}) async-start(), calls=%async_computation.23 | async-start | bytes 2621440 | tf_op jit(solution)/shard_map/all_gather | solution.py:117
  144.4 91.9 %all-gather.9.cloned.1.call-start = ((), (), s32[]{:S(2)}) async-start(), calls=%async_computation.22 | async-start | bytes 2621440 | tf_op jit(solution)/shard_map/all_gather | solution.py:118
  145.1 138.3 %all-gather.7.cloned.1.call-start = ((), (), s32[]{:S(2)}) async-start(), calls=%async_computation.21 | async-start | bytes 2621440 | tf_op jit(solution)/shard_map/all_gather | solution.py:117
  148.5 181.6 %all-gather.5.cloned.1.call-start = ((), (), s32[]{:S(2)}) async-start(), calls=%async_computation.20 | async-start | bytes 2621440 | tf_op jit(solution)/shard_map/all_gather | solution.py:118
  254.4 96.7 %collective-permute-start.2 = (f32[7,512]{1,0:T(8,128)S(1)}, f32[7,512]{1,0:T(8,128)S(1)}, u32[]{:S(2)}, u32[]{:S(2)}) collective-permute-start(f32[7,512]{1,0:T(8,128)S(1)} %get-tuple-element.210), channel_id=1, source_target_pairs={{0,1},{1,2},{2,3},{4,5},{5,6},{6,7},{8,9},{9,10},{10,11},{12,13},{... | collective-permute-start | bytes 43016 | tf_op jit(solution)/shard_map/ppermute | solution.py:20
  256.1 95.0 %collective-permute-start.3 = (f32[7,512]{1,0:T(8,128)S(1)}, f32[7,512]{1,0:T(8,128)S(1)}, u32[]{:S(2)}, u32[]{:S(2)}) collective-permute-start(f32[7,512]{1,0:T(8,128)S(1)} %get-tuple-element.211), channel_id=1, source_target_pairs={{1,0},{2,1},{3,2},{5,4},{6,5},{7,6},{9,8},{10,9},{11,10},{13,12},{... | collective-permute-start | bytes 43016 | tf_op jit(solution)/shard_map/ppermute | solution.py:21
  402.3 29.5 %all-to-all-start.2 = ((f32[4,128,512]{2,1,0:T(8,128)}), f32[4,128,512]{2,1,0:T(8,128)}, u32[]{:S(2)}, u32[]{:S(2)}) async-start(f32[4,128,512]{2,1,0:T(8,128)} %bitcast.518), calls=%async_computation.2 | async-start | bytes 2097152 | tf_op jit(solution)/shard_map/all_to_all | solution.py:63
  431.8 29.9 %all-to-all-start.6 = ((f32[4,128,512]{2,1,0:T(8,128)}), f32[4,128,512]{2,1,0:T(8,128)}, u32[]{:S(2)}, u32[]{:S(2)}) async-start(f32[4,128,512]{2,1,0:T(8,128)} %bitcast.519), calls=%async_computation.6 | async-start | bytes 2097152 | tf_op jit(solution)/shard_map/all_to_all | solution.py:63
  461.7 29.7 %all-to-all-start.3 = ((f32[4,128,512]{2,1,0:T(8,128)}), f32[4,128,512]{2,1,0:T(8,128)}, u32[]{:S(2)}, u32[]{:S(2)}) async-start(f32[4,128,512]{2,1,0:T(8,128)} %fusion.26), calls=%async_computation.3 | async-start | bytes 2097152 | tf_op jit(solution)/shard_map/all_to_all | solution.py:66
  491.4 29.5 %all-to-all-start.7 = ((f32[4,128,512]{2,1,0:T(8,128)}), f32[4,128,512]{2,1,0:T(8,128)}, u32[]{:S(2)}, u32[]{:S(2)}) async-start(f32[4,128,512]{2,1,0:T(8,128)} %fusion.24), calls=%async_computation.7 | async-start | bytes 2097152 | tf_op jit(solution)/shard_map/all_to_all | solution.py:66
  530.3 29.5 %all-to-all-start.12 = ((f32[4,128,512]{2,1,0:T(8,128)}), f32[4,128,512]{2,1,0:T(8,128)}, u32[]{:S(2)}, u32[]{:S(2)}) async-start(f32[4,128,512]{2,1,0:T(8,128)} %bitcast.520), calls=%async_computation.14 | async-start | bytes 2097152 | tf_op jit(solution)/shard_map/all_to_all | solution.py:78
  559.9 29.7 %all-to-all-start.8 = ((f32[4,128,512]{2,1,0:T(8,128)}), f32[4,128,512]{2,1,0:T(8,128)}, u32[]{:S(2)}, u32[]{:S(2)}) async-start(f32[4,128,512]{2,1,0:T(8,128)} %bitcast.521), calls=%async_computation.8 | async-start | bytes 2097152 | tf_op jit(solution)/shard_map/all_to_all | solution.py:78
  589.6 29.8 %all-to-all-start.13 = ((f32[4,128,512]{2,1,0:T(8,128)}), f32[4,128,512]{2,1,0:T(8,128)}, u32[]{:S(2)}, u32[]{:S(2)}) async-start(f32[4,128,512]{2,1,0:T(8,128)} %fusion.28), calls=%async_computation.15 | async-start | bytes 2097152 | tf_op jit(solution)/shard_map/all_to_all | solution.py:85
  619.4 29.6 %all-to-all-start.9 = ((f32[4,128,512]{2,1,0:T(8,128)}), f32[4,128,512]{2,1,0:T(8,128)}, u32[]{:S(2)}, u32[]{:S(2)}) async-start(f32[4,128,512]{2,1,0:T(8,128)} %fusion.30), calls=%async_computation.9 | async-start | bytes 2097152 | tf_op jit(solution)/shard_map/all_to_all | solution.py:85
  623.7 249.0 %reduce-scatter.11.cloned.1.call-start = ((), (), s32[]{:S(2)}) async-start(), calls=%async_computation.27 | async-start | bytes 2621440 | tf_op jit(solution)/shard_map/reduce_scatter | solution.py:161
  699.6 16.9 %collective-permute-start.4 = (f32[7,512]{1,0:T(8,128)S(1)}, f32[7,512]{1,0:T(8,128)S(1)}, u32[]{:S(2)}, u32[]{:S(2)}) collective-permute-start(f32[7,512]{1,0:T(8,128)S(1)} %get-tuple-element.204), channel_id=1, source_target_pairs={{1,0},{2,1},{3,2},{5,4},{6,5},{7,6},{9,8},{10,9},{11,10},{13,12},{... | collective-permute-start | bytes 43016 | tf_op jit(solution)/shard_map/ppermute | solution.py:21
  700.9 15.7 collective-permute-start.5
  710.4 7.8 collective-permute-start.6
  732.4 140.3 %reduce-scatter.9.cloned.1.call-start = ((), (), s32[]{:S(2)}) async-start(), calls=%async_computation.26 | async-start | bytes 2621440 | tf_op jit(solution)/shard_map/reduce_scatter | solution.py:160
  755.1 122.4 %reduce-scatter.7.cloned.1.call-start = ((), (), s32[]{:S(2)}) async-start(), calls=%async_computation.25 | async-start | bytes 2621440 | tf_op jit(solution)/shard_map/reduce_scatter | solution.py:161
  770.4 144.2 %reduce-scatter.5.cloned.1.call-start = ((), (), s32[]{:S(2)}) async-start(), calls=%async_computation.24 | async-start | bytes 2621440 | tf_op jit(solution)/shard_map/reduce_scatter | solution.py:160
  923.6 30.1 %all-to-all-start.14 = ((f32[4,128,512]{2,1,0:T(8,128)}), f32[4,128,512]{2,1,0:T(8,128)}, u32[]{:S(2)}, u32[]{:S(2)}) async-start(f32[4,128,512]{2,1,0:T(8,128)} %bitcast.517), calls=%async_computation.18 | async-start | bytes 2097152 | tf_op jit(solution)/shard_map/all_to_all | solution.py:78
  953.7 28.7 %all-to-all-start.10 = ((f32[4,128,512]{2,1,0:T(8,128)}), f32[4,128,512]{2,1,0:T(8,128)S(1)}, u32[]{:S(2)}, u32[]{:S(2)}) async-start(f32[4,128,512]{2,1,0:T(8,128)} %bitcast.96), calls=%async_computation.12 | async-start | bytes 2097152 | tf_op jit(solution)/shard_map/all_to_all | solution.py:78
  982.5 29.5 %all-to-all-start.15 = ((f32[4,128,512]{2,1,0:T(8,128)}), f32[4,128,512]{2,1,0:T(8,128)}, u32[]{:S(2)}, u32[]{:S(2)}) async-start(f32[4,128,512]{2,1,0:T(8,128)} %fusion.42), calls=%async_computation.19 | async-start | bytes 2097152 | tf_op jit(solution)/shard_map/all_to_all | solution.py:85
  1012.0 29.5 %all-to-all-start.11 = ((f32[4,128,512]{2,1,0:T(8,128)}), f32[4,128,512]{2,1,0:T(8,128)}, u32[]{:S(2)}, u32[]{:S(2)}) async-start(f32[4,128,512]{2,1,0:T(8,128)} %fusion.44), calls=%async_computation.13 | async-start | bytes 2097152 | tf_op jit(solution)/shard_map/all_to_all | solution.py:85
  1016.2 151.4 %all-reduce.13.cloned.1.call-start = ((), (), s32[]{:S(2)}) async-start(), calls=%async_computation.28 | async-start | bytes 164864 | tf_op jit(solution)/shard_map/psum | solution.py:333
  1046.2 297.8 %all-reduce.15.cloned.1.call-start = ((), (), s32[]{:S(2)}) async-start(), calls=%async_computation.29 | async-start | bytes 14680064 | tf_op jit(solution)/shard_map/psum | solution.py:333
  1054.8 512.2 %all-reduce.17.cloned.1.call-start = ((), (), s32[]{:S(2)}) async-start(), calls=%async_computation.30 | async-start | bytes 33554432 | tf_op jit(solution)/shard_map/psum | solution.py:347
  (191 other events, 3776.8 us)
Sparse Core Ops, SparseCore 0:
  144.5 44.9 all-gather.10
  191.7 44.6 all-gather.8
  238.5 44.9 all-gather.6
  285.5 44.5 all-gather.4
  732.5 44.7 reduce-scatter.10
  779.6 43.2 reduce-scatter.8
  825.2 43.1 reduce-scatter.6
  871.4 43.1 reduce-scatter.4
  1046.3 121.3 all-reduce.12
  1174.8 169.0 all-reduce.14
  1348.6 218.3 all-reduce.16
where the time goes:
time: 1610 us; the launch traced here: 1600 us
  waiting for transfers between devices  842 us (52%)
  matrix products  419 us (26%)
  starting transfers between devices  92 us (6%)
  blocking collectives  78.1 us (5%)
  local copies, waits for them, and re-layouts  75.7 us (5%)
  other arithmetic  70.7 us (4%)
  between operations  18.5 us (1%)
    psum x2, waiting for transfers between devices, body(): lax.psum((gain_grad, shift_grad, router_grad, packed_grad, mixing_grad, s...  230 us
    psum x1, waiting for transfers between devices, body(): inner_grad, outer_grad = lax.psum((inner_grad, outer_grad), 'dp')  223 us
    dot_general x52, matrix products, product(): return jnp.matmul(left, right, precision=HIGH)  139 us
    all_to_all x4, waiting for transfers between devices, mixture_forward(): lax.all_to_all(send, 'ep', split_axis=0, concat_axis=0, tiled=True)  64.6 us
    all_to_all x4, waiting for transfers between devices, mixture_forward(): back = lax.all_to_all(result, 'ep', split_axis=0, concat_axis=0, tiled=True)  63.7 us
    all_to_all x4, waiting for transfers between devices, mixture_backward(): lax.all_to_all(grad_back, 'ep', split_axis=0, concat_axis=0, tiled=True)  60 us
    all_gather x2, waiting for transfers between devices, attention_forward(): lax.all_gather(packed[:, 2 * width:], 'ep', axis=0, tiled=True)  56.7 us
    all_gather x2, waiting for transfers between devices, attention_forward(): lax.all_gather(packed[:, width:2 * width], 'ep', axis=0, tiled=True)  55 us
  transfers between devices with their start and end apart: 35, of which 25 were waited for; matrix products, arithmetic and copies ran while one was open for 28% of the time, Pallas kernels for 0%

commit v1 on v0

v1 whole, which is shorter than its diff:
```python
import functools

import jax
import jax.numpy as jnp
from jax import lax
from jax.experimental import pallas as pl
from jax.experimental.pallas import tpu as pltpu
from jax.sharding import PartitionSpec as P

HIGH = lax.Precision.HIGH
EPS = 1e-05
FAR = 1e30
LANES = 128


def product(left, right):
    return jnp.matmul(left, right, precision=HIGH)


def after(values, *earlier):
    return lax.optimization_barrier((values,) + earlier)[0]


def swap(values, axis, bit):
    count = lax.axis_size(axis)
    return lax.ppermute(values, axis, [(i, i ^ bit) for i in range(count)])


def bits_of(axis):
    count = lax.axis_size(axis)
    return [(axis, 1 << k) for k in range(count.bit_length() - 1)]


def butterfly(values, steps):
    for axis, bit in steps:
        values = values + swap(values, axis, bit)
    return values


def upper(step):
    axis, bit = step
    return (lax.axis_index(axis) // bit) % 2


def halve(values, step):
    side = upper(step)
    half = values.shape[0] // 2
    keep = lax.dynamic_slice_in_dim(values, side * half, half, 0)
    send = lax.dynamic_slice_in_dim(values, (1 - side) * half, half, 0)
    return keep + swap(send, *step)


def join(values, step):
    side = upper(step)
    other = swap(values, *step)
    half = values.shape[0]
    out = jnp.zeros((2 * half,) + values.shape[1:], values.dtype)
    out = lax.dynamic_update_slice_in_dim(out, values, side * half, 0)
    return lax.dynamic_update_slice_in_dim(out, other, (1 - side) * half, 0)


def reduce_pair(pair, steps, meanwhile):
    first, rest = steps[0], steps[1:]
    orders = [(first,) + tuple(rest), (first,) + tuple(rest[::-1])]
    pair = list(pair)
    for k in range(len(steps)):
        pair = [halve(part, order[k]) for part, order in zip(pair, orders)]
    middle = tuple(pair)
    pair, meanwhile = lax.optimization_barrier((pair, meanwhile))
    for k in range(len(steps) - 1, 0, -1):
        pair = [join(part, order[k]) for part, order in zip(pair, orders)]
    return [(part, swap(part, *first)) for part in pair], upper(first), middle, meanwhile


class Layout:
    def __init__(self, micro, rows, capacity):
        self.micro, self.rows, self.capacity = micro, rows, capacity
        self.ep, self.dp = lax.axis_size("ep"), lax.axis_size("dp")
        self.z, self.d = lax.axis_index("ep"), lax.axis_index("dp")
        self.paired = micro == 2 and self.ep == 4 and self.dp % 2 == 0
        self.core = self.d % 2

    def route(self, low, u, home):
        pairs = []
        for d in range(self.dp):
            for z in range(self.ep):
                there = (d - d % 2 + z // 2) * self.ep + 2 * ((z % 2) ^ u) + (low ^ (d % 2))
                pairs.append((d * self.ep + z, there))
        return [(j, i) for i, j in pairs] if home else pairs

    def piece(self, values, at, count, axis=0):
        return lax.slice_in_dim(values, at * self.capacity, (at + count) * self.capacity, axis=axis)

    def home_slots(self, ids, rank):
        block = jnp.arange(self.micro, dtype=jnp.int32)[:, None]
        if not self.paired:
            return self.work_slots(ids, rank)
        step = ids ^ (2 * block + self.core)
        u = (self.z % 2) ^ (ids // 2)
        return (((step % 2) * 2 + u) * 2 + step // 2) * self.capacity + rank

    def work_slots(self, ids, rank):
        block = jnp.arange(self.micro, dtype=jnp.int32)[:, None]
        step = ids ^ self.z
        groups = self.ep // 2
        inner = block ^ (ids // 2) if self.paired else block
        return ((step % groups * 2 + step // groups) * self.micro + inner) * self.capacity + rank

    def hop(self, values, step):
        return values if step == 0 else swap(values, "ep", step)

    def hops(self, values, group):
        half = values.shape[0] // 2
        return jnp.concatenate(
            [self.hop(values[h * half : (h + 1) * half], group + h * (self.ep // 2)) for h in (0, 1)], axis=0
        )

    def group_of(self, values, group):
        return self.piece(values, group * 2 * self.micro, 2 * self.micro)

    def home_to_expert(self, rows, extra):
        wide = rows.shape[1]
        few = extra.shape[0]
        count = self.micro * self.capacity
        out = []
        last = ()
        for group in range(self.ep // 2):
            got = []
            for u in (0, 1):
                at = (group * 2 + u) * self.micro
                more = self.piece(extra, at, self.micro, 1)
                message = jnp.concatenate(
                    [self.piece(rows, at, self.micro), jnp.pad(more, ((0, 0), (0, wide - count)))], axis=0
                )
                message = after(message, *last)
                if self.paired:
                    got.append(lax.ppermute(message, ("dp", "ep"), self.route(group, u, False)))
                else:
                    got.append(self.hop(message, group + u * (self.ep // 2)))
            last = tuple(got)
            rows_got = [v[:count] for v in got]
            more_got = [v[count:, :count] for v in got]
            if self.paired:
                order = [(u, h) for h in (0, 1) for u in (0, 1)]
                rows_got = [self.piece(rows_got[u], h, 1) for u, h in order]
                more_got = [self.piece(more_got[u], h, 1, 1) for u, h in order]
            out.append((jnp.concatenate(rows_got, axis=0), jnp.concatenate(more_got, axis=1).T))
        return out

    def expert_to_home(self, groups):
        rows_out, more_out = [], []
        count = self.micro * self.capacity
        for group, (rows, more) in enumerate(groups):
            wide = rows.shape[1]
            for u in (0, 1):
                if self.paired:
                    row = jnp.concatenate([self.piece(rows, 2 * h + u, 1) for h in (0, 1)], axis=0)
                    few = jnp.concatenate([self.piece(more, 2 * h + u, 1, 1) for h in (0, 1)], axis=1)
                else:
                    row, few = self.piece(rows, u * self.micro, self.micro), self.piece(more, u * self.micro, self.micro, 1)
                message = jnp.concatenate([row, jnp.pad(few, ((0, 0), (0, wide - count)))], axis=0)
                if self.paired:
                    got = lax.ppermute(message, ("dp", "ep"), self.route(group, u, True))
                else:
                    got = self.hop(message, group + u * (self.ep // 2))
                rows_out.append(got[:count])
                more_out.append(got[count:, :count])
        return jnp.concatenate(rows_out, axis=0), jnp.concatenate(more_out, axis=1)

    def ids_to_work(self, ids):
        if not self.paired:
            return ids
        values = jnp.swapaxes(ids, 1, 2).astype(jnp.float32)
        out = []
        for turn in (0, 1):
            pairs = []
            for d in range(self.dp):
                for z in range(self.ep):
                    m = (z % 2) ^ turn
                    pairs.append((d * self.ep + z, (d - d % 2 + z // 2) * self.ep + 2 * m + d % 2))
            block = lax.dynamic_index_in_dim(values, (self.z % 2) ^ turn, 0, keepdims=False)
            out.append(lax.ppermute(block, ("dp", "ep"), pairs))
        m = self.z // 2
        both = jnp.stack([jnp.where(m == 0, out[0], out[1]), jnp.where(m == 0, out[1], out[0])])
        return jnp.swapaxes(both, 1, 2).astype(jnp.int32)

    def places(self, lengths):
        counts = jnp.sum(lengths, axis=1).astype(jnp.float32)
        if self.paired:
            m = self.z // 2
            place = self.core * 2 * self.rows + jnp.arange(2 * self.rows, dtype=jnp.int32)
            group = self.d - self.core + self.z % 2
            return place, [lengths[m, group]], counts[m][None]
        place = self.z * self.rows + jnp.arange(self.rows, dtype=jnp.int32)
        return place, [lengths[m, self.d] for m in range(self.micro)], counts

    def gather(self, values):
        if self.paired:
            return jnp.concatenate([values, swap(values, "dp", 1)], axis=0)
        return lax.all_gather(values, "ep", axis=0, tiled=True)

    def key_places(self):
        if self.paired:
            base = jnp.arange(2 * self.rows, dtype=jnp.int32)
            return jnp.concatenate([base + self.core * 2 * self.rows, base + (1 - self.core) * 2 * self.rows])
        return jnp.arange(self.ep * self.rows, dtype=jnp.int32)

    def scatter(self, values):
        if self.paired:
            half = values.shape[1] // 2
            return values[:, :half] + swap(values[:, half:], "dp", 1)
        return lax.psum_scatter(values, "ep", scatter_dimension=1, tiled=True)

    def halo(self, values, width):
        length = values.shape[0]
        if self.paired:
            low = self.core == 0
            edge = jnp.where(low, values[length - width :], values[:width])
            other = swap(edge, "dp", 1)
            zero = jnp.zeros_like(other)
            before, after = jnp.where(low, zero, other), jnp.where(low, other, zero)
        else:
            up = [(i, i + 1) for i in range(self.ep - 1)]
            down = [(j, i) for i, j in up]
            before = lax.ppermute(values[length - width :], "ep", up)
            after = lax.ppermute(values[:width], "ep", down)
        return jnp.concatenate([before, values, after], axis=0)

    def batch_total(self, values):
        if self.paired:
            return butterfly(values, bits_of("dp") + [("ep", 1)])
        return butterfly(values, bits_of("dp") + bits_of("ep"))


def norm_rows(values, gain, shift):
    center = values - jnp.mean(values, axis=-1, keepdims=True)
    spread = jnp.mean(center * center, axis=-1, keepdims=True)
    return center * lax.rsqrt(spread + EPS) * gain + shift


def swish_slope(values):
    squash = jax.nn.sigmoid(values)
    return squash * (1.0 + values * (1.0 - squash))


def ranks(ids, experts):
    rows = ids.shape[1]
    onehot = (ids[..., None] == jnp.arange(experts, dtype=jnp.int32)).astype(jnp.float32)
    below = (jnp.arange(rows)[:, None] > jnp.arange(rows)[None, :]).astype(jnp.float32)
    before = jnp.einsum("rs,bse->bre", below, onehot)
    return jnp.sum(before * onehot, axis=2).astype(jnp.int32)


def tables_of(slot, count):
    spots = jnp.arange(count, dtype=jnp.int32)
    flat = slot.reshape(-1)
    return (
        (spots[:, None] == flat[None, :]).astype(jnp.bfloat16),
        (flat[:, None] == spots[None, :]).astype(jnp.bfloat16),
    )


def pick(table, values):
    return jnp.matmul(table.astype(jnp.float32), values, precision=HIGH)


def pick_columns(values, table):
    return jnp.matmul(values, table.astype(jnp.float32), precision=HIGH)


def expert_forward(hidden, extra, own, gain, shift, router, weight_in, weight_out):
    def front(source, gain_now, shift_now, router_now, extra_now):
        normed = norm_rows(source, gain_now, shift_now)
        probs = jax.nn.softmax(product(normed, router_now) + extra_now, axis=-1)
        return (normed, jnp.sum(probs * own, axis=-1))

    (normed, gate), front_pull = jax.vjp(front, hidden, gain, shift, router, extra)
    pre = product(normed, weight_in)
    result = product(jax.nn.silu(pre), weight_out)
    new = hidden + 0.5 * gate[:, None] * result
    return (new, (front_pull, normed, gate, pre, result))


def expert_backward(grad, saved, weight_in, weight_out):
    front_pull, normed, gate, pre, result = saved
    grad_result = 0.5 * gate[:, None] * grad
    grad_gate = 0.5 * jnp.sum(grad * result, axis=1)
    grad_active = jnp.einsum("cd,fd->cf", grad_result, weight_out, precision=HIGH)
    grad_pre = grad_active * swish_slope(pre)
    grad_normed = jnp.einsum("cf,df->cd", grad_pre, weight_in, precision=HIGH)
    grad_hidden, gain_grad, shift_grad, router_grad, extra_grad = front_pull((grad_normed, grad_gate))
    return (grad + grad_hidden, extra_grad, (gain_grad, shift_grad, router_grad), (normed, jax.nn.silu(pre), grad_result, grad_pre))


def expert_weight_grads(kept):
    normed, active, grad_result, grad_pre = kept
    outer = jnp.einsum("cf,cd->fd", active, grad_result, precision=HIGH)
    return jnp.einsum("cd,cf->df", normed, grad_pre, precision=HIGH), outer


def add_up(trees):
    total = trees[0]
    for tree in trees[1:]:
        total = jax.tree.map(jnp.add, total, tree)
    return total


def parted(values):
    head = values.astype(jnp.bfloat16).astype(jnp.float32)
    return head, values - head


def head_lanes(side):
    low = lax.broadcasted_iota(jnp.int32, (1, LANES), 1) < LANES // 2
    turn = lambda v: pltpu.roll(v, LANES // 2, 1)
    at_low = lambda v: v if side == 0 else turn(v)
    at_high = lambda v: turn(v) if side == 0 else v
    both = lambda v, w: jnp.where(low, at_low(v), at_high(w))
    alone = lambda v, rest=0.0: jnp.where(low, at_low(v), rest)
    return both, alone


def dot_nt(left, right):
    return lax.dot_general(left, right, (((1,), (1,)), ((), ())), preferred_element_type=jnp.float32)


def dot_tn(left, right):
    return lax.dot_general(left, right, (((0,), (0,)), ((), ())), preferred_element_type=jnp.float32)


def dot_nn(left, right):
    return lax.dot_general(left, right, (((1,), (0,)), ((), ())), preferred_element_type=jnp.float32)


def narrow(*parts):
    return jnp.concatenate(parts, axis=1).astype(jnp.bfloat16) if len(parts) > 1 else parts[0].astype(jnp.bfloat16)


def attend_kernel(chunk, scale, slopes, dist, q_ref, k_ref, v_ref, out_ref, log_ref, k3, v2, v1, scores):
    pair = pl.program_id(0)
    total = k_ref.shape[0]
    q_hi, q_lo = parted(q_ref[...] * scale)
    k_hi, k_lo = parted(k_ref[...])
    v_hi, v_lo = parted(v_ref[...])
    mixed = []
    for side in (0, 1):
        both, alone = head_lanes(side)
        k3[...] = narrow(both(k_hi, k_hi), alone(k_lo))
        v2[...] = narrow(both(v_hi, v_lo))
        v1[...] = narrow(alone(v_hi))
        q3 = narrow(both(q_hi, q_lo), alone(q_hi))
        slope = slopes[2 * pair + side]
        highest = None
        for at in range(0, total, chunk):
            now = pl.ds(at, chunk)
            score = dot_nt(k3[now], q3) - slope * dist[now]
            scores[now] = score
            top = jnp.max(score, axis=0, keepdims=True)
            highest = top if highest is None else jnp.maximum(highest, top)
        summed, weight = 0.0, 0.0
        for at in range(0, total, chunk):
            now = pl.ds(at, chunk)
            raised = jnp.exp(scores[now] - highest)
            weight = weight + jnp.sum(raised, axis=0, keepdims=True)
            r_hi, r_lo = parted(raised)
            summed = summed + dot_tn(v2[now], narrow(r_hi)) + dot_tn(v1[now], narrow(r_lo))
        mixed.append((summed[: LANES // 2] + summed[LANES // 2 :]) / weight)
        log_ref[0, side : side + 1, :] = highest + jnp.log(weight)
    out_ref[...] = jnp.concatenate(mixed, axis=0).T


def attend_back_kernel(
    chunk, scale, slopes, dist, q_ref, k_ref, v_ref, o_ref, g_ref, log_ref, dq_ref, dkv_ref, ds_ref, k3, v3, k2, k1, hold
):
    pair = pl.program_id(0)
    total = k_ref.shape[0]
    q_hi, q_lo = parted(q_ref[...] * scale)
    k_hi, k_lo = parted(k_ref[...])
    v_hi, v_lo = parted(v_ref[...])
    grad = g_ref[...]
    g_hi, g_lo = parted(grad)
    weighed = grad * o_ref[...]
    lane = lax.broadcasted_iota(jnp.int32, (1, LANES), 1)
    low = lane < LANES // 2
    half = LANES // 2
    grad_query = []
    for side in (0, 1):
        both, alone = head_lanes(side)
        own = low if side == 0 else jnp.logical_not(low)
        centre = -jnp.sum(jnp.where(own, weighed, 0.0), axis=1, keepdims=True)
        c_hi, c_rest = parted(centre)
        c_mid, c_lo = parted(c_rest)
        tail = jnp.where(lane == half, c_hi, jnp.where(lane == half + 1, c_mid, jnp.where(lane == half + 2, c_lo, 0.0)))
        ones = jnp.where(jnp.logical_and(lane >= half, lane < half + 3), 1.0, 0.0)
        k3[...] = narrow(both(k_hi, k_hi), alone(k_lo))
        v3[...] = narrow(both(v_hi, v_hi), alone(v_lo, ones))
        k2[...] = narrow(both(k_hi, k_lo))
        k1[...] = narrow(alone(k_hi))
        q3 = narrow(both(q_hi, q_lo), alone(q_hi))
        q2, q1 = narrow(both(q_hi, q_lo)), narrow(alone(q_hi))
        g3 = narrow(both(g_hi, g_lo), alone(g_hi, tail))
        g2, g1 = narrow(both(g_hi, g_lo)), narrow(alone(g_hi))
        slope = slopes[2 * pair + side]
        logs = log_ref[0, side : side + 1, :]
        slope_grad, query_grad = 0.0, 0.0
        for at in range(0, total, chunk):
            now = pl.ds(at, chunk)
            far = dist[now]
            probs = jnp.exp(dot_nt(k3[now], q3) - slope * far - logs)
            grad_score = probs * dot_nt(v3[now], g3)
            slope_grad = slope_grad + jnp.sum(grad_score * far, axis=0, keepdims=True)
            p_hi, p_lo = parted(probs)
            s_hi, s_lo = parted(grad_score)
            s_hi, s_lo = narrow(s_hi), narrow(s_lo)
            value_grad = dot_nn(narrow(p_hi), g2) + dot_nn(narrow(p_lo), g1)
            key_grad = dot_nn(s_hi, q2) + dot_nn(s_lo, q1)
            query_grad = query_grad + dot_tn(k2[now], s_hi) + dot_tn(k1[now], s_lo)
            value_grad = value_grad + pltpu.roll(value_grad, half, 1)
            key_grad = key_grad + pltpu.roll(key_grad, half, 1)
            if side == 0:
                hold[0, now], hold[1, now] = key_grad, value_grad
            else:
                dkv_ref[0, now] = jnp.where(low, hold[0, now], key_grad)
                dkv_ref[1, now] = jnp.where(low, hold[1, now], value_grad)
        grad_query.append(query_grad[:half] + query_grad[half:])
        ds_ref[0, side : side + 1, :] = slope_grad
    dq_ref[...] = jnp.concatenate(grad_query, axis=0).T * scale


def attend_specs(rows, total, pairs):
    lanes = lambda at: pl.BlockSpec((rows, LANES), lambda i, at=at: (0, at + i))
    wide = lambda at: pl.BlockSpec((total, LANES), lambda i, at=at: (0, at + i))
    return [
        pl.BlockSpec(memory_space=pltpu.SMEM),
        pl.BlockSpec((total, rows), lambda i: (0, 0)),
        lanes(0),
        wide(0),
        wide(pairs),
    ], lanes(0), pl.BlockSpec((1, 8, rows), lambda i: (i, 0, 0))


def attend_params(rows, total, width, passes):
    return dict(
        compiler_params=pltpu.CompilerParams(vmem_limit_bytes=40 * 1024 * 1024),
        cost_estimate=pl.CostEstimate(
            flops=2 * rows * total * width * passes, bytes_accessed=16 * total * width, transcendentals=rows * total * 8
        ),
    )


def attend(packed, both, dist, slopes):
    rows, total = packed.shape[0], both.shape[0]
    width = both.shape[1] // 2
    pairs = width // LANES
    chunk = min(total, 256)
    in_specs, lanes, logs = attend_specs(rows, total, pairs)
    return pl.pallas_call(
        functools.partial(attend_kernel, chunk, (width // slopes.shape[0]) ** -0.5),
        grid=(pairs,),
        in_specs=in_specs,
        out_specs=[lanes, logs],
        out_shape=[
            jax.ShapeDtypeStruct((rows, width), jnp.float32),
            jax.ShapeDtypeStruct((pairs, 8, rows), jnp.float32),
        ],
        scratch_shapes=[
            pltpu.VMEM((total, 2 * LANES), jnp.bfloat16),
            pltpu.VMEM((total, LANES), jnp.bfloat16),
            pltpu.VMEM((total, LANES), jnp.bfloat16),
            pltpu.VMEM((total, rows), jnp.float32),
        ],
        name="attend",
        **attend_params(rows, total, width, 12),
    )(slopes, dist, packed, both, both)


def attend_back(packed, both, dist, slopes, mixed, logs, grad_mixed):
    rows, total = packed.shape[0], both.shape[0]
    width = both.shape[1] // 2
    pairs = width // LANES
    chunk = min(total, 256)
    in_specs, lanes, log_spec = attend_specs(rows, total, pairs)
    dq, dkv, ds = pl.pallas_call(
        functools.partial(attend_back_kernel, chunk, (width // slopes.shape[0]) ** -0.5),
        grid=(pairs,),
        in_specs=in_specs + [lanes, lanes, log_spec],
        out_specs=[lanes, pl.BlockSpec((2, total, LANES), lambda i: (0, 0, i)), log_spec],
        out_shape=[
            jax.ShapeDtypeStruct((rows, width), jnp.float32),
            jax.ShapeDtypeStruct((2, total, width), jnp.float32),
            jax.ShapeDtypeStruct((pairs, 8, rows), jnp.float32),
        ],
        scratch_shapes=[
            pltpu.VMEM((total, 2 * LANES), jnp.bfloat16),
            pltpu.VMEM((total, 2 * LANES), jnp.bfloat16),
            pltpu.VMEM((total, LANES), jnp.bfloat16),
            pltpu.VMEM((total, LANES), jnp.bfloat16),
            pltpu.VMEM((2, total, LANES), jnp.float32),
        ],
        name="attend_back",
        **attend_params(rows, total, width, 30),
    )(slopes, dist, packed, both, both, mixed, grad_mixed, logs)
    return dq, dkv, -jnp.sum(ds[:, :2], axis=2).reshape(-1)


def body(
    frames,
    embedding,
    cotangent,
    expert_ids,
    lengths,
    norm_gain,
    norm_bias,
    router,
    attention_in,
    attention_out,
    slopes,
    conv_point,
    conv_depth,
    batch_gain,
    batch_bias,
    conv_out,
    expert_in,
    expert_out,
):
    packed_weight = attention_in.astype(jnp.float32)
    mixing_weight = attention_out.astype(jnp.float32)
    point_weight = conv_point.astype(jnp.float32)
    project_weight = conv_out.astype(jnp.float32)
    inner_weight = expert_in[:, 0].astype(jnp.float32)
    outer_weight = expert_out[:, 0].astype(jnp.float32)
    micro, rows, width = frames.shape
    experts = router.shape[2]
    heads = slopes.shape[0]
    kernel = conv_depth.shape[0]
    half = kernel // 2
    capacity = 2 * rows // experts
    everyone = bits_of("dp") + bits_of("ep")
    layout = Layout(micro, rows, capacity)
    place, part_lengths, counts = layout.places(lengths)
    key_place = layout.key_places()
    parts = len(part_lengths)
    part_rows = micro * rows // parts
    valid_f = jnp.concatenate([(place < length) for length in part_lengths]).astype(jnp.float32)[:, None]
    to_parts = lambda v: v.reshape((parts, part_rows) + v.shape[1:])
    spread = lambda v: jnp.broadcast_to(v[:, None], (parts, part_rows) + v.shape[1:]).reshape(parts * part_rows, -1)

    slots = experts * micro * capacity
    own = (jnp.arange(experts, dtype=jnp.int32) == layout.z).astype(jnp.float32)[None, :]
    ids = jnp.moveaxis(expert_ids[..., 0], 0, 2)
    rank = [ranks(ids[..., b], experts) for b in (0, 1)]
    home = [tables_of(layout.home_slots(ids[..., b], rank[b]), slots) for b in (0, 1)]
    groups = range(experts // 2)
    home_rows = embedding.reshape(-1, width)
    home_logits = [product(router[b].T, home_rows.T) for b in (0, 1)]
    home_place = layout.z * rows + jnp.arange(rows, dtype=jnp.int32)
    home_valid = (home_place[None, :] < lengths[:, layout.d][:, None]).astype(jnp.float32).reshape(1, -1)
    spare = jnp.zeros((-(experts + 1) % 8, micro * rows), jnp.float32)
    extras = [
        pick_columns(jnp.concatenate([home_logits[b], home_valid, spare], axis=0), home[b][1]) for b in (0, 1)
    ]

    sources = layout.home_to_expert(pick(home[0][0], frames.reshape(-1, width)), extras[0])
    kept_first = []
    back = []
    last = ()
    for group in groups:
        hidden, extra = sources[group]
        new, kept = expert_forward(
            after(hidden, *last),
            extra[:, :experts],
            own,
            norm_gain[0],
            norm_bias[0],
            router[0],
            inner_weight[0],
            outer_weight[0],
        )
        last = (new,)
        kept_first.append(kept)
        back.append(layout.hops(new, group))
    work_ids = layout.ids_to_work(after(ids, sources[-1][0]))
    work = [
        tables_of(layout.work_slots(work_ids[..., b], ranks(work_ids[..., b], experts)), slots) for b in (0, 1)
    ]
    first = pick(work[0][1], jnp.concatenate(back, axis=0))

    def attention_front(values, gain_now, shift_now, weight_now):
        return product(norm_rows(values, gain_now, shift_now), weight_now)

    packed, attention_pull = jax.vjp(attention_front, first, norm_gain[1], norm_bias[1], packed_weight)
    packed, cot_rows = lax.optimization_barrier((packed, cotangent.reshape(-1, width)))
    pulls = layout.home_to_expert(pick(home[1][0], cot_rows), extras[1])
    packed_parts = to_parts(packed)
    apart = jnp.abs(key_place[:, None] - place[None, :]).astype(jnp.float32)
    kept_attention = []
    mixed_parts = []
    for part in range(parts):
        both = layout.gather(packed_parts[part, :, width:])
        dist = jnp.where((key_place < part_lengths[part])[:, None], apart, FAR)
        mixed, logs = attend(packed_parts[part], both, dist, slopes)
        kept_attention.append((both, dist, mixed, logs))
        mixed_parts.append(mixed)
    mixed_all = jnp.concatenate(mixed_parts, axis=0)
    second = first + product(mixed_all, mixing_weight)

    def conv_front(values, gain_now, shift_now, point_now):
        both = product(norm_rows(values, gain_now, shift_now), point_now)
        return both[:, :width] * jax.nn.sigmoid(both[:, width:]) * valid_f

    gated, conv_pull = jax.vjp(conv_front, second, norm_gain[2], norm_bias[2], point_weight)
    padded = [layout.halo(v, half) for v in to_parts(gated)]
    conv_parts = []
    for part in range(parts):
        total = conv_depth[0] * padded[part][0:part_rows]
        for offset in range(1, kernel):
            total = total + conv_depth[offset] * padded[part][offset : offset + part_rows]
        conv_parts.append(total)
    conv = jnp.concatenate(conv_parts, axis=0)
    stats = layout.batch_total(
        jnp.stack([jnp.sum(to_parts(conv * valid_f), axis=1), jnp.sum(to_parts(conv * conv * valid_f), axis=1)], axis=1)
    )
    centre = stats[:, 0] / counts[:, None]
    inverse_dev = lax.rsqrt(stats[:, 1] / counts[:, None] - centre * centre + EPS)
    scaled = (conv - spread(centre)) * spread(inverse_dev)
    shaped = scaled * batch_gain + batch_bias
    swished = jax.nn.silu(shaped)
    third = second + product(swished, project_weight)

    def final(values, gain_now, shift_now, valid_now):
        return norm_rows(values, gain_now, shift_now) * valid_now

    sent = pick(work[1][0], third)
    results, back, kept, small = [], [], [], []
    arrived, last = (), ()
    for group in groups:
        hidden = layout.hops(after(layout.group_of(sent, group), *arrived), group)
        arrived = (hidden,)
        pull_now, extra = pulls[group]
        fourth, saved = expert_forward(
            after(hidden, *last),
            extra[:, :experts],
            own,
            norm_gain[3],
            norm_bias[3],
            router[1],
            inner_weight[1],
            outer_weight[1],
        )
        valid_now = extra[:, experts : experts + 1]
        result, final_pull = jax.vjp(lambda v, g, b: final(v, g, b, valid_now), fourth, norm_gain[4], norm_bias[4])
        grad_fourth, gain_four, shift_four = final_pull(pull_now)
        grad, extra_grad, small_now, kept_now = expert_backward(grad_fourth, saved, inner_weight[1], outer_weight[1])
        last = (grad,)
        results.append((result, jnp.pad(extra_grad.T, ((0, -experts % 8), (0, 0)))))
        kept.append(kept_now)
        small.append(small_now + (gain_four, shift_four))
        back.append(layout.hops(grad, group))
    gain_three, shift_three, router_one, gain_four, shift_four = add_up(small)
    kept, _ = lax.optimization_barrier((kept, back[:-1]))
    inner_one, outer_one = lax.psum(add_up([expert_weight_grads(v) for v in kept]), "dp")
    grad_third = pick(work[1][1], jnp.concatenate(back, axis=0))
    project_grad = product(swished.T, grad_third)
    grad_shaped = product(grad_third, project_weight.T) * swish_slope(shaped)
    sums = jnp.stack(
        [jnp.sum(to_parts(grad_shaped), axis=1), jnp.sum(to_parts(grad_shaped * scaled), axis=1)], axis=1
    )
    totals = layout.batch_total(sums)
    shift_total, gain_total = totals[:, 0], totals[:, 1]
    results, _ = lax.optimization_barrier((results, totals))
    output_slots, logit_slots = layout.expert_to_home(results)
    output = pick(home[1][1], output_slots).reshape(micro, rows, width)
    logit_one = pick_columns(logit_slots[:experts], home[1][0])
    router_one = router_one + product(logit_one, home_rows).T
    grad_conv = (
        batch_gain
        * spread(inverse_dev)
        * (grad_shaped - valid_f * (spread(shift_total) + scaled * spread(gain_total)) / spread(counts[:, None]))
    )
    depth_grad = 0.0
    gated_parts = []
    for part, now in enumerate(to_parts(grad_conv)):
        grad_pad = layout.halo(now, half)
        total = conv_depth[0] * grad_pad[2 * half : 2 * half + part_rows]
        for offset in range(1, kernel):
            total = total + conv_depth[offset] * grad_pad[2 * half - offset : 2 * half - offset + part_rows]
        gated_parts.append(total)
        depth_grad = depth_grad + jnp.stack(
            [jnp.sum(now * padded[part][offset : offset + part_rows], axis=0) for offset in range(kernel)]
        )
    grad_hidden, gain_two, shift_two, point_grad = conv_pull(jnp.concatenate(gated_parts, axis=0))
    grad_second = grad_third + grad_hidden

    mixing_grad = product(mixed_all.T, grad_second)
    grad_mixed = to_parts(product(grad_second, mixing_weight.T))
    packed_back = []
    slope_grad = 0.0
    for part in range(parts):
        both, dist, mixed, logs = kept_attention[part]
        grad_query, grad_both, slope_now = attend_back(
            packed_parts[part], both, dist, slopes, mixed, logs, grad_mixed[part]
        )
        slope_grad = slope_grad + slope_now
        grad_both = layout.scatter(grad_both)
        packed_back.append(jnp.concatenate([grad_query, grad_both[0], grad_both[1]], axis=1))
    grad_hidden, gain_one, shift_one, packed_grad = attention_pull(jnp.concatenate(packed_back, axis=0))
    grad_first = grad_second + grad_hidden
    early = jnp.concatenate(
        [
            jnp.stack([gain_one, gain_two, gain_three, gain_four, shift_one, shift_two, shift_three, shift_four]),
            router_one.T,
            jnp.pad(slope_grad, (0, width - heads))[None],
            depth_grad,
            jnp.sum(sums, axis=0),
        ],
        axis=0,
    )
    few = early.shape[0]
    mixing_grad = jnp.concatenate([mixing_grad, jnp.pad(early, ((0, -few % 8), (0, 0)))], axis=0)
    packed_grad, mixing_grad, project_grad, point_grad = lax.psum(
        after((packed_grad, mixing_grad, project_grad, point_grad), inner_one), ("dp", "ep")
    )
    mixing_grad, early = mixing_grad[:width], mixing_grad[width:]

    sent = pick(work[0][0], grad_first)
    sources, kept, small = [], [], []
    arrived, last = (), ()
    for group in groups:
        grad = layout.hops(after(layout.group_of(sent, group), *arrived), group)
        arrived = (grad,)
        grad, extra_grad, small_now, kept_now = expert_backward(
            after(grad, *last), kept_first[group], inner_weight[0], outer_weight[0]
        )
        last = (grad,)
        sources.append((grad, jnp.pad(extra_grad.T, ((0, -experts % 8), (0, 0)))))
        kept.append(kept_now)
        small.append(small_now)
    gain_zero, shift_zero, router_zero = add_up(small)
    expert_zero = add_up([expert_weight_grads(v) for v in kept])
    dense = (packed_grad, mixing_grad, early, project_grad, point_grad)
    halves_zero, side, middle, dense = reduce_pair(expert_zero, bits_of("dp"), dense)
    packed_grad, mixing_grad, early, project_grad, point_grad = dense
    rows_back, logit_slots = layout.expert_to_home(sources)
    rows_back, logit_slots, inner_one, outer_one, _ = lax.optimization_barrier(
        (rows_back, logit_slots, inner_one, outer_one, middle)
    )
    logit_zero = pick_columns(logit_slots[:experts], home[0][0])
    router_zero = router_zero + product(logit_zero, home_rows).T
    frames_grad = pick(home[0][1], rows_back).reshape(micro, rows, width)
    late = butterfly(
        jnp.concatenate([gain_zero[None], shift_zero[None], router_zero.T], axis=0),
        bits_of("ep") + bits_of("dp"),
    )
    expert_grads = []
    for one, (mine, other) in zip((inner_one, outer_one), halves_zero):
        whole = lax.pad(one[None], 0.0, ((1, 0, 0), (0, 0, 0), (0, 0, 0)))
        half_rows = mine.shape[0]
        whole = lax.dynamic_update_slice(whole, mine[None], (0, side * half_rows, 0))
        expert_grads.append(lax.dynamic_update_slice(whole, other[None], (0, (1 - side) * half_rows, 0))[:, None])

    at = 8 + experts
    gain_grad = jnp.concatenate([late[:1], early[:4]], axis=0)
    shift_grad = jnp.concatenate([late[1:2], early[4:8]], axis=0)
    router_grad = jnp.stack([late[2 : 2 + experts].T, early[8:at].T])
    return (
        output,
        frames_grad,
        gain_grad,
        shift_grad,
        router_grad,
        packed_grad,
        mixing_grad,
        early[at, :heads],
        point_grad,
        early[at + 1 : at + 1 + kernel],
        early[at + 2 + kernel],
        early[at + 1 + kernel],
        project_grad,
        expert_grads[0],
        expert_grads[1],
    )


def solution(mesh):
    rows = P(None, ("dp", "ep"), None)
    whole = P()
    split = P(None, "ep", None, None)
    return jax.shard_map(
        body,
        mesh=mesh,
        in_specs=(rows, rows, rows, P(None, None, ("dp", "ep"), None)) + (whole,) * 12 + (split, split),
        out_specs=(rows, rows) + (whole,) * 11 + (split, split),
        check_vma=False,
    )
```

time: 1610 us -> 824 us (0.51)
  waiting for transfers between devices: 842 us -> 303 us
  matrix products: 419 us -> 160 us
  blocking collectives: 78.1 us -> 0 us
  starting transfers between devices: 92 us -> 143 us
  Pallas kernels: 0 us -> 39.7 us
    psum x3 -> x2, waiting for transfers between devices: 453 us -> 116 us  [the longest x1 116 us: body(): lax.psum(after((packed_grad, mixing_grad, project_grad, point_grad), inne...]
    all_to_all x16 -> x0, waiting for transfers between devices: 237 us -> none  [the longest x4 64.6 us: mixture_forward(): lax.all_to_all(send, 'ep', split_axis=0, concat_axis=0, tiled=True)]
    dot_general x36 -> x32, matrix products: 280 us -> 78.8 us  [the longest x4 20.1 us: expert_weight_grads(): outer = jnp.einsum('cf,cd->fd', active, grad_result, precision=HIGH)]
    ppermute x8 -> x59, waiting for transfers between devices: 2.65 us -> 186 us  [the longest x41 155 us: swap(): return lax.ppermute(values, axis, [(i, i ^ bit) for i in range(count)])]
    ppermute x8 -> x59, starting transfers between devices: 19 us -> 143 us  [the longest x41 62.4 us: swap(): return lax.ppermute(values, axis, [(i, i ^ bit) for i in range(count)])]
    all_gather x4 -> x0, waiting for transfers between devices: 112 us -> none  [the longest x2 56.7 us: attention_forward(): lax.all_gather(packed[:, 2 * width:], 'ep', axis=0, tiled=True)]
    psum x2 -> x0, blocking collectives: 78.1 us -> none  [the longest x1 40.4 us: body(): lax.psum((jnp.sum(conv * valid_f, axis=0), jnp.sum(conv * conv * valid_f,...]
    all_to_all x16 -> x0, starting transfers between devices: 70.5 us -> none  [the longest x4 19.5 us: mixture_forward(): lax.all_to_all(send, 'ep', split_axis=0, concat_axis=0, tiled=True)]
  transfers between devices with their start and end apart: 35 -> 61, of which waited for: 25 -> 25; matrix products, arithmetic and copies ran while one was open for 28% -> 30% of each run, Pallas kernels for 0% -> 5%
where the time goes in v1:
time: 824 us; the launch traced here: 813 us
  waiting for transfers between devices  303 us (37%)
  matrix products  160 us (19%)
  starting transfers between devices  143 us (17%)
  local copies, waits for them, and re-layouts  74.9 us (9%)
  other arithmetic  74.3 us (9%)
  Pallas kernels  39.7 us (5%)
  between operations  18.6 us (2%)
    ppermute x41, waiting for transfers between devices, swap(): return lax.ppermute(values, axis, [(i, i ^ bit) for i in range(count)])  155 us
    psum x1, waiting for transfers between devices, body(): lax.psum(after((packed_grad, mixing_grad, project_grad, point_grad), inne...  116 us
    dot_general x36, matrix products, product(): return jnp.matmul(left, right, precision=HIGH)  81.4 us
    ppermute x41, starting transfers between devices, swap(): return lax.ppermute(values, axis, [(i, i ^ bit) for i in range(count)])  62.4 us
    ppermute x8, starting transfers between devices, home_to_expert(): got.append(lax.ppermute(message, ('dp', 'ep'), self.route(group, u, False)))  40.7 us
    pallas_call x1, Pallas kernels, attend_back(): pl.pallas_call(functools.partial(attend_back_kernel, chunk, (width // slo...  26.5 us
    ppermute x2, starting transfers between devices, ids_to_work(): out.append(lax.ppermute(block, ('dp', 'ep'), pairs))  22.8 us
    dot_general x4, matrix products, expert_weight_grads(): outer = jnp.einsum('cf,cd->fd', active, grad_result, precision=HIGH)  20.1 us
  transfers between devices with their start and end apart: 61, of which 25 were waited for; matrix products, arithmetic and copies ran while one was open for 30% of the time, Pallas kernels for 5%

profile of v1, /device:TPU:0, one launch (start us, length us, event | category | flops | bytes accessed | tf_op | source)
XLA Modules:
  0.0 812.9 jit_solution(12359026262077669479)
XLA Ops:
  31.2 6.2 collective-permute-done.1
  37.4 10.5 %collective-permute-start.2 = (f32[264,512]{1,0:T(8,128)}, f32[264,512]{1,0:T(8,128)S(1)}, u32[]{:S(2)}, u32[]{:S(2)}) collective-permute-start(f32[264,512]{1,0:T(8,128)} %get-tuple-element.59), channel_id=1, source_target_pairs={{0,1},{1,3},{2,5},{3,7},{4,0},{5,2},{6,4},{7,6},{8,9},{9,11},{10,1... | collective-permute-start | bytes 1622024 | tf_op jit(solution)/shard_map/ppermute | solution.py:137
  47.9 5.2 collective-permute-start.3
  68.6 22.1 %collective-permute-start.5 = (f32[2,256]{1,0:T(2,128)S(1)}, f32[2,256]{1,0:T(2,128)S(1)}, u32[]{:S(2)}, u32[]{:S(2)}) collective-permute-start(f32[2,256]{1,0:T(2,128)S(1)} %bitcast.521), channel_id=1, source_target_pairs={{0,2},{1,0},{2,6},{3,4},{4,3},{5,1},{6,7},{7,5},{8,10},{9,8},{10,1... | collective-permute-start | bytes 6152 | tf_op jit(solution)/shard_map/ppermute | solution.py:182
  105.0 8.1 collective-permute-done.7
  113.2 14.1 %collective-permute-done.8 = f32[256,512]{1,0:T(8,128)S(1)} collective-permute-done((f32[256,512]{1,0:T(8,128)S(1)}, f32[256,512]{1,0:T(8,128)S(1)}, u32[]{:S(2)}, u32[]{:S(2)}) %collective-permute-start.8) | collective-permute-done | bytes 524320 | tf_op jit(solution)/shard_map/ppermute | solution.py:26
  141.4 11.5 %collective-permute-done.17 = f32[264,512]{1,0:T(8,128)S(1)} collective-permute-done((f32[264,512]{1,0:T(8,128)S(1)}, f32[264,512]{1,0:T(8,128)S(1)}, u32[]{:S(2)}, u32[]{:S(2)}) %collective-permute-start.17) | collective-permute-done | bytes 540704 | tf_op jit(solution)/shard_map/ppermute | solution.py:137
  153.0 10.7 %collective-permute-start.20 = (f32[264,512]{1,0:T(8,128)S(1)}, f32[264,512]{1,0:T(8,128)S(1)}, u32[]{:S(2)}, u32[]{:S(2)}) collective-permute-start(f32[264,512]{1,0:T(8,128)S(1)} %select_maximum_fusion.2), channel_id=1, source_target_pairs={{0,1},{1,3},{2,5},{3,7},{4,0},{5,2},{6,4},{7,6},{8,9},{9,11},{10,1... | collective-permute-start | bytes 1622024 | tf_op jit(solution)/shard_map/ppermute | solution.py:137
  169.9 13.2 %attend.1 = (f32[512,512]{1,0:T(8,128)S(1)}, f32[4,8,512]{2,1,0:T(8,128)S(1)}) custom-call(f32[8]{0:T(128)S(1)} %copy-done.10, f32[1024,512]{1,0:T(8,128)S(1)} %copy-done.4, f32[512,1536]{1,0:T(8,128)S(1)} %fusion.170.q_ref, f32[1024,1024]{1,0:T(8,128)S(1)} %pad_maximum_fusion.k_ref.v_ref, f32[1024,1024]{1,0:T(8,128)S(1)} %pad_maximum_fusion.k_ref.v_ref), custom_call_target="tpu_custom_call" | custom-call | flops 6442450944 | bytes 8388608 | tf_op jit(solution)/shard_map/attend/pallas_call | solution.py:457
  213.6 18.6 %collective-permute-done.15 = f32[256,512]{1,0:T(8,128)S(1)} collective-permute-done((f32[256,512]{1,0:T(8,128)S(1)}, f32[256,512]{1,0:T(8,128)S(1)}, u32[]{:S(2)}, u32[]{:S(2)}) %collective-permute-start.15) | collective-permute-done | bytes 524320 | tf_op jit(solution)/shard_map/ppermute | solution.py:26
  238.8 6.5 fusion.1
  264.2 8.9 %collective-permute-done.18 = f32[256,512]{1,0:T(8,128)S(1)} collective-permute-done((f32[256,512]{1,0:T(8,128)S(1)}, f32[256,512]{1,0:T(8,128)S(1)}, u32[]{:S(2)}, u32[]{:S(2)}) %collective-permute-start.18) | collective-permute-done | bytes 524320 | tf_op jit(solution)/shard_map/ppermute | solution.py:26
  273.1 12.5 %collective-permute-done.19 = f32[256,512]{1,0:T(8,128)S(1)} collective-permute-done((f32[256,512]{1,0:T(8,128)S(1)}, f32[256,512]{1,0:T(8,128)S(1)}, u32[]{:S(2)}, u32[]{:S(2)}) %collective-permute-start.19) | collective-permute-done | bytes 524320 | tf_op jit(solution)/shard_map/ppermute | solution.py:26
  291.0 4.5 fusion
  309.2 12.9 %collective-permute-start.23 = (f32[256,512]{1,0:T(8,128)S(1)}, f32[256,512]{1,0:T(8,128)S(1)}, u32[]{:S(2)}, u32[]{:S(2)}) collective-permute-start(f32[256,512]{1,0:T(8,128)S(1)} %get-tuple-element.244), channel_id=1, source_target_pairs={{0,1},{1,0},{2,3},{3,2},{4,5},{5,4},{6,7},{7,6},{8,9},{9,8},{10,11... | collective-permute-start | bytes 1572872 | tf_op jit(solution)/shard_map/ppermute | solution.py:26
  331.9 5.1 convolution_add_fusion.2
  337.1 8.1 collective-permute-done.24
  349.9 5.2 convolution_add_fusion.3
  369.5 7.9 multiply_reduce_fusion
  398.8 26.5 %attend_back.1 = (f32[512,512]{1,0:T(8,128)S(1)}, f32[2,1024,512]{2,1,0:T(8,128)S(1)}, f32[4,8,512]{2,1,0:T(8,128)S(1)}) custom-call(f32[8]{0:T(128)S(1)} %copy-done.10, f32[1024,512]{1,0:T(8,128)S(1)} %copy-done.5, f32[512,1536]{1,0:T(8,128)S(1)} %copy-done.7, f32[1024,1024]{1,0:T(8,128)} %copy-done.3, f32[1024,1024]{1,0:T(8,128)} %copy-done.3, ...), custom_call_target="tpu_custom_call" | custom-call | flops 16106127360 | bytes 8388608 | tf_op jit(solution)/shard_map/attend_back/pallas_call | solution.py:483
  439.3 5.1 fusion.67
  472.7 6.8 fusion.4
  479.5 15.2 %collective-permute-done.35 = f32[256,512]{1,0:T(8,128)} collective-permute-done((f32[256,512]{1,0:T(8,128)}, f32[256,512]{1,0:T(8,128)}, u32[]{:S(2)}, u32[]{:S(2)}) %collective-permute-start.35) | collective-permute-done | bytes 524320 | tf_op jit(solution)/shard_map/ppermute | solution.py:26
  519.3 12.2 %collective-permute-done.39 = f32[256,512]{1,0:T(8,128)S(1)} collective-permute-done((f32[256,512]{1,0:T(8,128)S(1)}, f32[256,512]{1,0:T(8,128)S(1)}, u32[]{:S(2)}, u32[]{:S(2)}) %collective-permute-start.39) | collective-permute-done | bytes 524320 | tf_op jit(solution)/shard_map/ppermute | solution.py:26
  531.6 5.4 fusion.165
  540.2 6.0 convolution_add_fusion
  565.3 6.3 collective-permute-start.41
  578.9 9.3 %collective-permute-done.41 = f32[264,512]{1,0:T(8,128)} collective-permute-done((f32[264,512]{1,0:T(8,128)}, f32[264,512]{1,0:T(8,128)}, u32[]{:S(2)}, u32[]{:S(2)}) %collective-permute-start.41) | collective-permute-done | bytes 540704 | tf_op jit(solution)/shard_map/ppermute | solution.py:163
  594.7 18.4 %collective-permute-done.47 = f32[256,512]{1,0:T(8,128)S(1)} collective-permute-done((f32[256,512]{1,0:T(8,128)S(1)}, f32[256,512]{1,0:T(8,128)S(1)}, u32[]{:S(2)}, u32[]{:S(2)}) %collective-permute-start.47) | collective-permute-done | bytes 524320 | tf_op jit(solution)/shard_map/ppermute | solution.py:26
  633.6 116.3 %all-reduce.29.cloned.1.call-done = (f32[512,1536]{1,0:T(8,128)}, f32[544,512]{1,0:T(8,128)}, f32[512,512]{1,0:T(8,128)}, f32[512,1024]{1,0:T(8,128)}) async-done(((f32[512,1536]{1,0:T(8,128)}, f32[544,512]{1,0:T(8,128)}, f32[512,512]{1,0:T(8,128)}, f32[512,1024]{1,0:T(8,128)}), (f32[512,1536]{1,0:T(8,128)}, f32[544,512]{1,0:T(8,128)}, f32[512,512]{1,0:T(8,128)}, ...) | async-done | bytes 7405584 | tf_op jit(solution)/shard_map/psum | solution.py:720
  760.2 6.6 collective-permute-done.56
  773.0 18.0 %collective-permute-done.57 = f32[512,512]{1,0:T(8,128)S(1)} collective-permute-done((f32[512,512]{1,0:T(8,128)S(1)}, f32[512,512]{1,0:T(8,128)S(1)}, u32[]{:S(2)}, u32[]{:S(2)}) %collective-permute-start.57) | collective-permute-done | bytes 1048608 | tf_op jit(solution)/shard_map/ppermute | solution.py:26
  (905 shorter events, 350.5 us)
Async XLA Ops:
  7.2 567.3 %all-reduce.31.cloned.1.call-start = ((), (), s32[]{:S(2)}) async-start(), calls=%async_computation.1 | async-start | bytes 16777216 | tf_op jit(solution)/shard_map/psum | solution.py:661
  37.4 29.3 %collective-permute-start.2 = (f32[264,512]{1,0:T(8,128)}, f32[264,512]{1,0:T(8,128)S(1)}, u32[]{:S(2)}, u32[]{:S(2)}) collective-permute-start(f32[264,512]{1,0:T(8,128)} %get-tuple-element.59), channel_id=1, source_target_pairs={{0,1},{1,3},{2,5},{3,7},{4,0},{5,2},{6,4},{7,6},{8,9},{9,11},{10,1... | collective-permute-start | bytes 1622024 | tf_op jit(solution)/shard_map/ppermute | solution.py:137
  47.9 18.8 %collective-permute-start.3 = (f32[264,512]{1,0:T(8,128)}, f32[264,512]{1,0:T(8,128)}, u32[]{:S(2)}, u32[]{:S(2)}) collective-permute-start(f32[264,512]{1,0:T(8,128)} %get-tuple-element.60), channel_id=1, source_target_pairs={{0,3},{1,1},{2,7},{3,5},{4,2},{5,0},{6,6},{7,4},{8,11},{9,9},{10,1... | collective-permute-start | bytes 1622024 | tf_op jit(solution)/shard_map/ppermute | solution.py:137
  66.7 38.4 %collective-permute-start.6 = (f32[256,512]{1,0:T(8,128)}, f32[256,512]{1,0:T(8,128)}, u32[]{:S(2)}, u32[]{:S(2)}) collective-permute-start(f32[256,512]{1,0:T(8,128)} %get-tuple-element.251), channel_id=1, source_target_pairs={{0,2},{1,3},{2,0},{3,1},{4,6},{5,7},{6,4},{7,5},{8,10},{9,11},{10,... | collective-permute-start | bytes 1572872 | tf_op jit(solution)/shard_map/ppermute | solution.py:26
  67.9 36.5 %collective-permute-start.4 = (f32[2,256]{1,0:T(2,128)S(1)}, f32[2,256]{1,0:T(2,128)S(1)}, u32[]{:S(2)}, u32[]{:S(2)}) collective-permute-start(f32[2,256]{1,0:T(2,128)S(1)} %bitcast.520), channel_id=1, source_target_pairs={{0,0},{1,2},{2,4},{3,6},{4,1},{5,3},{6,5},{7,7},{8,8},{9,10},{10,1... | collective-permute-start | bytes 6152 | tf_op jit(solution)/shard_map/ppermute | solution.py:182
  68.6 35.9 %collective-permute-start.5 = (f32[2,256]{1,0:T(2,128)S(1)}, f32[2,256]{1,0:T(2,128)S(1)}, u32[]{:S(2)}, u32[]{:S(2)}) collective-permute-start(f32[2,256]{1,0:T(2,128)S(1)} %bitcast.521), channel_id=1, source_target_pairs={{0,2},{1,0},{2,6},{3,4},{4,3},{5,1},{6,7},{7,5},{8,10},{9,8},{10,1... | collective-permute-start | bytes 6152 | tf_op jit(solution)/shard_map/ppermute | solution.py:182
  100.9 26.4 %collective-permute-start.8 = (f32[256,512]{1,0:T(8,128)S(1)}, f32[256,512]{1,0:T(8,128)S(1)}, u32[]{:S(2)}, u32[]{:S(2)}) collective-permute-start(f32[256,512]{1,0:T(8,128)S(1)} %get-tuple-element.253), channel_id=1, source_target_pairs={{0,3},{1,2},{2,1},{3,0},{4,7},{5,6},{6,5},{7,4},{8,11},{9,10},{10,... | collective-permute-start | bytes 1572872 | tf_op jit(solution)/shard_map/ppermute | solution.py:26
  132.2 36.1 %collective-permute-start.9 = (f32[512,1024]{1,0:T(8,128)S(1)}, f32[512,1024]{1,0:T(8,128)S(1)}, u32[]{:S(2)}, u32[]{:S(2)}) collective-permute-start(f32[512,1024]{1,0:T(8,128)S(1)} %slice_bitcast_fusion), channel_id=1, source_target_pairs={{0,4},{4,0},{8,12},{12,8},{16,20},{20,16},{24,28},{28,24},{1,5},{5... | collective-permute-start | bytes 6291464 | tf_op jit(solution)/shard_map/ppermute | solution.py:26
  153.0 46.2 %collective-permute-start.20 = (f32[264,512]{1,0:T(8,128)S(1)}, f32[264,512]{1,0:T(8,128)S(1)}, u32[]{:S(2)}, u32[]{:S(2)}) collective-permute-start(f32[264,512]{1,0:T(8,128)S(1)} %select_maximum_fusion.2), channel_id=1, source_target_pairs={{0,1},{1,3},{2,5},{3,7},{4,0},{5,2},{6,4},{7,6},{8,9},{9,11},{10,1... | collective-permute-start | bytes 1622024 | tf_op jit(solution)/shard_map/ppermute | solution.py:137
  163.7 38.1 %collective-permute-start.21 = (f32[264,512]{1,0:T(8,128)S(1)}, f32[264,512]{1,0:T(8,128)S(1)}, u32[]{:S(2)}, u32[]{:S(2)}) collective-permute-start(f32[264,512]{1,0:T(8,128)S(1)} %select_maximum_fusion.1), channel_id=1, source_target_pairs={{0,3},{1,1},{2,7},{3,5},{4,2},{5,0},{6,6},{7,4},{8,11},{9,9},{10,1... | collective-permute-start | bytes 1622024 | tf_op jit(solution)/shard_map/ppermute | solution.py:137
  209.2 22.9 %collective-permute-start.15 = (f32[256,512]{1,0:T(8,128)S(1)}, f32[256,512]{1,0:T(8,128)S(1)}, u32[]{:S(2)}, u32[]{:S(2)}) collective-permute-start(f32[256,512]{1,0:T(8,128)S(1)} %get-tuple-element.249), channel_id=1, source_target_pairs={{0,2},{1,3},{2,0},{3,1},{4,6},{5,7},{6,4},{7,5},{8,10},{9,11},{10,... | collective-permute-start | bytes 1572872 | tf_op jit(solution)/shard_map/ppermute | solution.py:26
  259.2 26.4 %collective-permute-start.19 = (f32[256,512]{1,0:T(8,128)S(1)}, f32[256,512]{1,0:T(8,128)S(1)}, u32[]{:S(2)}, u32[]{:S(2)}) collective-permute-start(f32[256,512]{1,0:T(8,128)S(1)} %get-tuple-element.247), channel_id=1, source_target_pairs={{0,3},{1,2},{2,1},{3,0},{4,7},{5,6},{6,5},{7,4},{8,11},{9,10},{10,... | collective-permute-start | bytes 1572872 | tf_op jit(solution)/shard_map/ppermute | solution.py:26
  262.7 74.3 %collective-permute-start.22 = (f32[256,512]{1,0:T(8,128)}, f32[256,512]{1,0:T(8,128)}, u32[]{:S(2)}, u32[]{:S(2)}) collective-permute-start(f32[256,512]{1,0:T(8,128)} %get-tuple-element.243), channel_id=1, source_target_pairs={{0,2},{1,3},{2,0},{3,1},{4,6},{5,7},{6,4},{7,5},{8,10},{9,11},{10,... | collective-permute-start | bytes 1572872 | tf_op jit(solution)/shard_map/ppermute | solution.py:26
  309.2 27.9 %collective-permute-start.23 = (f32[256,512]{1,0:T(8,128)S(1)}, f32[256,512]{1,0:T(8,128)S(1)}, u32[]{:S(2)}, u32[]{:S(2)}) collective-permute-start(f32[256,512]{1,0:T(8,128)S(1)} %get-tuple-element.244), channel_id=1, source_target_pairs={{0,1},{1,0},{2,3},{3,2},{4,5},{5,4},{6,7},{7,6},{8,9},{9,8},{10,11... | collective-permute-start | bytes 1572872 | tf_op jit(solution)/shard_map/ppermute | solution.py:26
  322.1 23.0 %collective-permute-start.24 = (f32[256,512]{1,0:T(8,128)S(1)}, f32[256,512]{1,0:T(8,128)S(1)}, u32[]{:S(2)}, u32[]{:S(2)}) collective-permute-start(f32[256,512]{1,0:T(8,128)S(1)} %get-tuple-element.245), channel_id=1, source_target_pairs={{0,3},{1,2},{2,1},{3,0},{4,7},{5,6},{6,5},{7,4},{8,11},{9,10},{10,... | collective-permute-start | bytes 1572872 | tf_op jit(solution)/shard_map/ppermute | solution.py:26
  360.5 389.4 %all-reduce.29.cloned.1.call-start = ((), (), s32[]{:S(2)}) async-start(), calls=%async_computation | async-start | bytes 14811136 | tf_op jit(solution)/shard_map/psum | solution.py:720
  377.7 66.7 %collective-permute-start.29 = (f32[264,512]{1,0:T(8,128)S(1)}, f32[264,512]{1,0:T(8,128)}, u32[]{:S(2)}, u32[]{:S(2)}) collective-permute-start(f32[264,512]{1,0:T(8,128)S(1)} %pad_maximum_fusion.17), channel_id=1, source_target_pairs={{0,0},{2,1},{4,2},{6,3},{1,4},{3,5},{5,6},{7,7},{8,8},{10,9},{12,1... | collective-permute-start | bytes 1622024 | tf_op jit(solution)/shard_map/ppermute | solution.py:163
  380.0 65.1 %collective-permute-start.30 = (f32[264,512]{1,0:T(8,128)}, f32[264,512]{1,0:T(8,128)}, u32[]{:S(2)}, u32[]{:S(2)}) collective-permute-start(f32[264,512]{1,0:T(8,128)} %pad_maximum_fusion.18), channel_id=1, source_target_pairs={{2,0},{0,1},{6,2},{4,3},{3,4},{1,5},{7,6},{5,7},{10,8},{8,9},{14,1... | collective-permute-start | bytes 1622024 | tf_op jit(solution)/shard_map/ppermute | solution.py:163
  426.8 24.7 %collective-permute-start.34 = (f32[2,512,512]{2,1,0:T(8,128)}, f32[2,512,512]{2,1,0:T(8,128)}, u32[]{:S(2)}, u32[]{:S(2)}) collective-permute-start(f32[2,512,512]{2,1,0:T(8,128)} %slice.945), channel_id=1, source_target_pairs={{0,4},{4,0},{8,12},{12,8},{16,20},{20,16},{24,28},{28,24},{1,5},{5... | collective-permute-start | bytes 6291464 | tf_op jit(solution)/shard_map/ppermute | solution.py:26
  468.0 26.7 %collective-permute-start.35 = (f32[256,512]{1,0:T(8,128)}, f32[256,512]{1,0:T(8,128)}, u32[]{:S(2)}, u32[]{:S(2)}) collective-permute-start(f32[256,512]{1,0:T(8,128)} %get-tuple-element.233), channel_id=1, source_target_pairs={{0,2},{1,3},{2,0},{3,1},{4,6},{5,7},{6,4},{7,5},{8,10},{9,11},{10,... | collective-permute-start | bytes 1572872 | tf_op jit(solution)/shard_map/ppermute | solution.py:26
  504.6 26.9 %collective-permute-start.39 = (f32[256,512]{1,0:T(8,128)S(1)}, f32[256,512]{1,0:T(8,128)S(1)}, u32[]{:S(2)}, u32[]{:S(2)}) collective-permute-start(f32[256,512]{1,0:T(8,128)S(1)} %get-tuple-element.231), channel_id=1, source_target_pairs={{0,3},{1,2},{2,1},{3,0},{4,7},{5,6},{6,5},{7,4},{8,11},{9,10},{10,... | collective-permute-start | bytes 1572872 | tf_op jit(solution)/shard_map/ppermute | solution.py:26
  507.8 57.5 %collective-permute-start.36 = (f32[264,512]{1,0:T(8,128)S(1)}, f32[264,512]{1,0:T(8,128)S(1)}, u32[]{:S(2)}, u32[]{:S(2)}) collective-permute-start(f32[264,512]{1,0:T(8,128)S(1)} %pad_maximum_fusion.21), channel_id=1, source_target_pairs={{0,0},{2,1},{4,2},{6,3},{1,4},{3,5},{5,6},{7,7},{8,8},{10,9},{12,1... | collective-permute-start | bytes 1622024 | tf_op jit(solution)/shard_map/ppermute | solution.py:163
  509.4 65.7 %collective-permute-start.37 = (f32[264,512]{1,0:T(8,128)}, f32[264,512]{1,0:T(8,128)}, u32[]{:S(2)}, u32[]{:S(2)}) collective-permute-start(f32[264,512]{1,0:T(8,128)} %pad_maximum_fusion.22), channel_id=1, source_target_pairs={{2,0},{0,1},{6,2},{4,3},{3,4},{1,5},{7,6},{5,7},{10,8},{8,9},{14,1... | collective-permute-start | bytes 1622024 | tf_op jit(solution)/shard_map/ppermute | solution.py:163
  557.4 19.7 %collective-permute-start.40 = (f32[264,512]{1,0:T(8,128)}, f32[264,512]{1,0:T(8,128)}, u32[]{:S(2)}, u32[]{:S(2)}) collective-permute-start(f32[264,512]{1,0:T(8,128)} %pad_maximum_fusion.23), channel_id=1, source_target_pairs={{1,0},{3,1},{5,2},{7,3},{0,4},{2,5},{4,6},{6,7},{9,8},{11,9},{13,1... | collective-permute-start | bytes 1622024 | tf_op jit(solution)/shard_map/ppermute | solution.py:163
  559.5 30.5 %collective-permute-start.46 = (f32[512,512]{1,0:T(8,128)}, f32[512,512]{1,0:T(8,128)}, u32[]{:S(2)}, u32[]{:S(2)}) collective-permute-start(f32[512,512]{1,0:T(8,128)} %constant_dynamic-slice_fusion.1), channel_id=1, source_target_pairs={{0,16},{4,20},{8,24},{12,28},{16,0},{20,4},{24,8},{28,12},{1,17},{... | collective-permute-start | bytes 3145736 | tf_op jit(solution)/shard_map/ppermute | solution.py:26
  563.0 28.7 %collective-permute-start.43 = (f32[128,2048]{1,0:T(8,128)}, f32[128,2048]{1,0:T(8,128)}, u32[]{:S(2)}, u32[]{:S(2)}) collective-permute-start(f32[128,2048]{1,0:T(8,128)} %constant_dynamic-slice_fusion.4), channel_id=1, source_target_pairs={{0,8},{4,12},{8,0},{12,4},{16,24},{20,28},{24,16},{28,20},{1,9},{5... | collective-permute-start | bytes 3145736 | tf_op jit(solution)/shard_map/ppermute | solution.py:26
  565.3 22.8 %collective-permute-start.41 = (f32[264,512]{1,0:T(8,128)}, f32[264,512]{1,0:T(8,128)}, u32[]{:S(2)}, u32[]{:S(2)}) collective-permute-start(f32[264,512]{1,0:T(8,128)} %pad_maximum_fusion.24), channel_id=1, source_target_pairs={{3,0},{1,1},{7,2},{5,3},{2,4},{0,5},{6,6},{4,7},{11,8},{9,9},{15,1... | collective-permute-start | bytes 1622024 | tf_op jit(solution)/shard_map/ppermute | solution.py:163
  591.5 21.5 %collective-permute-start.47 = (f32[256,512]{1,0:T(8,128)S(1)}, f32[256,512]{1,0:T(8,128)S(1)}, u32[]{:S(2)}, u32[]{:S(2)}) collective-permute-start(f32[256,512]{1,0:T(8,128)S(1)} %constant_dynamic-slice_fusion), channel_id=1, source_target_pairs={{0,8},{4,12},{8,0},{12,4},{16,24},{20,28},{24,16},{28,20},{1,9},{5... | collective-permute-start | bytes 1572872 | tf_op jit(solution)/shard_map/ppermute | solution.py:26
  593.1 20.1 %collective-permute-start.44 = (f32[64,2048]{1,0:T(8,128)S(1)}, f32[64,2048]{1,0:T(8,128)S(1)}, u32[]{:S(2)}, u32[]{:S(2)}) collective-permute-start(f32[64,2048]{1,0:T(8,128)S(1)} %constant_dynamic-slice_fusion.3), channel_id=1, source_target_pairs={{0,16},{4,20},{8,24},{12,28},{16,0},{20,4},{24,8},{28,12},{1,17},{... | collective-permute-start | bytes 1572872 | tf_op jit(solution)/shard_map/ppermute | solution.py:26
  631.9 127.4 %collective-permute-start.51 = (f32[6,512]{1,0:T(8,128)S(1)}, f32[6,512]{1,0:T(8,128)S(1)}, u32[]{:S(2)}, u32[]{:S(2)}) collective-permute-start(f32[6,512]{1,0:T(8,128)S(1)} %add.1130), channel_id=1, source_target_pairs={{0,8},{4,12},{8,0},{12,4},{16,24},{20,28},{24,16},{28,20},{1,9},{5... | collective-permute-start | bytes 36872 | tf_op jit(solution)/shard_map/ppermute | solution.py:26
  766.8 24.1 %collective-permute-start.57 = (f32[512,512]{1,0:T(8,128)S(1)}, f32[512,512]{1,0:T(8,128)S(1)}, u32[]{:S(2)}, u32[]{:S(2)}) collective-permute-start(f32[512,512]{1,0:T(8,128)S(1)} %constant_dynamic-update-slice_fusion.2), channel_id=1, source_target_pairs={{0,16},{4,20},{8,24},{12,28},{16,0},{20,4},{24,8},{28,12},{1,17},{... | collective-permute-start | bytes 3145736 | tf_op jit(solution)/shard_map/ppermute | solution.py:26
  768.4 23.8 %collective-permute-start.54 = (f32[128,2048]{1,0:T(8,128)S(1)}, f32[128,2048]{1,0:T(8,128)S(1)}, u32[]{:S(2)}, u32[]{:S(2)}) collective-permute-start(f32[128,2048]{1,0:T(8,128)S(1)} %constant_dynamic-update-slice_fusion.6), channel_id=1, source_target_pairs={{0,8},{4,12},{8,0},{12,4},{16,24},{20,28},{24,16},{28,20},{1,9},{5... | collective-permute-start | bytes 3145736 | tf_op jit(solution)/shard_map/ppermute | solution.py:26
  (234 other events, 2715.6 us)
Sparse Core Ops, SparseCore 0:
  360.6 124.2 all-reduce.30
  574.7 175.2 all-reduce.28

commit v2 on v1

--- a/solution.py
+++ b/solution.py
@@ -11,6 +11,7 @@
 EPS = 1e-05
 FAR = 1e30
 LANES = 128
+BRIEF = pl.CostEstimate(flops=1, bytes_accessed=1, transcendentals=0)
 
 
 def product(left, right):
@@ -59,17 +60,21 @@
     return lax.dynamic_update_slice_in_dim(out, other, (1 - side) * half, 0)
 
 
-def reduce_pair(pair, steps, meanwhile):
-    first, rest = steps[0], steps[1:]
-    orders = [(first,) + tuple(rest), (first,) + tuple(rest[::-1])]
-    pair = list(pair)
-    for k in range(len(steps)):
-        pair = [halve(part, order[k]) for part, order in zip(pair, orders)]
-    middle = tuple(pair)
-    pair, meanwhile = lax.optimization_barrier((pair, meanwhile))
-    for k in range(len(steps) - 1, 0, -1):
-        pair = [join(part, order[k]) for part, order in zip(pair, orders)]
-    return [(part, swap(part, *first)) for part in pair], upper(first), middle, meanwhile
+class DenseSum:
+    def __init__(self, pair):
+        first, *rest = bits_of("dp")
+        far = bits_of("ep")[::-1]
+        self.orders = [[first] + rest + far, [first] + rest[::-1] + far]
+        self.parts = list(pair)
+        count = len(self.orders[0])
+        self.ways = [(halve, k) for k in range(count)] + [(join, k) for k in range(count - 1, -1, -1)]
+
+    def step(self, value, count=1):
+        for _ in range(count):
+            way, k = self.ways.pop(0)
+            self.parts = [way(part, order[k]) for part, order in zip(self.parts, self.orders)]
+        value, self.parts = lax.optimization_barrier((value, self.parts))
+        return value
 
 
 class Layout:
@@ -111,9 +116,7 @@
 
     def hops(self, values, group):
         half = values.shape[0] // 2
-        return jnp.concatenate(
-            [self.hop(values[h * half : (h + 1) * half], group + h * (self.ep // 2)) for h in (0, 1)], axis=0
-        )
+        return [self.hop(values[h * half : (h + 1) * half], group + h * (self.ep // 2)) for h in (0, 1)]
 
     def group_of(self, values, group):
         return self.piece(values, group * 2 * self.micro, 2 * self.micro)
@@ -144,12 +147,11 @@
                 order = [(u, h) for h in (0, 1) for u in (0, 1)]
                 rows_got = [self.piece(rows_got[u], h, 1) for u, h in order]
                 more_got = [self.piece(more_got[u], h, 1, 1) for u, h in order]
-            out.append((jnp.concatenate(rows_got, axis=0), jnp.concatenate(more_got, axis=1).T))
+            out.append((jnp.concatenate(rows_got, axis=0), jnp.concatenate(more_got, axis=1)))
         return out
 
     def expert_to_home(self, groups):
-        rows_out, more_out = [], []
-        count = self.micro * self.capacity
+        messages = []
         for group, (rows, more) in enumerate(groups):
             wide = rows.shape[1]
             for u in (0, 1):
@@ -158,14 +160,21 @@
                     few = jnp.concatenate([self.piece(more, 2 * h + u, 1, 1) for h in (0, 1)], axis=1)
                 else:
                     row, few = self.piece(rows, u * self.micro, self.micro), self.piece(more, u * self.micro, self.micro, 1)
-                message = jnp.concatenate([row, jnp.pad(few, ((0, 0), (0, wide - count)))], axis=0)
+                message = row
+                if more.shape[0]:
+                    message = jnp.concatenate([row, jnp.pad(few, ((0, 0), (0, wide - few.shape[1])))], axis=0)
                 if self.paired:
-                    got = lax.ppermute(message, ("dp", "ep"), self.route(group, u, True))
+                    messages.append(lax.ppermute(message, ("dp", "ep"), self.route(group, u, True)))
                 else:
-                    got = self.hop(message, group + u * (self.ep // 2))
-                rows_out.append(got[:count])
-                more_out.append(got[count:, :count])
-        return jnp.concatenate(rows_out, axis=0), jnp.concatenate(more_out, axis=1)
+                    messages.append(self.hop(message, group + u * (self.ep // 2)))
+        return messages
+
+    def opened(self, messages):
+        count = self.micro * self.capacity
+        return (
+            jnp.concatenate([v[:count] for v in messages], axis=0),
+            jnp.concatenate([v[count:, :count] for v in messages], axis=1),
+        )
 
     def ids_to_work(self, ids):
         if not self.paired:
@@ -268,34 +277,188 @@
     return jnp.matmul(values, table.astype(jnp.float32), precision=HIGH)
 
 
-def expert_forward(hidden, extra, own, gain, shift, router, weight_in, weight_out):
-    def front(source, gain_now, shift_now, router_now, extra_now):
-        normed = norm_rows(source, gain_now, shift_now)
-        probs = jax.nn.softmax(product(normed, router_now) + extra_now, axis=-1)
-        return (normed, jnp.sum(probs * own, axis=-1))
-
-    (normed, gate), front_pull = jax.vjp(front, hidden, gain, shift, router, extra)
-    pre = product(normed, weight_in)
-    result = product(jax.nn.silu(pre), weight_out)
-    new = hidden + 0.5 * gate[:, None] * result
-    return (new, (front_pull, normed, gate, pre, result))
-
-
-def expert_backward(grad, saved, weight_in, weight_out):
-    front_pull, normed, gate, pre, result = saved
-    grad_result = 0.5 * gate[:, None] * grad
-    grad_gate = 0.5 * jnp.sum(grad * result, axis=1)
-    grad_active = jnp.einsum("cd,fd->cf", grad_result, weight_out, precision=HIGH)
-    grad_pre = grad_active * swish_slope(pre)
-    grad_normed = jnp.einsum("cf,df->cd", grad_pre, weight_in, precision=HIGH)
-    grad_hidden, gain_grad, shift_grad, router_grad, extra_grad = front_pull((grad_normed, grad_gate))
-    return (grad + grad_hidden, extra_grad, (gain_grad, shift_grad, router_grad), (normed, jax.nn.silu(pre), grad_result, grad_pre))
+def product_two(left, right, dot):
+    head, rest = parted(left)
+    return dot(narrow(head), right) + dot(narrow(rest), right)
+
+
+def exact_dot(left, right, contract):
+    return lax.dot_general(
+        left, right, (contract, ((), ())), precision=lax.Precision.HIGHEST, preferred_element_type=jnp.float32
+    )
+
+
+def norm_parts(values):
+    center = values - jnp.mean(values, axis=1, keepdims=True)
+    scale = lax.rsqrt(jnp.mean(center * center, axis=1, keepdims=True) + EPS)
+    return center * scale, scale
+
+
+def norm_back(grad, gain, normal, scale):
+    weighed = grad * gain
+    centred = weighed - jnp.mean(weighed, axis=1, keepdims=True)
+    return scale * (centred - normal * jnp.mean(weighed * normal, axis=1, keepdims=True))
+
+
+def gate_parts(hidden, extra, own, norm, router, experts):
+    normal, scale = norm_parts(hidden)
+    normed = normal * norm[0:1] + norm[1:2]
+    lane = lax.broadcasted_iota(jnp.int32, (1, LANES), 1)
+    logits = exact_dot(normed, router, ((1,), (0,))) + extra
+    logits = jnp.where(lane < experts, logits, -FAR)
+    raised = jnp.exp(logits - jnp.max(logits, axis=1, keepdims=True))
+    probs = raised / jnp.sum(raised, axis=1, keepdims=True)
+    return normal, scale, normed, probs, jnp.sum(probs * own, axis=1, keepdims=True)
+
+
+def hidden_columns(weight_in):
+    wide = min(512, weight_in.shape[1])
+    return [pl.ds(at, wide) for at in range(0, weight_in.shape[1], wide)]
+
+
+def forward_part(hidden, extra, own, norm, router, weight_in, weight_out, pre, experts):
+    parts = gate_parts(hidden, extra, own, norm, router, experts)
+    result = 0.0
+    for now in hidden_columns(weight_in):
+        before = product_two(parts[2], weight_in[:, now], dot_nn)
+        pre[:, now] = before
+        result = result + product_two(before * jax.nn.sigmoid(before), weight_out[now, :], dot_nn)
+    return parts, result, hidden + 0.5 * parts[4] * result
+
+
+def backward_part(grad, result, parts, own, norm, router, weight_in, weight_out, pre, active, grad_pre):
+    normal, scale, normed, probs, gate = parts
+    grad_result = 0.5 * gate * grad
+    grad_gate = 0.5 * jnp.sum(grad * result, axis=1, keepdims=True)
+    grad_logits = grad_gate * probs * (own - gate)
+    grad_normed = exact_dot(grad_logits, router, ((1,), (1,)))
+    for now in hidden_columns(weight_in):
+        before = pre[:, now]
+        squash = jax.nn.sigmoid(before)
+        active[:, now] = before * squash
+        slope = squash * (1.0 + before * (1.0 - squash))
+        now_grad = product_two(grad_result, weight_out[now, :], dot_nt) * slope
+        grad_pre[:, now] = now_grad
+        grad_normed = grad_normed + product_two(now_grad, weight_in[:, now], dot_nt)
+    sums = [jnp.sum(grad_normed * normal, axis=0, keepdims=True), jnp.sum(grad_normed, axis=0, keepdims=True)]
+    return grad + norm_back(grad_normed, norm[0:1], normal, scale), grad_result, grad_logits, sums
+
+
+def add_rows(out, rows):
+    @pl.when(pl.program_id(0) == 0)
+    def _():
+        out[...] = jnp.zeros_like(out)
+
+    for at, row in enumerate(rows):
+        out[at : at + 1, :] += row
+
+
+def forward_kernel(experts, hidden, extra, own, norm, router, weight_in, weight_out, new, result, pre):
+    _, result[...], new[...] = forward_part(
+        hidden[...], extra[...], own[...], norm[...], router[...], weight_in, weight_out, pre, experts
+    )
+
+
+def backward_kernel(
+    experts, hidden, extra, grad, result, pre, own, norm, router, weight_in, weight_out,
+    back, logits, normed, active, grad_result, grad_pre, sums,
+):
+    parts = gate_parts(hidden[...], extra[...], own[...], norm[...], router[...], experts)
+    back[...], grad_result[...], logits[...], rows = backward_part(
+        grad[...], result[...], parts, own[...], norm[...], router[...], weight_in, weight_out, pre, active, grad_pre
+    )
+    normed[...] = parts[2]
+    add_rows(sums, rows)
+
+
+def both_kernel(
+    experts, hidden, extra, pull, own, norm, last, router, weight_in, weight_out,
+    output, back, logits, normed, active, grad_result, grad_pre, sums, pre,
+):
+    parts, result, new = forward_part(
+        hidden[...], extra[...], own[...], norm[...], router[...], weight_in, weight_out, pre, experts
+    )
+    lane = lax.broadcasted_iota(jnp.int32, (1, LANES), 1)
+    valid = jnp.sum(jnp.where(lane == experts, extra[...], 0.0), axis=1, keepdims=True)
+    normal, scale = norm_parts(new)
+    output[...] = (normal * last[0:1] + last[1:2]) * valid
+    grad = pull[...] * valid
+    last_sums = [jnp.sum(grad * normal, axis=0, keepdims=True), jnp.sum(grad, axis=0, keepdims=True)]
+    back[...], grad_result[...], logits[...], rows = backward_part(
+        norm_back(grad, last[0:1], normal, scale), result, parts, own[...], norm[...], router[...],
+        weight_in, weight_out, pre, active, grad_pre,
+    )
+    normed[...] = parts[2]
+    add_rows(sums, rows + last_sums)
+
+
+def expert_call(kernel, name, experts, by_rows, fixed, widths, sums, hold, products):
+    rows, width = by_rows[0].shape
+    block = min(256, rows)
+    row_spec = lambda wide: pl.BlockSpec((block, wide), lambda i: (i, 0))
+    full = lambda v: pl.BlockSpec(v.shape, lambda i: (0, 0))
+    out_specs = [row_spec(wide) for wide in widths]
+    out_shape = [jax.ShapeDtypeStruct((rows, wide), jnp.float32) for wide in widths]
+    if sums:
+        out_specs.append(pl.BlockSpec((8, width), lambda i: (0, 0)))
+        out_shape.append(jax.ShapeDtypeStruct((8, width), jnp.float32))
+    inner = fixed[-2].shape[1]
+    return pl.pallas_call(
+        functools.partial(kernel, experts),
+        grid=(rows // block,),
+        in_specs=[row_spec(v.shape[1]) for v in by_rows] + [full(v) for v in fixed],
+        out_specs=out_specs,
+        out_shape=out_shape,
+        scratch_shapes=[pltpu.VMEM((block, inner), jnp.float32)] if hold else [],
+        compiler_params=pltpu.CompilerParams(vmem_limit_bytes=48 * 1024 * 1024),
+        cost_estimate=BRIEF,
+        name=name,
+    )(*by_rows, *fixed)
+
+
+def lanes_of(extra):
+    return jnp.pad(extra.T, ((0, 0), (0, LANES - extra.shape[0])))
+
+
+def weight_kernel(groups, *refs):
+    normed, grad_result, active, grad_pre = (refs[k * groups : (k + 1) * groups] for k in range(4))
+    inner, outer = refs[4 * groups :]
+
+    def summed(left, right):
+        total = 0.0
+        for one, two in zip(left, right):
+            (a_hi, a_lo), (b_hi, b_lo) = parted(one[...]), parted(two[...])
+            a_hi, a_lo, b_hi, b_lo = narrow(a_hi), narrow(a_lo), narrow(b_hi), narrow(b_lo)
+            total = total + dot_tn(a_hi, b_hi) + dot_tn(a_lo, b_hi) + dot_tn(a_hi, b_lo)
+        return total
+
+    outer[...] = summed(active, grad_result)
+    inner[...] = summed(normed, grad_pre)
 
 
 def expert_weight_grads(kept):
-    normed, active, grad_result, grad_pre = kept
-    outer = jnp.einsum("cf,cd->fd", active, grad_result, precision=HIGH)
-    return jnp.einsum("cd,cf->df", normed, grad_pre, precision=HIGH), outer
+    normed, active, grad_result, grad_pre = zip(*kept)
+    rows, width = normed[0].shape
+    inner = active[0].shape[1]
+    wide = min(512, inner)
+    full = pl.BlockSpec((rows, width), lambda i: (0, 0))
+    part = pl.BlockSpec((rows, wide), lambda i: (0, i))
+    count = len(kept)
+    return pl.pallas_call(
+        functools.partial(weight_kernel, count),
+        grid=(inner // wide,),
+        in_specs=[full] * (2 * count) + [part] * (2 * count),
+        out_specs=[pl.BlockSpec((width, wide), lambda i: (0, i)), pl.BlockSpec((wide, width), lambda i: (i, 0))],
+        out_shape=[
+            jax.ShapeDtypeStruct((width, inner), jnp.float32),
+            jax.ShapeDtypeStruct((inner, width), jnp.float32),
+        ],
+        compiler_params=pltpu.CompilerParams(vmem_limit_bytes=48 * 1024 * 1024),
+        cost_estimate=pl.CostEstimate(
+            flops=12 * count * rows * width * inner, bytes_accessed=16 * count * rows * inner, transcendentals=0
+        ),
+        name="weights",
+    )(*normed, *grad_result, *active, *grad_pre)
 
 
 def add_up(trees):
@@ -442,9 +605,7 @@
 def attend_params(rows, total, width, passes):
     return dict(
         compiler_params=pltpu.CompilerParams(vmem_limit_bytes=40 * 1024 * 1024),
-        cost_estimate=pl.CostEstimate(
-            flops=2 * rows * total * width * passes, bytes_accessed=16 * total * width, transcendentals=rows * total * 8
-        ),
+        cost_estimate=BRIEF,
     )
 
 
@@ -527,8 +688,8 @@
     mixing_weight = attention_out.astype(jnp.float32)
     point_weight = conv_point.astype(jnp.float32)
     project_weight = conv_out.astype(jnp.float32)
-    inner_weight = expert_in[:, 0].astype(jnp.float32)
-    outer_weight = expert_out[:, 0].astype(jnp.float32)
+    inner_weight = [expert_in[b, 0] for b in (0, 1)]
+    outer_weight = [expert_out[b, 0] for b in (0, 1)]
     micro, rows, width = frames.shape
     experts = router.shape[2]
     heads = slopes.shape[0]
@@ -546,7 +707,10 @@
     spread = lambda v: jnp.broadcast_to(v[:, None], (parts, part_rows) + v.shape[1:]).reshape(parts * part_rows, -1)
 
     slots = experts * micro * capacity
-    own = (jnp.arange(experts, dtype=jnp.int32) == layout.z).astype(jnp.float32)[None, :]
+    own = (jnp.arange(LANES, dtype=jnp.int32) == layout.z).astype(jnp.float32)[None, :]
+    norms = [jnp.stack([norm_gain[i], norm_bias[i]]) for i in range(norm_gain.shape[0])]
+    routers = [jnp.pad(router[b], ((0, 0), (0, LANES - experts))) for b in (0, 1)]
+    wide = inner_weight[0].shape[1]
     ids = jnp.moveaxis(expert_ids[..., 0], 0, 2)
     rank = [ranks(ids[..., b], experts) for b in (0, 1)]
     home = [tables_of(layout.home_slots(ids[..., b], rank[b]), slots) for b in (0, 1)]
@@ -566,19 +730,14 @@
     last = ()
     for group in groups:
         hidden, extra = sources[group]
-        new, kept = expert_forward(
-            after(hidden, *last),
-            extra[:, :experts],
-            own,
-            norm_gain[0],
-            norm_bias[0],
-            router[0],
-            inner_weight[0],
-            outer_weight[0],
+        hidden, extra = after(hidden, *last), lanes_of(extra)
+        fixed = (own, norms[0], routers[0], inner_weight[0], outer_weight[0])
+        new, result, pre = expert_call(
+            forward_kernel, "forward", experts, (hidden, extra), fixed, (width, width, wide), False, False, 2
         )
         last = (new,)
-        kept_first.append(kept)
-        back.append(layout.hops(new, group))
+        kept_first.append(((hidden, extra), (result, pre), fixed))
+        back += layout.hops(new, group)
     work_ids = layout.ids_to_work(after(ids, sources[-1][0]))
     work = [
         tables_of(layout.work_slots(work_ids[..., b], ranks(work_ids[..., b], experts)), slots) for b in (0, 1)
@@ -627,38 +786,33 @@
     swished = jax.nn.silu(shaped)
     third = second + product(swished, project_weight)
 
-    def final(values, gain_now, shift_now, valid_now):
-        return norm_rows(values, gain_now, shift_now) * valid_now
-
     sent = pick(work[1][0], third)
     results, back, kept, small = [], [], [], []
     arrived, last = (), ()
     for group in groups:
         hidden = layout.hops(after(layout.group_of(sent, group), *arrived), group)
-        arrived = (hidden,)
+        arrived = tuple(hidden)
         pull_now, extra = pulls[group]
-        fourth, saved = expert_forward(
-            after(hidden, *last),
-            extra[:, :experts],
-            own,
-            norm_gain[3],
-            norm_bias[3],
-            router[1],
-            inner_weight[1],
-            outer_weight[1],
+        result, grad, grad_logits, normed, active, grad_result, grad_pre, sums = expert_call(
+            both_kernel,
+            "both",
+            experts,
+            (jnp.concatenate(after(hidden, *last), axis=0), lanes_of(extra), pull_now),
+            (own, norms[3], norms[4], routers[1], inner_weight[1], outer_weight[1]),
+            (width, width, LANES, width, wide, width, wide),
+            True,
+            True,
+            4,
         )
-        valid_now = extra[:, experts : experts + 1]
-        result, final_pull = jax.vjp(lambda v, g, b: final(v, g, b, valid_now), fourth, norm_gain[4], norm_bias[4])
-        grad_fourth, gain_four, shift_four = final_pull(pull_now)
-        grad, extra_grad, small_now, kept_now = expert_backward(grad_fourth, saved, inner_weight[1], outer_weight[1])
         last = (grad,)
-        results.append((result, jnp.pad(extra_grad.T, ((0, -experts % 8), (0, 0)))))
-        kept.append(kept_now)
-        small.append(small_now + (gain_four, shift_four))
-        back.append(layout.hops(grad, group))
-    gain_three, shift_three, router_one, gain_four, shift_four = add_up(small)
-    kept, _ = lax.optimization_barrier((kept, back[:-1]))
-    inner_one, outer_one = lax.psum(add_up([expert_weight_grads(v) for v in kept]), "dp")
+        results.append((result, grad_logits[:, : experts + (-experts % 8)].T))
+        kept.append((normed, active, grad_result, grad_pre))
+        small.append((sums, product(normed.T, grad_logits[:, :experts])))
+        back += layout.hops(grad, group)
+    sums, router_one = add_up(small)
+    gain_three, shift_three, gain_four, shift_four = (sums[k] for k in range(4))
+    kept, _ = lax.optimization_barrier((kept, back[:-2]))
+    expert_one = lax.psum(expert_weight_grads(kept), "dp")
     grad_third = pick(work[1][1], jnp.concatenate(back, axis=0))
     project_grad = product(swished.T, grad_third)
     grad_shaped = product(grad_third, project_weight.T) * swish_slope(shaped)
@@ -668,7 +822,7 @@
     totals = layout.batch_total(sums)
     shift_total, gain_total = totals[:, 0], totals[:, 1]
     results, _ = lax.optimization_barrier((results, totals))
-    output_slots, logit_slots = layout.expert_to_home(results)
+    output_slots, logit_slots = layout.opened(layout.expert_to_home(results))
     output = pick(home[1][1], output_slots).reshape(micro, rows, width)
     logit_one = pick_columns(logit_slots[:experts], home[1][0])
     router_one = router_one + product(logit_one, home_rows).T
@@ -715,48 +869,61 @@
         ],
         axis=0,
     )
-    few = early.shape[0]
-    mixing_grad = jnp.concatenate([mixing_grad, jnp.pad(early, ((0, -few % 8), (0, 0)))], axis=0)
-    packed_grad, mixing_grad, project_grad, point_grad = lax.psum(
-        after((packed_grad, mixing_grad, project_grad, point_grad), inner_one), ("dp", "ep")
-    )
-    mixing_grad, early = mixing_grad[:width], mixing_grad[width:]
+    dense = DenseSum(
+        [jnp.concatenate([packed_grad, project_grad], axis=1), jnp.concatenate([mixing_grad, point_grad], axis=1)]
+    )
+    over_dp, over_ep = len(bits_of("dp")), len(bits_of("ep"))
 
     sent = pick(work[0][0], grad_first)
     sources, kept, small = [], [], []
     arrived, last = (), ()
     for group in groups:
         grad = layout.hops(after(layout.group_of(sent, group), *arrived), group)
-        arrived = (grad,)
-        grad, extra_grad, small_now, kept_now = expert_backward(
-            after(grad, *last), kept_first[group], inner_weight[0], outer_weight[0]
+        arrived = tuple(grad)
+        grad = after(grad, *last)
+        if group == 0:
+            grad, expert_one = lax.optimization_barrier((dense.step(grad), expert_one))
+        if group == 1:
+            grad = dense.step(grad)
+        (hidden, extra), saved, fixed = kept_first[group]
+        new, grad_logits, normed, active, grad_result, grad_pre, sums = expert_call(
+            backward_kernel,
+            "backward",
+            experts,
+            (hidden, extra, jnp.concatenate(grad, axis=0)) + saved,
+            fixed,
+            (width, LANES, width, wide, width, wide),
+            True,
+            False,
+            2,
         )
-        last = (grad,)
-        sources.append((grad, jnp.pad(extra_grad.T, ((0, -experts % 8), (0, 0)))))
-        kept.append(kept_now)
-        small.append(small_now)
-    gain_zero, shift_zero, router_zero = add_up(small)
-    expert_zero = add_up([expert_weight_grads(v) for v in kept])
-    dense = (packed_grad, mixing_grad, early, project_grad, point_grad)
-    halves_zero, side, middle, dense = reduce_pair(expert_zero, bits_of("dp"), dense)
-    packed_grad, mixing_grad, early, project_grad, point_grad = dense
-    rows_back, logit_slots = layout.expert_to_home(sources)
-    rows_back, logit_slots, inner_one, outer_one, _ = lax.optimization_barrier(
-        (rows_back, logit_slots, inner_one, outer_one, middle)
-    )
+        if group == 0:
+            new = dense.step(new, over_dp - 2)
+        if group == 1:
+            new = dense.step(new, over_ep - 1)
+        last = (new,)
+        sources.append((new, grad_logits[:, : experts + (-experts % 8)].T))
+        kept.append((normed, active, grad_result, grad_pre))
+        small.append((sums, product(normed.T, grad_logits[:, :experts])))
+    sums, router_zero = add_up(small)
+    gain_zero, shift_zero = sums[0], sums[1]
+    expert_zero = lax.psum(expert_weight_grads(kept), "dp")
+    sources = dense.step(sources, over_ep + 1)
+    frame_messages = layout.expert_to_home(sources)
+    frame_messages = dense.step(frame_messages, over_dp - 1)
+    rows_back, logit_slots = layout.opened(frame_messages)
     logit_zero = pick_columns(logit_slots[:experts], home[0][0])
     router_zero = router_zero + product(logit_zero, home_rows).T
     frames_grad = pick(home[0][1], rows_back).reshape(micro, rows, width)
-    late = butterfly(
-        jnp.concatenate([gain_zero[None], shift_zero[None], router_zero.T], axis=0),
-        bits_of("ep") + bits_of("dp"),
-    )
+    late = jnp.concatenate([gain_zero[None], shift_zero[None], router_zero.T, early], axis=0)
+    late = butterfly(dense.step(late), bits_of("ep") + bits_of("dp"))
+    late, early = late[: 2 + experts], late[2 + experts :]
+    packed_grad, project_grad = dense.parts[0][:, : 3 * width], dense.parts[0][:, 3 * width :]
+    mixing_grad, point_grad = dense.parts[1][:, :width], dense.parts[1][:, width:]
     expert_grads = []
-    for one, (mine, other) in zip((inner_one, outer_one), halves_zero):
-        whole = lax.pad(one[None], 0.0, ((1, 0, 0), (0, 0, 0), (0, 0, 0)))
-        half_rows = mine.shape[0]
-        whole = lax.dynamic_update_slice(whole, mine[None], (0, side * half_rows, 0))
-        expert_grads.append(lax.dynamic_update_slice(whole, other[None], (0, (1 - side) * half_rows, 0))[:, None])
+    for zero, one in zip(expert_zero, expert_one):
+        whole = lax.optimization_barrier(lax.pad(after(one, late)[None], 0.0, ((1, 0, 0), (0, 0, 0), (0, 0, 0))))
+        expert_grads.append(lax.dynamic_update_slice(whole, zero[None], (0, 0, 0))[:, None])
 
     at = 8 + experts
     gain_grad = jnp.concatenate([late[:1], early[:4]], axis=0)

time: 824 us -> 764 us (0.927)
  waiting for transfers between devices: 303 us -> 152 us
  Pallas kernels: 39.7 us -> 162 us
  matrix products: 160 us -> 55.1 us
  local copies, waits for them, and re-layouts: 74.9 us -> 149 us
    pallas_call x0 -> x8, Pallas kernels: none -> 122 us  [the longest x6 86.8 us: expert_call(): pl.pallas_call(functools.partial(kernel, experts), grid=(rows // block,),...]
    psum x2, waiting for transfers between devices: 116 us -> 0.02 us  [the longest x1 0.02 us: body(): expert_zero = lax.psum(expert_weight_grads(kept), 'dp')]
    dot_general x16 -> x0, matrix products: 59.2 us -> none  [the longest x4 20.1 us: expert_weight_grads(): outer = jnp.einsum('cf,cd->fd', active, grad_result, precision=HIGH)]
    dot_general x36 -> x20, matrix products: 81.4 us -> 36.7 us  [product(): return jnp.matmul(left, right, precision=HIGH)]
    pad x2 -> x8, local copies, waits for them, and re-layouts: 0.02 us -> 13.2 us  [the longest x2 8.82 us: body(): lax.pad(after(one, late)[None], 0.0, ((1, 0, 0), (0, 0, 0), (0, 0, 0)))]
    ppermute x8, waiting for transfers between devices: 13.1 us -> 0.02 us  [expert_to_home(): lax.ppermute(message, ('dp', 'ep'), self.route(group, u, True))]
    slice x30 -> x38, local copies, waits for them, and re-layouts: 10.8 us -> 23.4 us  [piece(): lax.slice_in_dim(values, at * self.capacity, (at + count) * self.capacity...]
    unnamed x428 -> x377, local copies, waits for them, and re-layouts: 13.5 us -> 25.2 us
  transfers between devices with their start and end apart: 61 -> 69, of which waited for: 25 -> 26; matrix products, arithmetic and copies ran while one was open for 30% -> 30% of each run, Pallas kernels for 5% -> 22%
where the time goes in v2:
time: 764 us; the launch traced here: 753 us
  Pallas kernels  162 us (21%)
  waiting for transfers between devices  152 us (20%)
  local copies, waits for them, and re-layouts  149 us (20%)
  starting transfers between devices  136 us (18%)
  other arithmetic  80.3 us (11%)
  matrix products  55.1 us (7%)
  between operations  17.7 us (2%)
    ppermute x49, waiting for transfers between devices, swap(): return lax.ppermute(values, axis, [(i, i ^ bit) for i in range(count)])  145 us
    pallas_call x6, Pallas kernels, expert_call(): pl.pallas_call(functools.partial(kernel, experts), grid=(rows // block,),...  86.8 us
    ppermute x49, starting transfers between devices, swap(): return lax.ppermute(values, axis, [(i, i ^ bit) for i in range(count)])  61.3 us
    ppermute x8, starting transfers between devices, home_to_expert(): got.append(lax.ppermute(message, ('dp', 'ep'), self.route(group, u, False)))  39.1 us
    dot_general x20, matrix products, product(): return jnp.matmul(left, right, precision=HIGH)  36.7 us
    pallas_call x2, Pallas kernels, expert_weight_grads(): pl.pallas_call(functools.partial(weight_kernel, count), grid=(inner // wi...  35.3 us
    pallas_call x1, Pallas kernels, attend_back(): pl.pallas_call(functools.partial(attend_back_kernel, chunk, (width // slo...  26.4 us
    unnamed x377, local copies, waits for them, and re-layouts  25.2 us
  transfers between devices with their start and end apart: 69, of which 26 were waited for; matrix products, arithmetic and copies ran while one was open for 30% of the time, Pallas kernels for 22%

profile of v2, /device:TPU:0, one launch (start us, length us, event | category | flops | bytes accessed | tf_op | source)
XLA Modules:
  0.0 752.8 jit_solution(8458103129081208778)
XLA Ops:
  15.8 5.8 collective-permute-start
  31.6 4.8 slice_bitcast_fusion.2
  36.4 10.1 %collective-permute-start.2 = (f32[264,512]{1,0:T(8,128)}, f32[264,512]{1,0:T(8,128)}, u32[]{:S(2)}, u32[]{:S(2)}) collective-permute-start(f32[264,512]{1,0:T(8,128)} %get-tuple-element.125), channel_id=1, source_target_pairs={{0,1},{1,3},{2,5},{3,7},{4,0},{5,2},{6,4},{7,6},{8,9},{9,11},{10,1... | collective-permute-start | bytes 1622024 | tf_op jit(solution)/shard_map/ppermute | solution.py:140
  46.5 5.1 collective-permute-start.3
  57.2 9.4 %forward.2 = (f32[512,512]{1,0:T(8,128)S(1)}, f32[512,512]{1,0:T(8,128)S(1)}, f32[512,2048]{1,0:T(8,128)}) custom-call(f32[512,512]{1,0:T(8,128)S(1)} %pad_maximum_fusion.9.hidden, f32[512,128]{1,0:T(8,128)S(1)} %pad.89.extra, f32[1,128]{1,0:T(1,128)S(1)} %compare_convert_fusion.2.own, f32[2,512]{1,0:T(2,128)S(1)} %get-tuple-element.495.norm, ...), custom_call_target="tpu_custom_call" | custom-call | flops 1 | bytes 1 | tf_op jit(solution)/shard_map/forward/pallas_call | solution.py:406
  70.7 20.0 %collective-permute-start.5 = (f32[2,256]{1,0:T(2,128)S(1)}, f32[2,256]{1,0:T(2,128)S(1)}, u32[]{:S(2)}, u32[]{:S(2)}) collective-permute-start(f32[2,256]{1,0:T(2,128)S(1)} %bitcast.354), channel_id=1, source_target_pairs={{0,2},{1,0},{2,6},{3,4},{4,3},{5,1},{6,7},{7,5},{8,10},{9,8},{10,1... | collective-permute-start | bytes 6152 | tf_op jit(solution)/shard_map/ppermute | solution.py:191
  93.8 9.4 %forward.3 = (f32[512,512]{1,0:T(8,128)S(1)}, f32[512,512]{1,0:T(8,128)S(1)}, f32[512,2048]{1,0:T(8,128)}) custom-call(f32[512,512]{1,0:T(8,128)S(1)} %pad_maximum_fusion.8.hidden, f32[512,128]{1,0:T(8,128)S(1)} %pad.91.extra, f32[1,128]{1,0:T(1,128)S(1)} %compare_convert_fusion.2.own, f32[2,512]{1,0:T(2,128)S(1)} %get-tuple-element.495.norm, ...), custom_call_target="tpu_custom_call" | custom-call | flops 1 | bytes 1 | tf_op jit(solution)/shard_map/forward/pallas_call | solution.py:406
  108.3 7.6 %collective-permute-done.7 = f32[256,512]{1,0:T(8,128)S(1)} collective-permute-done((f32[256,512]{1,0:T(8,128)S(1)}, f32[256,512]{1,0:T(8,128)S(1)}, u32[]{:S(2)}, u32[]{:S(2)}) %collective-permute-start.7) | collective-permute-done | bytes 524320 | tf_op jit(solution)/shard_map/ppermute | solution.py:27
  116.0 13.9 %collective-permute-done.8 = f32[256,512]{1,0:T(8,128)S(1)} collective-permute-done((f32[256,512]{1,0:T(8,128)S(1)}, f32[256,512]{1,0:T(8,128)S(1)}, u32[]{:S(2)}, u32[]{:S(2)}) %collective-permute-start.8) | collective-permute-done | bytes 524320 | tf_op jit(solution)/shard_map/ppermute | solution.py:27
  139.9 5.8 collective-permute-start.16
  152.3 7.3 collective-permute-done.17
  159.6 8.7 %collective-permute-start.20 = (f32[264,512]{1,0:T(8,128)}, f32[264,512]{1,0:T(8,128)}, u32[]{:S(2)}, u32[]{:S(2)}) collective-permute-start(f32[264,512]{1,0:T(8,128)} %select_maximum_fusion.1), channel_id=1, source_target_pairs={{0,1},{1,3},{2,5},{3,7},{4,0},{5,2},{6,4},{7,6},{8,9},{9,11},{10,1... | collective-permute-start | bytes 1622024 | tf_op jit(solution)/shard_map/ppermute | solution.py:140
  178.5 13.4 %attend.1 = (f32[512,512]{1,0:T(8,128)S(1)}, f32[4,8,512]{2,1,0:T(8,128)S(1)}) custom-call(f32[8]{0:T(128)S(1)} %copy-done.33, f32[1024,512]{1,0:T(8,128)S(1)} %convert_select_fusion.dist, f32[512,1536]{1,0:T(8,128)S(1)} %copy-done.6, f32[1024,1024]{1,0:T(8,128)S(1)} %pad_maximum_fusion.k_ref.v_ref, f32[1024,1024]{1,0:T(8,128)S(1)} %pad_maximum_fusion.k_ref.v_ref), custom_call_target="tpu_custom_call" | custom-call | flops 1 | bytes 1 | tf_op jit(solution)/shard_map/attend/pallas_call | solution.py:618
  232.5 18.2 %collective-permute-done.15 = f32[256,512]{1,0:T(8,128)S(1)} collective-permute-done((f32[256,512]{1,0:T(8,128)S(1)}, f32[256,512]{1,0:T(8,128)S(1)}, u32[]{:S(2)}, u32[]{:S(2)}) %collective-permute-start.15) | collective-permute-done | bytes 524320 | tf_op jit(solution)/shard_map/ppermute | solution.py:27
  253.5 19.6 %both.2 = (f32[512,512]{1,0:T(8,128)S(1)}, f32[512,512]{1,0:T(8,128)S(1)}, f32[512,128]{1,0:T(8,128)S(1)}, f32[512,512]{1,0:T(8,128)S(1)}, f32[512,2048]{1,0:T(8...) custom-call(f32[512,512]{1,0:T(8,128)S(1)} %pad_maximum_fusion.10.hidden, ...), custom_call_target="tpu_custom_call" | custom-call | flops 1 | bytes 1 | tf_op jit(solution)/shard_map/both/pallas_call | solution.py:406
  285.0 19.5 %both.3 = (f32[512,512]{1,0:T(8,128)S(1)}, f32[512,512]{1,0:T(8,128)S(1)}, f32[512,128]{1,0:T(8,128)S(1)}, f32[512,512]{1,0:T(8,128)S(1)}, f32[512,2048]{1,0:T(8...) custom-call(f32[512,512]{1,0:T(8,128)S(1)} %pad_maximum_fusion.12.hidden, ...), custom_call_target="tpu_custom_call" | custom-call | flops 1 | bytes 1 | tf_op jit(solution)/shard_map/both/pallas_call | solution.py:406
  308.3 17.9 %weights.2 = (f32[512,2048]{1,0:T(8,128)}, f32[2048,512]{1,0:T(8,128)}) custom-call(f32[512,512]{1,0:T(8,128)S(1)} %copy-done.21, f32[512,512]{1,0:T(8,128)S(1)} %get-tuple-element.167.refs_1_, f32[512,512]{1,0:T(8,128)S(1)} %copy-done.37, f32[512,512]{1,0:T(8,128)S(1)} %get-tuple-element.169.refs_3_, f32[512,2048]{1,0:T(8,128)} %get-tuple-element.170.refs_4_, ...), custom_call_target="tpu_custom_call" | custom-call | flops 12884901888 | bytes 33554432 | tf_op jit(solution)/shard_map/weights/pallas_call | solution.py:447
  351.9 8.5 %multiply_reduce_fusion = (f32[512]{0:T(512)}, f32[512]{0:T(512)}, f32[512]{0:T(512)}, f32[512]{0:T(512)}, f32[512]{0:T(512)}, /*index=5*/f32[512]{0:T(512)}, f32[512]{0:T(512)}, f32[512]{0:T(512)}, f32[512,512]{1,0:T(8,128)S(1)}) fusion(f32[7,512]{1,0:T(8,128)S(1)} %get-tuple-element.463, f32[512,512]{1,0:T(8,128)} %copy-done.49, ...), kind=kLoop, calls=%fused_computation.204 | loop fusion | flops 8122368 | bytes 4237316 | tf_op jit(solution)/shard_map/reduce_sum | solution.py:843
  361.5 5.9 collective-permute-start.29
  371.5 10.5 %fusion.58 = (f32[512,512]{1,0:T(8,128)S(1)}, f32[512,512]{1,0:T(8,128)S(1)}) fusion(f32[512,1024]{1,0:T(8,128)} %copy-done.45, f32[512]{0:T(512)S(1)} %copy-done.99, f32[512,512]{1,0:T(8,128)} %copy-done.52, f32[7,512]{1,0:T(8,128)S(1)} %get-tuple-element.445, f32[512]{0:T(512)} %bitcast.311, f32[512]{0:T(512)} %bitcast.313, f32[512]{0:T(512)} %bitcast.287, ...), kind=kLoop, calls=%fused_computation.124 | loop fusion | flops 13369344 | bytes 5304320 | tf_op jit(solution)/shard_map/transpose(jvp())/mul | solution.py:768
  396.4 26.4 %attend_back.1 = (f32[512,512]{1,0:T(8,128)S(1)}, f32[2,1024,512]{2,1,0:T(8,128)S(1)}, f32[4,8,512]{2,1,0:T(8,128)S(1)}) custom-call(f32[8]{0:T(128)S(1)} %copy-done.33, f32[1024,512]{1,0:T(8,128)S(1)} %copy-done.9, f32[512,1536]{1,0:T(8,128)S(1)} %copy-done.7, f32[1024,1024]{1,0:T(8,128)} %copy-done.2, f32[1024,1024]{1,0:T(8,128)} %copy-done.2, ...), custom_call_target="tpu_custom_call" | custom-call | flops 1 | bytes 1 | tf_op jit(solution)/shard_map/attend_back/pallas_call | solution.py:644
  435.2 5.4 multiply_reduce_fusion.8
  477.2 23.5 %collective-permute-done.35 = f32[256,512]{1,0:T(8,128)S(1)} collective-permute-done((f32[256,512]{1,0:T(8,128)S(1)}, f32[256,512]{1,0:T(8,128)S(1)}, u32[]{:S(2)}, u32[]{:S(2)}) %collective-permute-start.35) | collective-permute-done | bytes 524320 | tf_op jit(solution)/shard_map/ppermute | solution.py:27
  510.8 14.4 %backward.2 = (f32[512,512]{1,0:T(8,128)S(1)}, f32[512,128]{1,0:T(8,128)S(1)}, f32[512,512]{1,0:T(8,128)S(1)}, f32[512,2048]{1,0:T(8,128)}, f32[512,512]{1,0:T(8...) custom-call(f32[512,512]{1,0:T(8,128)S(1)} %copy-done.13, f32[512,128]{1,0:T(8,128)S(1)} %copy-done.17, ...), custom_call_target="tpu_custom_call" | custom-call | flops 1 | bytes 1 | tf_op jit(solution)/shard_map/backward/pallas_call | solution.py:406
  535.1 7.7 %collective-permute-done.43 = f32[64,1536]{1,0:T(8,128)S(1)} collective-permute-done((f32[64,1536]{1,0:T(8,128)S(1)}, f32[64,1536]{1,0:T(8,128)S(1)}, u32[]{:S(2)}, u32[]{:S(2)}) %collective-permute-start.43) | collective-permute-done | bytes 393248 | tf_op jit(solution)/shard_map/ppermute | solution.py:27
  551.9 14.5 %backward.3 = (f32[512,512]{1,0:T(8,128)S(1)}, f32[512,128]{1,0:T(8,128)S(1)}, f32[512,512]{1,0:T(8,128)S(1)}, f32[512,2048]{1,0:T(8,128)}, f32[512,512]{1,0:T(8...) custom-call(f32[512,512]{1,0:T(8,128)S(1)} %copy-done.11, f32[512,128]{1,0:T(8,128)S(1)} %pad.91.extra, ...), custom_call_target="tpu_custom_call" | custom-call | flops 1 | bytes 1 | tf_op jit(solution)/shard_map/backward/pallas_call | solution.py:406
  566.4 17.5 %weights.3 = (f32[512,2048]{1,0:T(8,128)}, f32[2048,512]{1,0:T(8,128)}) custom-call(f32[512,512]{1,0:T(8,128)S(1)} %get-tuple-element.213.refs_0_, f32[512,512]{1,0:T(8,128)S(1)} %get-tuple-element.214.refs_1_, f32[512,512]{1,0:T(8,128)S(1)} %copy-done.35, f32[512,512]{1,0:T(8,128)S(1)} %get-tuple-element.226.refs_3_, ...), custom_call_target="tpu_custom_call" | custom-call | flops 12884901888 | bytes 33554432 | tf_op jit(solution)/shard_map/weights/pallas_call | solution.py:447
  601.9 9.5 %collective-permute-done.51 = f32[32,1536]{1,0:T(8,128)S(1)} collective-permute-done((f32[32,1536]{1,0:T(8,128)S(1)}, f32[32,1536]{1,0:T(8,128)S(1)}, u32[]{:S(2)}, u32[]{:S(2)}) %collective-permute-start.51) | collective-permute-done | bytes 196640 | tf_op jit(solution)/shard_map/ppermute | solution.py:27
  642.2 20.4 %collective-permute-done.59 = f32[128,1536]{1,0:T(8,128)S(1)} collective-permute-done((f32[128,1536]{1,0:T(8,128)}, f32[128,1536]{1,0:T(8,128)S(1)}, u32[]{:S(2)}, u32[]{:S(2)}) %collective-permute-start.59) | collective-permute-done | bytes 786464 | tf_op jit(solution)/shard_map/ppermute | solution.py:27
  685.1 8.4 %collective-permute-start.62 = (f32[36,512]{1,0:T(8,128)S(1)}, f32[36,512]{1,0:T(8,128)S(1)}, u32[]{:S(2)}, u32[]{:S(2)}) collective-permute-start(f32[36,512]{1,0:T(8,128)S(1)} %concatenate.252), channel_id=1, source_target_pairs={{0,1},{1,0},{2,3},{3,2},{4,5},{5,4},{6,7},{7,6},{8,9},{9,8},{10,11... | collective-permute-start | bytes 221192 | tf_op jit(solution)/shard_map/ppermute | solution.py:27
  696.7 5.1 collective-permute-done.63
  733.5 4.9 bitcast_dynamic-update-slice_fusion
  (804 shorter events, 356.2 us)
Async XLA Ops:
  7.2 503.5 %all-reduce.32.cloned.1.call-start = ((), (), s32[]{:S(2)}) async-start(), calls=%async_computation.1 | async-start | bytes 16777216 | tf_op jit(solution)/shard_map/psum | solution.py:815
  36.4 31.3 %collective-permute-start.2 = (f32[264,512]{1,0:T(8,128)}, f32[264,512]{1,0:T(8,128)}, u32[]{:S(2)}, u32[]{:S(2)}) collective-permute-start(f32[264,512]{1,0:T(8,128)} %get-tuple-element.125), channel_id=1, source_target_pairs={{0,1},{1,3},{2,5},{3,7},{4,0},{5,2},{6,4},{7,6},{8,9},{9,11},{10,1... | collective-permute-start | bytes 1622024 | tf_op jit(solution)/shard_map/ppermute | solution.py:140
  67.7 40.6 %collective-permute-start.6 = (f32[256,512]{1,0:T(8,128)}, f32[256,512]{1,0:T(8,128)}, u32[]{:S(2)}, u32[]{:S(2)}) collective-permute-start(f32[256,512]{1,0:T(8,128)} %get-tuple-element.364), channel_id=1, source_target_pairs={{0,2},{1,3},{2,0},{3,1},{4,6},{5,7},{6,4},{7,5},{8,10},{9,11},{10,... | collective-permute-start | bytes 1572872 | tf_op jit(solution)/shard_map/ppermute | solution.py:27
  70.0 37.2 %collective-permute-start.4 = (f32[2,256]{1,0:T(2,128)S(1)}, f32[2,256]{1,0:T(2,128)S(1)}, u32[]{:S(2)}, u32[]{:S(2)}) collective-permute-start(f32[2,256]{1,0:T(2,128)S(1)} %bitcast.353), channel_id=1, source_target_pairs={{0,0},{1,2},{2,4},{3,6},{4,1},{5,3},{6,5},{7,7},{8,8},{9,10},{10,1... | collective-permute-start | bytes 6152 | tf_op jit(solution)/shard_map/ppermute | solution.py:191
  70.7 36.5 %collective-permute-start.5 = (f32[2,256]{1,0:T(2,128)S(1)}, f32[2,256]{1,0:T(2,128)S(1)}, u32[]{:S(2)}, u32[]{:S(2)}) collective-permute-start(f32[2,256]{1,0:T(2,128)S(1)} %bitcast.354), channel_id=1, source_target_pairs={{0,2},{1,0},{2,6},{3,4},{4,3},{5,1},{6,7},{7,5},{8,10},{9,8},{10,1... | collective-permute-start | bytes 6152 | tf_op jit(solution)/shard_map/ppermute | solution.py:191
  103.6 26.2 %collective-permute-start.8 = (f32[256,512]{1,0:T(8,128)S(1)}, f32[256,512]{1,0:T(8,128)S(1)}, u32[]{:S(2)}, u32[]{:S(2)}) collective-permute-start(f32[256,512]{1,0:T(8,128)S(1)} %get-tuple-element.366), channel_id=1, source_target_pairs={{0,3},{1,2},{2,1},{3,0},{4,7},{5,6},{6,5},{7,4},{8,11},{9,10},{10,... | collective-permute-start | bytes 1572872 | tf_op jit(solution)/shard_map/ppermute | solution.py:27
  137.6 37.7 %collective-permute-start.9 = (f32[512,1024]{1,0:T(8,128)}, f32[512,1024]{1,0:T(8,128)}, u32[]{:S(2)}, u32[]{:S(2)}) collective-permute-start(f32[512,1024]{1,0:T(8,128)} %slice_bitcast_fusion), channel_id=1, source_target_pairs={{0,4},{4,0},{8,12},{12,8},{16,20},{20,16},{24,28},{28,24},{1,5},{5... | collective-permute-start | bytes 6291464 | tf_op jit(solution)/shard_map/ppermute | solution.py:27
  159.6 47.6 %collective-permute-start.20 = (f32[264,512]{1,0:T(8,128)}, f32[264,512]{1,0:T(8,128)}, u32[]{:S(2)}, u32[]{:S(2)}) collective-permute-start(f32[264,512]{1,0:T(8,128)} %select_maximum_fusion.1), channel_id=1, source_target_pairs={{0,1},{1,3},{2,5},{3,7},{4,0},{5,2},{6,4},{7,6},{8,9},{9,11},{10,1... | collective-permute-start | bytes 1622024 | tf_op jit(solution)/shard_map/ppermute | solution.py:140
  168.3 43.4 %collective-permute-start.21 = (f32[264,512]{1,0:T(8,128)}, f32[264,512]{1,0:T(8,128)}, u32[]{:S(2)}, u32[]{:S(2)}) collective-permute-start(f32[264,512]{1,0:T(8,128)} %select_maximum_fusion), channel_id=1, source_target_pairs={{0,3},{1,1},{2,7},{3,5},{4,2},{5,0},{6,6},{7,4},{8,11},{9,9},{10,1... | collective-permute-start | bytes 1622024 | tf_op jit(solution)/shard_map/ppermute | solution.py:140
  226.9 23.8 %collective-permute-start.15 = (f32[256,512]{1,0:T(8,128)S(1)}, f32[256,512]{1,0:T(8,128)S(1)}, u32[]{:S(2)}, u32[]{:S(2)}) collective-permute-start(f32[256,512]{1,0:T(8,128)S(1)} %get-tuple-element.361), channel_id=1, source_target_pairs={{0,2},{1,3},{2,0},{3,1},{4,6},{5,7},{6,4},{7,5},{8,10},{9,11},{10,... | collective-permute-start | bytes 1572872 | tf_op jit(solution)/shard_map/ppermute | solution.py:27
  251.7 30.7 %collective-permute-start.18 = (f32[256,512]{1,0:T(8,128)}, f32[256,512]{1,0:T(8,128)}, u32[]{:S(2)}, u32[]{:S(2)}) collective-permute-start(f32[256,512]{1,0:T(8,128)} %get-tuple-element.360), channel_id=1, source_target_pairs={{0,1},{1,0},{2,3},{3,2},{4,5},{5,4},{6,7},{7,6},{8,9},{9,8},{10,11... | collective-permute-start | bytes 1572872 | tf_op jit(solution)/shard_map/ppermute | solution.py:27
  251.7 30.7 %collective-permute-start.19 = (f32[256,512]{1,0:T(8,128)}, f32[256,512]{1,0:T(8,128)}, u32[]{:S(2)}, u32[]{:S(2)}) collective-permute-start(f32[256,512]{1,0:T(8,128)} %get-tuple-element.359), channel_id=1, source_target_pairs={{0,3},{1,2},{2,1},{3,0},{4,7},{5,6},{6,5},{7,4},{8,11},{9,10},{10,... | collective-permute-start | bytes 1572872 | tf_op jit(solution)/shard_map/ppermute | solution.py:27
  277.1 31.2 %collective-permute-start.22 = (f32[256,512]{1,0:T(8,128)}, f32[256,512]{1,0:T(8,128)}, u32[]{:S(2)}, u32[]{:S(2)}) collective-permute-start(f32[256,512]{1,0:T(8,128)} %get-tuple-element.356), channel_id=1, source_target_pairs={{0,2},{1,3},{2,0},{3,1},{4,6},{5,7},{6,4},{7,5},{8,10},{9,11},{10,... | collective-permute-start | bytes 1572872 | tf_op jit(solution)/shard_map/ppermute | solution.py:27
  306.6 24.3 %collective-permute-start.24 = (f32[256,512]{1,0:T(8,128)S(1)}, f32[256,512]{1,0:T(8,128)S(1)}, u32[]{:S(2)}, u32[]{:S(2)}) collective-permute-start(f32[256,512]{1,0:T(8,128)S(1)} %get-tuple-element.358), channel_id=1, source_target_pairs={{0,3},{1,2},{2,1},{3,0},{4,7},{5,6},{6,5},{7,4},{8,11},{9,10},{10,... | collective-permute-start | bytes 1572872 | tf_op jit(solution)/shard_map/ppermute | solution.py:27
  343.2 390.4 %all-reduce.30.cloned.1.call-start = ((), (), s32[]{:S(2)}) async-start(), calls=%async_computation | async-start | bytes 16777216 | tf_op jit(solution)/shard_map/psum | solution.py:910
  361.5 87.2 %collective-permute-start.29 = (f32[264,512]{1,0:T(8,128)}, f32[264,512]{1,0:T(8,128)}, u32[]{:S(2)}, u32[]{:S(2)}) collective-permute-start(f32[264,512]{1,0:T(8,128)} %pad_maximum_fusion.18), channel_id=1, source_target_pairs={{0,0},{2,1},{4,2},{6,3},{1,4},{3,5},{5,6},{7,7},{8,8},{10,9},{12,1... | collective-permute-start | bytes 1622024 | tf_op jit(solution)/shard_map/ppermute | solution.py:167
  368.2 82.3 %collective-permute-start.30 = (f32[264,512]{1,0:T(8,128)}, f32[264,512]{1,0:T(8,128)}, u32[]{:S(2)}, u32[]{:S(2)}) collective-permute-start(f32[264,512]{1,0:T(8,128)} %pad_maximum_fusion.19), channel_id=1, source_target_pairs={{2,0},{0,1},{6,2},{4,3},{3,4},{1,5},{7,6},{5,7},{10,8},{8,9},{14,1... | collective-permute-start | bytes 1622024 | tf_op jit(solution)/shard_map/ppermute | solution.py:167
  426.4 26.3 %collective-permute-start.34 = (f32[2,512,512]{2,1,0:T(8,128)}, f32[2,512,512]{2,1,0:T(8,128)}, u32[]{:S(2)}, u32[]{:S(2)}) collective-permute-start(f32[2,512,512]{2,1,0:T(8,128)} %slice.960), channel_id=1, source_target_pairs={{0,4},{4,0},{8,12},{12,8},{16,20},{20,16},{24,28},{28,24},{1,5},{5... | collective-permute-start | bytes 6291464 | tf_op jit(solution)/shard_map/ppermute | solution.py:27
  448.7 26.0 %collective-permute-start.37 = (f32[256,1536]{1,0:T(8,128)}, f32[256,1536]{1,0:T(8,128)}, u32[]{:S(2)}, u32[]{:S(2)}) collective-permute-start(f32[256,1536]{1,0:T(8,128)} %fusion.47), channel_id=1, source_target_pairs={{0,4},{4,0},{8,12},{12,8},{16,20},{20,16},{24,28},{28,24},{1,5},{5... | collective-permute-start | bytes 4718600 | tf_op jit(solution)/shard_map/ppermute | solution.py:27
  461.7 39.0 %collective-permute-start.36 = (f32[256,2048]{1,0:T(8,128)}, f32[256,2048]{1,0:T(8,128)}, u32[]{:S(2)}, u32[]{:S(2)}) collective-permute-start(f32[256,2048]{1,0:T(8,128)} %fusion.2), channel_id=1, source_target_pairs={{0,4},{4,0},{8,12},{12,8},{16,20},{20,16},{24,28},{28,24},{1,5},{5... | collective-permute-start | bytes 6291464 | tf_op jit(solution)/shard_map/ppermute | solution.py:27
  474.3 26.4 %collective-permute-start.35 = (f32[256,512]{1,0:T(8,128)S(1)}, f32[256,512]{1,0:T(8,128)S(1)}, u32[]{:S(2)}, u32[]{:S(2)}) collective-permute-start(f32[256,512]{1,0:T(8,128)S(1)} %get-tuple-element.345), channel_id=1, source_target_pairs={{0,2},{1,3},{2,0},{3,1},{4,6},{5,7},{6,4},{7,5},{8,10},{9,11},{10,... | collective-permute-start | bytes 1572872 | tf_op jit(solution)/shard_map/ppermute | solution.py:27
  503.9 23.4 %collective-permute-start.39 = (f32[128,1536]{1,0:T(8,128)}, f32[128,1536]{1,0:T(8,128)}, u32[]{:S(2)}, u32[]{:S(2)}) collective-permute-start(f32[128,1536]{1,0:T(8,128)} %constant_dynamic-slice_fusion.6), channel_id=1, source_target_pairs={{0,16},{4,20},{8,24},{12,28},{16,0},{20,4},{24,8},{28,12},{1,17},{... | collective-permute-start | bytes 2359304 | tf_op jit(solution)/shard_map/ppermute | solution.py:27
  506.4 25.1 %collective-permute-start.38 = (f32[128,2048]{1,0:T(8,128)}, f32[128,2048]{1,0:T(8,128)}, u32[]{:S(2)}, u32[]{:S(2)}) collective-permute-start(f32[128,2048]{1,0:T(8,128)} %constant_dynamic-slice_fusion.7), channel_id=1, source_target_pairs={{0,8},{4,12},{8,0},{12,4},{16,24},{20,28},{24,16},{28,20},{1,9},{5... | collective-permute-start | bytes 3145736 | tf_op jit(solution)/shard_map/ppermute | solution.py:27
  509.5 25.6 %collective-permute-start.40 = (f32[256,512]{1,0:T(8,128)}, f32[256,512]{1,0:T(8,128)}, u32[]{:S(2)}, u32[]{:S(2)}) collective-permute-start(f32[256,512]{1,0:T(8,128)} %get-tuple-element.344), channel_id=1, source_target_pairs={{0,1},{1,0},{2,3},{3,2},{4,5},{5,4},{6,7},{7,6},{8,9},{9,8},{10,11... | collective-permute-start | bytes 1572872 | tf_op jit(solution)/shard_map/ppermute | solution.py:27
  509.5 25.6 %collective-permute-start.41 = (f32[256,512]{1,0:T(8,128)}, f32[256,512]{1,0:T(8,128)}, u32[]{:S(2)}, u32[]{:S(2)}) collective-permute-start(f32[256,512]{1,0:T(8,128)} %get-tuple-element.343), channel_id=1, source_target_pairs={{0,3},{1,2},{2,1},{3,0},{4,7},{5,6},{6,5},{7,4},{8,11},{9,10},{10,... | collective-permute-start | bytes 1572872 | tf_op jit(solution)/shard_map/ppermute | solution.py:27
  546.9 37.0 %collective-permute-start.45 = (f32[32,1536]{1,0:T(8,128)S(1)}, f32[32,1536]{1,0:T(8,128)}, u32[]{:S(2)}, u32[]{:S(2)}) collective-permute-start(f32[32,1536]{1,0:T(8,128)S(1)} %constant_dynamic-slice_fusion.2), channel_id=1, source_target_pairs={{0,2},{1,3},{2,0},{3,1},{4,6},{5,7},{6,4},{7,5},{8,10},{9,11},{10,... | collective-permute-start | bytes 589832 | tf_op jit(solution)/shard_map/ppermute | solution.py:27
  547.7 37.3 %collective-permute-start.44 = (f32[32,2048]{1,0:T(8,128)}, f32[32,2048]{1,0:T(8,128)}, u32[]{:S(2)}, u32[]{:S(2)}) collective-permute-start(f32[32,2048]{1,0:T(8,128)} %constant_dynamic-slice_fusion.3), channel_id=1, source_target_pairs={{0,2},{1,3},{2,0},{3,1},{4,6},{5,7},{6,4},{7,5},{8,10},{9,11},{10,... | collective-permute-start | bytes 786440 | tf_op jit(solution)/shard_map/ppermute | solution.py:27
  624.4 48.1 %collective-permute-start.55 = (f32[264,512]{1,0:T(8,128)}, f32[264,512]{1,0:T(8,128)}, u32[]{:S(2)}, u32[]{:S(2)}) collective-permute-start(f32[264,512]{1,0:T(8,128)} %pad_maximum_fusion.25), channel_id=1, source_target_pairs={{3,0},{1,1},{7,2},{5,3},{2,4},{0,5},{6,6},{4,7},{11,8},{9,9},{15,1... | collective-permute-start | bytes 1622024 | tf_op jit(solution)/shard_map/ppermute | solution.py:167
  628.3 44.2 %collective-permute-start.54 = (f32[264,512]{1,0:T(8,128)S(1)}, f32[264,512]{1,0:T(8,128)S(1)}, u32[]{:S(2)}, u32[]{:S(2)}) collective-permute-start(f32[264,512]{1,0:T(8,128)S(1)} %pad_maximum_fusion.24), channel_id=1, source_target_pairs={{1,0},{3,1},{5,2},{7,3},{0,4},{2,5},{4,6},{6,7},{9,8},{11,9},{13,1... | collective-permute-start | bytes 1622024 | tf_op jit(solution)/shard_map/ppermute | solution.py:167
  632.8 29.9 %collective-permute-start.59 = (f32[128,1536]{1,0:T(8,128)}, f32[128,1536]{1,0:T(8,128)S(1)}, u32[]{:S(2)}, u32[]{:S(2)}) collective-permute-start(f32[128,1536]{1,0:T(8,128)} %constant_dynamic-update-slice_fusion.6), channel_id=1, source_target_pairs={{0,16},{4,20},{8,24},{12,28},{16,0},{20,4},{24,8},{28,12},{1,17},{... | collective-permute-start | bytes 2359304 | tf_op jit(solution)/shard_map/ppermute | solution.py:27
  636.2 35.2 %collective-permute-start.57 = (f32[128,2048]{1,0:T(8,128)}, f32[128,2048]{1,0:T(8,128)S(1)}, u32[]{:S(2)}, u32[]{:S(2)}) collective-permute-start(f32[128,2048]{1,0:T(8,128)} %constant_dynamic-update-slice_fusion.10), channel_id=1, source_target_pairs={{0,8},{4,12},{8,0},{12,4},{16,24},{20,28},{24,16},{28,20},{1,9},{5... | collective-permute-start | bytes 3145736 | tf_op jit(solution)/shard_map/ppermute | solution.py:27
  637.2 35.3 %collective-permute-start.53 = (f32[264,512]{1,0:T(8,128)S(1)}, f32[264,512]{1,0:T(8,128)S(1)}, u32[]{:S(2)}, u32[]{:S(2)}) collective-permute-start(f32[264,512]{1,0:T(8,128)S(1)} %pad_maximum_fusion.23), channel_id=1, source_target_pairs={{2,0},{0,1},{6,2},{4,3},{3,4},{1,5},{7,6},{5,7},{10,8},{8,9},{14,1... | collective-permute-start | bytes 1622024 | tf_op jit(solution)/shard_map/ppermute | solution.py:167
  (218 other events, 1703.1 us)
Sparse Core Ops, SparseCore 0:
  343.3 125.6 all-reduce.31
  584.0 145.3 all-reduce.29

commit v3 on v2

--- a/solution.py
+++ b/solution.py
@@ -121,7 +121,7 @@
     def group_of(self, values, group):
         return self.piece(values, group * 2 * self.micro, 2 * self.micro)
 
-    def home_to_expert(self, rows, extra):
+    def home_to_expert(self, rows, extra, ahead=()):
         wide = rows.shape[1]
         few = extra.shape[0]
         count = self.micro * self.capacity
@@ -140,7 +140,7 @@
                     got.append(lax.ppermute(message, ("dp", "ep"), self.route(group, u, False)))
                 else:
                     got.append(self.hop(message, group + u * (self.ep // 2)))
-            last = tuple(got)
+            last = tuple(got) + tuple(ahead)
             rows_got = [v[:count] for v in got]
             more_got = [v[count:, :count] for v in got]
             if self.paired:
@@ -724,7 +724,8 @@
         pick_columns(jnp.concatenate([home_logits[b], home_valid, spare], axis=0), home[b][1]) for b in (0, 1)
     ]
 
-    sources = layout.home_to_expert(pick(home[0][0], frames.reshape(-1, width)), extras[0])
+    work_ids = layout.ids_to_work(ids)
+    sources = layout.home_to_expert(pick(home[0][0], frames.reshape(-1, width)), extras[0], (work_ids,))
     kept_first = []
     back = []
     last = ()
@@ -738,7 +739,6 @@
         last = (new,)
         kept_first.append(((hidden, extra), (result, pre), fixed))
         back += layout.hops(new, group)
-    work_ids = layout.ids_to_work(after(ids, sources[-1][0]))
     work = [
         tables_of(layout.work_slots(work_ids[..., b], ranks(work_ids[..., b], experts)), slots) for b in (0, 1)
     ]
@@ -882,9 +882,7 @@
         arrived = tuple(grad)
         grad = after(grad, *last)
         if group == 0:
-            grad, expert_one = lax.optimization_barrier((dense.step(grad), expert_one))
-        if group == 1:
-            grad = dense.step(grad)
+            grad, expert_one = lax.optimization_barrier((grad, expert_one))
         (hidden, extra), saved, fixed = kept_first[group]
         new, grad_logits, normed, active, grad_result, grad_pre, sums = expert_call(
             backward_kernel,
@@ -898,9 +896,9 @@
             2,
         )
         if group == 0:
+            new = dense.step(new)
+        if group == 1:
             new = dense.step(new, over_dp - 2)
-        if group == 1:
-            new = dense.step(new, over_ep - 1)
         last = (new,)
         sources.append((new, grad_logits[:, : experts + (-experts % 8)].T))
         kept.append((normed, active, grad_result, grad_pre))
@@ -908,9 +906,10 @@
     sums, router_zero = add_up(small)
     gain_zero, shift_zero = sums[0], sums[1]
     expert_zero = lax.psum(expert_weight_grads(kept), "dp")
-    sources = dense.step(sources, over_ep + 1)
+    sources = dense.step(sources, 2 * over_ep + 1)
     frame_messages = layout.expert_to_home(sources)
-    frame_messages = dense.step(frame_messages, over_dp - 1)
+    wholes = [lax.pad(one[None], 0.0, ((1, 0, 0), (0, 0, 0), (0, 0, 0))) for one in expert_one]
+    frame_messages, wholes = dense.step((frame_messages, wholes), over_dp - 1)
     rows_back, logit_slots = layout.opened(frame_messages)
     logit_zero = pick_columns(logit_slots[:experts], home[0][0])
     router_zero = router_zero + product(logit_zero, home_rows).T
@@ -921,8 +920,7 @@
     packed_grad, project_grad = dense.parts[0][:, : 3 * width], dense.parts[0][:, 3 * width :]
     mixing_grad, point_grad = dense.parts[1][:, :width], dense.parts[1][:, width:]
     expert_grads = []
-    for zero, one in zip(expert_zero, expert_one):
-        whole = lax.optimization_barrier(lax.pad(after(one, late)[None], 0.0, ((1, 0, 0), (0, 0, 0), (0, 0, 0))))
+    for zero, whole in zip(expert_zero, wholes):
         expert_grads.append(lax.dynamic_update_slice(whole, zero[None], (0, 0, 0))[:, None])
 
     at = 8 + experts

time: 764 us -> 771 us (level)
  local copies, waits for them, and re-layouts: 149 us -> 158 us
    ppermute x2, starting transfers between devices: 20.7 us -> 5.62 us  [ids_to_work(): out.append(lax.ppermute(block, ('dp', 'ep'), pairs))]
    ppermute x49, starting transfers between devices: 61.3 us -> 72.8 us  [swap(): return lax.ppermute(values, axis, [(i, i ^ bit) for i in range(count)])]
    unnamed x377 -> x381, local copies, waits for them, and re-layouts: 25.2 us -> 24.8 us
  transfers between devices with their start and end apart: 69 -> 69, of which waited for: 26 -> 21; matrix products, arithmetic and copies ran while one was open for 30% -> 32% of each run, Pallas kernels for 22% -> 21%
where the time goes in v3:
time: 771 us; the launch traced here: 763 us
  Pallas kernels  163 us (21%)
  local copies, waits for them, and re-layouts  158 us (20%)
  waiting for transfers between devices  155 us (20%)
  starting transfers between devices  133 us (17%)
  other arithmetic  79.6 us (10%)
  matrix products  57.2 us (7%)
  between operations  17.7 us (2%)
    ppermute x49, waiting for transfers between devices, swap(): return lax.ppermute(values, axis, [(i, i ^ bit) for i in range(count)])  146 us
    pallas_call x6, Pallas kernels, expert_call(): pl.pallas_call(functools.partial(kernel, experts), grid=(rows // block,),...  87.7 us
    ppermute x49, starting transfers between devices, swap(): return lax.ppermute(values, axis, [(i, i ^ bit) for i in range(count)])  72.8 us
    dot_general x20, matrix products, product(): return jnp.matmul(left, right, precision=HIGH)  38.7 us
    ppermute x8, starting transfers between devices, home_to_expert(): got.append(lax.ppermute(message, ('dp', 'ep'), self.route(group, u, False)))  36.3 us
    pallas_call x2, Pallas kernels, expert_weight_grads(): pl.pallas_call(functools.partial(weight_kernel, count), grid=(inner // wi...  35.4 us
    pallas_call x1, Pallas kernels, attend_back(): pl.pallas_call(functools.partial(attend_back_kernel, chunk, (width // slo...  26.4 us
    unnamed x381, local copies, waits for them, and re-layouts  24.8 us
  transfers between devices with their start and end apart: 69, of which 21 were waited for; matrix products, arithmetic and copies ran while one was open for 32% of the time, Pallas kernels for 21%

profile of v3, /device:TPU:0, one launch (start us, length us, event | category | flops | bytes accessed | tf_op | source)
XLA Modules:
  0.0 763.2 jit_solution(6413286936648165534)
XLA Ops:
  15.8 5.8 collective-permute-start.2
  40.3 7.1 collective-permute-start.5
  47.4 5.4 collective-permute-start.6
  58.5 9.4 %forward.2 = (f32[512,512]{1,0:T(8,128)S(1)}, f32[512,512]{1,0:T(8,128)S(1)}, f32[512,2048]{1,0:T(8,128)}) custom-call(f32[512,512]{1,0:T(8,128)S(1)} %pad_maximum_fusion.8.hidden, f32[512,128]{1,0:T(8,128)S(1)} %pad.87.extra, f32[1,128]{1,0:T(1,128)S(1)} %compare_convert_fusion.2.own, f32[2,512]{1,0:T(2,128)S(1)} %get-tuple-element.481.norm, ...), custom_call_target="tpu_custom_call" | custom-call | flops 1 | bytes 1 | tf_op jit(solution)/shard_map/forward/pallas_call | solution.py:406
  72.9 10.3 %forward.3 = (f32[512,512]{1,0:T(8,128)S(1)}, f32[512,512]{1,0:T(8,128)S(1)}, f32[512,2048]{1,0:T(8,128)}) custom-call(f32[512,512]{1,0:T(8,128)S(1)} %pad_maximum_fusion.9.hidden, f32[512,128]{1,0:T(8,128)S(1)} %pad.91.extra, f32[1,128]{1,0:T(1,128)S(1)} %compare_convert_fusion.2.own, f32[2,512]{1,0:T(2,128)S(1)} %get-tuple-element.481.norm, ...), custom_call_target="tpu_custom_call" | custom-call | flops 1 | bytes 1 | tf_op jit(solution)/shard_map/forward/pallas_call | solution.py:406
  83.3 18.2 %collective-permute-start.7 = (f32[256,512]{1,0:T(8,128)S(1)}, f32[256,512]{1,0:T(8,128)S(1)}, u32[]{:S(2)}, u32[]{:S(2)}) collective-permute-start(f32[256,512]{1,0:T(8,128)S(1)} %get-tuple-element.347), channel_id=1, source_target_pairs={{0,1},{1,0},{2,3},{3,2},{4,5},{5,4},{6,7},{7,6},{8,9},{9,8},{10,11... | collective-permute-start | bytes 1572872 | tf_op jit(solution)/shard_map/ppermute | solution.py:27
  105.2 18.6 %collective-permute-done.7 = f32[256,512]{1,0:T(8,128)S(1)} collective-permute-done((f32[256,512]{1,0:T(8,128)S(1)}, f32[256,512]{1,0:T(8,128)S(1)}, u32[]{:S(2)}, u32[]{:S(2)}) %collective-permute-start.7) | collective-permute-done | bytes 524320 | tf_op jit(solution)/shard_map/ppermute | solution.py:27
  132.7 5.8 collective-permute-start.16
  145.0 8.6 %collective-permute-done.17 = f32[264,512]{1,0:T(8,128)} collective-permute-done((f32[264,512]{1,0:T(8,128)}, f32[264,512]{1,0:T(8,128)}, u32[]{:S(2)}, u32[]{:S(2)}) %collective-permute-start.17) | collective-permute-done | bytes 540704 | tf_op jit(solution)/shard_map/ppermute | solution.py:140
  153.7 5.6 collective-permute-start.20
  159.2 6.4 collective-permute-start.21
  172.3 13.4 %attend.1 = (f32[512,512]{1,0:T(8,128)S(1)}, f32[4,8,512]{2,1,0:T(8,128)S(1)}) custom-call(f32[8]{0:T(128)S(1)} %copy-done.33, f32[1024,512]{1,0:T(8,128)S(1)} %convert_select_fusion.dist, f32[512,1536]{1,0:T(8,128)S(1)} %copy-done.6, f32[1024,1024]{1,0:T(8,128)S(1)} %pad_maximum_fusion.k_ref.v_ref, f32[1024,1024]{1,0:T(8,128)S(1)} %pad_maximum_fusion.k_ref.v_ref), custom_call_target="tpu_custom_call" | custom-call | flops 1 | bytes 1 | tf_op jit(solution)/shard_map/attend/pallas_call | solution.py:618
  226.3 18.2 %collective-permute-done.15 = f32[256,512]{1,0:T(8,128)S(1)} collective-permute-done((f32[256,512]{1,0:T(8,128)S(1)}, f32[256,512]{1,0:T(8,128)S(1)}, u32[]{:S(2)}, u32[]{:S(2)}) %collective-permute-start.15) | collective-permute-done | bytes 524320 | tf_op jit(solution)/shard_map/ppermute | solution.py:27
  247.2 19.6 %both.2 = (f32[512,512]{1,0:T(8,128)S(1)}, f32[512,512]{1,0:T(8,128)S(1)}, f32[512,128]{1,0:T(8,128)S(1)}, f32[512,512]{1,0:T(8,128)S(1)}, f32[512,2048]{1,0:T(8...) custom-call(f32[512,512]{1,0:T(8,128)S(1)} %pad_maximum_fusion.10.hidden, ...), custom_call_target="tpu_custom_call" | custom-call | flops 1 | bytes 1 | tf_op jit(solution)/shard_map/both/pallas_call | solution.py:406
  278.8 19.6 %both.3 = (f32[512,512]{1,0:T(8,128)S(1)}, f32[512,512]{1,0:T(8,128)S(1)}, f32[512,128]{1,0:T(8,128)S(1)}, f32[512,512]{1,0:T(8,128)S(1)}, f32[512,2048]{1,0:T(8...) custom-call(f32[512,512]{1,0:T(8,128)S(1)} %pad_maximum_fusion.12.hidden, ...), custom_call_target="tpu_custom_call" | custom-call | flops 1 | bytes 1 | tf_op jit(solution)/shard_map/both/pallas_call | solution.py:406
  302.1 17.9 %weights.2 = (f32[512,2048]{1,0:T(8,128)}, f32[2048,512]{1,0:T(8,128)}) custom-call(f32[512,512]{1,0:T(8,128)S(1)} %copy-done.21, f32[512,512]{1,0:T(8,128)S(1)} %get-tuple-element.155.refs_1_, f32[512,512]{1,0:T(8,128)S(1)} %copy-done.35, f32[512,512]{1,0:T(8,128)S(1)} %get-tuple-element.157.refs_3_, f32[512,2048]{1,0:T(8,128)} %get-tuple-element.158.refs_4_, ...), custom_call_target="tpu_custom_call" | custom-call | flops 12884901888 | bytes 33554432 | tf_op jit(solution)/shard_map/weights/pallas_call | solution.py:447
  345.5 8.8 %multiply_reduce_fusion = (f32[512]{0:T(512)}, f32[512]{0:T(512)}, f32[512]{0:T(512)}, f32[512]{0:T(512)}, f32[512]{0:T(512)}, /*index=5*/f32[512]{0:T(512)}, f32[512]{0:T(512)}, f32[512]{0:T(512)}, f32[512,512]{1,0:T(8,128)S(1)}) fusion(f32[7,512]{1,0:T(8,128)S(1)} %get-tuple-element.445, f32[512,512]{1,0:T(8,128)} %copy-done.49, ...), kind=kLoop, calls=%fused_computation.204 | loop fusion | flops 8122368 | bytes 4237316 | tf_op jit(solution)/shard_map/reduce_sum | solution.py:843
  355.3 6.0 collective-permute-start.29
  366.4 10.6 %fusion.58 = (f32[512,512]{1,0:T(8,128)S(1)}, f32[512,512]{1,0:T(8,128)S(1)}) fusion(f32[512,1024]{1,0:T(8,128)} %copy-done.45, f32[512]{0:T(512)S(1)} %copy-done.100, f32[512,512]{1,0:T(8,128)} %copy-done.54, f32[7,512]{1,0:T(8,128)S(1)} %get-tuple-element.427, f32[512]{0:T(512)} %bitcast.305, f32[512]{0:T(512)} %bitcast.307, f32[512]{0:T(512)} %bitcast.281, ...), kind=kLoop, calls=%fused_computation.124 | loop fusion | flops 13369344 | bytes 5304320 | tf_op jit(solution)/shard_map/transpose(jvp())/mul | solution.py:768
  390.9 26.4 %attend_back.1 = (f32[512,512]{1,0:T(8,128)S(1)}, f32[2,1024,512]{2,1,0:T(8,128)S(1)}, f32[4,8,512]{2,1,0:T(8,128)S(1)}) custom-call(f32[8]{0:T(128)S(1)} %copy-done.33, f32[1024,512]{1,0:T(8,128)S(1)} %copy-done.9, f32[512,1536]{1,0:T(8,128)S(1)} %copy-done.7, f32[1024,1024]{1,0:T(8,128)} %copy-done.2, f32[1024,1024]{1,0:T(8,128)} %copy-done.2, ...), custom_call_target="tpu_custom_call" | custom-call | flops 1 | bytes 1 | tf_op jit(solution)/shard_map/attend_back/pallas_call | solution.py:644
  428.9 5.7 multiply_reduce_fusion.8
  475.5 21.9 %collective-permute-done.35 = f32[256,512]{1,0:T(8,128)S(1)} collective-permute-done((f32[256,512]{1,0:T(8,128)S(1)}, f32[256,512]{1,0:T(8,128)S(1)}, u32[]{:S(2)}, u32[]{:S(2)}) %collective-permute-start.35) | collective-permute-done | bytes 524320 | tf_op jit(solution)/shard_map/ppermute | solution.py:27
  502.2 14.4 %backward.2 = (f32[512,512]{1,0:T(8,128)S(1)}, f32[512,128]{1,0:T(8,128)S(1)}, f32[512,512]{1,0:T(8,128)S(1)}, f32[512,2048]{1,0:T(8,128)}, f32[512,512]{1,0:T(8...) custom-call(f32[512,512]{1,0:T(8,128)S(1)} %copy-done.11, f32[512,128]{1,0:T(8,128)S(1)} %copy-done.17, ...), custom_call_target="tpu_custom_call" | custom-call | flops 1 | bytes 1 | tf_op jit(solution)/shard_map/backward/pallas_call | solution.py:406
  518.7 7.0 pad.109
  538.4 14.4 %backward.3 = (f32[512,512]{1,0:T(8,128)S(1)}, f32[512,128]{1,0:T(8,128)S(1)}, f32[512,512]{1,0:T(8,128)S(1)}, f32[512,2048]{1,0:T(8,128)}, f32[512,512]{1,0:T(8...) custom-call(f32[512,512]{1,0:T(8,128)S(1)} %copy-done.13, f32[512,128]{1,0:T(8,128)S(1)} %pad.91.extra, ...), custom_call_target="tpu_custom_call" | custom-call | flops 1 | bytes 1 | tf_op jit(solution)/shard_map/backward/pallas_call | solution.py:406
  552.8 17.5 %weights.3 = (f32[512,2048]{1,0:T(8,128)}, f32[2048,512]{1,0:T(8,128)}) custom-call(f32[512,512]{1,0:T(8,128)S(1)} %get-tuple-element.197.refs_0_, f32[512,512]{1,0:T(8,128)S(1)} %get-tuple-element.198.refs_1_, f32[512,512]{1,0:T(8,128)S(1)} %copy-done.37, f32[512,512]{1,0:T(8,128)S(1)} %get-tuple-element.209.refs_3_, ...), custom_call_target="tpu_custom_call" | custom-call | flops 12884901888 | bytes 33554432 | tf_op jit(solution)/shard_map/weights/pallas_call | solution.py:447
  575.1 18.2 %collective-permute-done.47 = f32[64,1536]{1,0:T(8,128)S(1)} collective-permute-done((f32[64,1536]{1,0:T(8,128)S(1)}, f32[64,1536]{1,0:T(8,128)S(1)}, u32[]{:S(2)}, u32[]{:S(2)}) %collective-permute-start.47) | collective-permute-done | bytes 393248 | tf_op jit(solution)/shard_map/ppermute | solution.py:27
  608.3 7.1 collective-permute-done.43
  628.4 9.9 %collective-permute-done.46 = f32[32,2048]{1,0:T(8,128)S(1)} collective-permute-done((f32[32,2048]{1,0:T(8,128)S(1)}, f32[32,2048]{1,0:T(8,128)S(1)}, u32[]{:S(2)}, u32[]{:S(2)}) %collective-permute-start.46) | collective-permute-done | bytes 262176 | tf_op jit(solution)/shard_map/ppermute | solution.py:27
  667.7 14.3 %collective-permute-done.59 = f32[128,1536]{1,0:T(8,128)S(1)} collective-permute-done((f32[128,1536]{1,0:T(8,128)}, f32[128,1536]{1,0:T(8,128)S(1)}, u32[]{:S(2)}, u32[]{:S(2)}) %collective-permute-start.59) | collective-permute-done | bytes 786464 | tf_op jit(solution)/shard_map/ppermute | solution.py:27
  687.4 5.4 collective-permute-done.57
  712.2 6.6 collective-permute-start.62
  (809 shorter events, 361.5 us)
Async XLA Ops:
  7.2 493.8 %all-reduce.32.cloned.1.call-start = ((), (), s32[]{:S(2)}) async-start(), calls=%async_computation.1 | async-start | bytes 16777216 | tf_op jit(solution)/shard_map/psum | solution.py:815
  15.8 24.5 %collective-permute-start.2 = (f32[264,512]{1,0:T(8,128)}, f32[264,512]{1,0:T(8,128)}, u32[]{:S(2)}, u32[]{:S(2)}) collective-permute-start(f32[264,512]{1,0:T(8,128)} %pad_maximum_fusion.16), channel_id=1, source_target_pairs={{0,0},{1,2},{2,4},{3,6},{4,1},{5,3},{6,5},{7,7},{8,8},{9,10},{10,1... | collective-permute-start | bytes 1622024 | tf_op jit(solution)/shard_map/ppermute | solution.py:140
  40.3 28.6 %collective-permute-start.5 = (f32[264,512]{1,0:T(8,128)}, f32[264,512]{1,0:T(8,128)}, u32[]{:S(2)}, u32[]{:S(2)}) collective-permute-start(f32[264,512]{1,0:T(8,128)} %get-tuple-element.117), channel_id=1, source_target_pairs={{0,1},{1,3},{2,5},{3,7},{4,0},{5,2},{6,4},{7,6},{8,9},{9,11},{10,1... | collective-permute-start | bytes 1622024 | tf_op jit(solution)/shard_map/ppermute | solution.py:140
  68.9 36.3 %collective-permute-start.4 = (f32[256,512]{1,0:T(8,128)S(1)}, f32[256,512]{1,0:T(8,128)}, u32[]{:S(2)}, u32[]{:S(2)}) collective-permute-start(f32[256,512]{1,0:T(8,128)S(1)} %get-tuple-element.346), channel_id=1, source_target_pairs={{0,2},{1,3},{2,0},{3,1},{4,6},{5,7},{6,4},{7,5},{8,10},{9,11},{10,... | collective-permute-start | bytes 1572872 | tf_op jit(solution)/shard_map/ppermute | solution.py:27
  83.3 40.6 %collective-permute-start.7 = (f32[256,512]{1,0:T(8,128)S(1)}, f32[256,512]{1,0:T(8,128)S(1)}, u32[]{:S(2)}, u32[]{:S(2)}) collective-permute-start(f32[256,512]{1,0:T(8,128)S(1)} %get-tuple-element.347), channel_id=1, source_target_pairs={{0,1},{1,0},{2,3},{3,2},{4,5},{5,4},{6,7},{7,6},{8,9},{9,8},{10,11... | collective-permute-start | bytes 1572872 | tf_op jit(solution)/shard_map/ppermute | solution.py:27
  101.5 22.4 %collective-permute-start.8 = (f32[256,512]{1,0:T(8,128)S(1)}, f32[256,512]{1,0:T(8,128)S(1)}, u32[]{:S(2)}, u32[]{:S(2)}) collective-permute-start(f32[256,512]{1,0:T(8,128)S(1)} %get-tuple-element.348), channel_id=1, source_target_pairs={{0,3},{1,2},{2,1},{3,0},{4,7},{5,6},{6,5},{7,4},{8,11},{9,10},{10,... | collective-permute-start | bytes 1572872 | tf_op jit(solution)/shard_map/ppermute | solution.py:27
  131.6 37.5 %collective-permute-start.9 = (f32[512,1024]{1,0:T(8,128)}, f32[512,1024]{1,0:T(8,128)}, u32[]{:S(2)}, u32[]{:S(2)}) collective-permute-start(f32[512,1024]{1,0:T(8,128)} %slice_bitcast_fusion), channel_id=1, source_target_pairs={{0,4},{4,0},{8,12},{12,8},{16,20},{20,16},{24,28},{28,24},{1,5},{5... | collective-permute-start | bytes 6291464 | tf_op jit(solution)/shard_map/ppermute | solution.py:27
  153.7 47.2 %collective-permute-start.20 = (f32[264,512]{1,0:T(8,128)}, f32[264,512]{1,0:T(8,128)}, u32[]{:S(2)}, u32[]{:S(2)}) collective-permute-start(f32[264,512]{1,0:T(8,128)} %select_maximum_fusion.1), channel_id=1, source_target_pairs={{0,1},{1,3},{2,5},{3,7},{4,0},{5,2},{6,4},{7,6},{8,9},{9,11},{10,1... | collective-permute-start | bytes 1622024 | tf_op jit(solution)/shard_map/ppermute | solution.py:140
  159.2 46.0 %collective-permute-start.21 = (f32[264,512]{1,0:T(8,128)}, f32[264,512]{1,0:T(8,128)}, u32[]{:S(2)}, u32[]{:S(2)}) collective-permute-start(f32[264,512]{1,0:T(8,128)} %select_maximum_fusion), channel_id=1, source_target_pairs={{0,3},{1,1},{2,7},{3,5},{4,2},{5,0},{6,6},{7,4},{8,11},{9,9},{10,1... | collective-permute-start | bytes 1622024 | tf_op jit(solution)/shard_map/ppermute | solution.py:140
  220.7 23.8 %collective-permute-start.15 = (f32[256,512]{1,0:T(8,128)S(1)}, f32[256,512]{1,0:T(8,128)S(1)}, u32[]{:S(2)}, u32[]{:S(2)}) collective-permute-start(f32[256,512]{1,0:T(8,128)S(1)} %get-tuple-element.343), channel_id=1, source_target_pairs={{0,2},{1,3},{2,0},{3,1},{4,6},{5,7},{6,4},{7,5},{8,10},{9,11},{10,... | collective-permute-start | bytes 1572872 | tf_op jit(solution)/shard_map/ppermute | solution.py:27
  245.5 30.7 %collective-permute-start.18 = (f32[256,512]{1,0:T(8,128)}, f32[256,512]{1,0:T(8,128)}, u32[]{:S(2)}, u32[]{:S(2)}) collective-permute-start(f32[256,512]{1,0:T(8,128)} %get-tuple-element.342), channel_id=1, source_target_pairs={{0,1},{1,0},{2,3},{3,2},{4,5},{5,4},{6,7},{7,6},{8,9},{9,8},{10,11... | collective-permute-start | bytes 1572872 | tf_op jit(solution)/shard_map/ppermute | solution.py:27
  245.5 30.7 %collective-permute-start.19 = (f32[256,512]{1,0:T(8,128)}, f32[256,512]{1,0:T(8,128)}, u32[]{:S(2)}, u32[]{:S(2)}) collective-permute-start(f32[256,512]{1,0:T(8,128)} %get-tuple-element.341), channel_id=1, source_target_pairs={{0,3},{1,2},{2,1},{3,0},{4,7},{5,6},{6,5},{7,4},{8,11},{9,10},{10,... | collective-permute-start | bytes 1572872 | tf_op jit(solution)/shard_map/ppermute | solution.py:27
  270.8 31.2 %collective-permute-start.22 = (f32[256,512]{1,0:T(8,128)}, f32[256,512]{1,0:T(8,128)}, u32[]{:S(2)}, u32[]{:S(2)}) collective-permute-start(f32[256,512]{1,0:T(8,128)} %get-tuple-element.338), channel_id=1, source_target_pairs={{0,2},{1,3},{2,0},{3,1},{4,6},{5,7},{6,4},{7,5},{8,10},{9,11},{10,... | collective-permute-start | bytes 1572872 | tf_op jit(solution)/shard_map/ppermute | solution.py:27
  300.4 24.2 %collective-permute-start.24 = (f32[256,512]{1,0:T(8,128)S(1)}, f32[256,512]{1,0:T(8,128)S(1)}, u32[]{:S(2)}, u32[]{:S(2)}) collective-permute-start(f32[256,512]{1,0:T(8,128)S(1)} %get-tuple-element.340), channel_id=1, source_target_pairs={{0,3},{1,2},{2,1},{3,0},{4,7},{5,6},{6,5},{7,4},{8,11},{9,10},{10,... | collective-permute-start | bytes 1572872 | tf_op jit(solution)/shard_map/ppermute | solution.py:27
  336.8 397.3 %all-reduce.30.cloned.1.call-start = ((), (), s32[]{:S(2)}) async-start(), calls=%async_computation | async-start | bytes 16777216 | tf_op jit(solution)/shard_map/psum | solution.py:908
  355.3 87.6 %collective-permute-start.29 = (f32[264,512]{1,0:T(8,128)}, f32[264,512]{1,0:T(8,128)}, u32[]{:S(2)}, u32[]{:S(2)}) collective-permute-start(f32[264,512]{1,0:T(8,128)} %pad_maximum_fusion.18), channel_id=1, source_target_pairs={{0,0},{2,1},{4,2},{6,3},{1,4},{3,5},{5,6},{7,7},{8,8},{10,9},{12,1... | collective-permute-start | bytes 1622024 | tf_op jit(solution)/shard_map/ppermute | solution.py:167
  362.1 82.5 %collective-permute-start.30 = (f32[264,512]{1,0:T(8,128)}, f32[264,512]{1,0:T(8,128)}, u32[]{:S(2)}, u32[]{:S(2)}) collective-permute-start(f32[264,512]{1,0:T(8,128)} %pad_maximum_fusion.19), channel_id=1, source_target_pairs={{2,0},{0,1},{6,2},{4,3},{3,4},{1,5},{7,6},{5,7},{10,8},{8,9},{14,1... | collective-permute-start | bytes 1622024 | tf_op jit(solution)/shard_map/ppermute | solution.py:167
  420.9 26.5 %collective-permute-start.34 = (f32[2,512,512]{2,1,0:T(8,128)}, f32[2,512,512]{2,1,0:T(8,128)}, u32[]{:S(2)}, u32[]{:S(2)}) collective-permute-start(f32[2,512,512]{2,1,0:T(8,128)} %slice.958), channel_id=1, source_target_pairs={{0,4},{4,0},{8,12},{12,8},{16,20},{20,16},{24,28},{28,24},{1,5},{5... | collective-permute-start | bytes 6291464 | tf_op jit(solution)/shard_map/ppermute | solution.py:27
  421.8 23.6 %collective-permute-start.31 = (f32[264,512]{1,0:T(8,128)}, f32[264,512]{1,0:T(8,128)}, u32[]{:S(2)}, u32[]{:S(2)}) collective-permute-start(f32[264,512]{1,0:T(8,128)} %pad_maximum_fusion.20), channel_id=1, source_target_pairs={{1,0},{3,1},{5,2},{7,3},{0,4},{2,5},{4,6},{6,7},{9,8},{11,9},{13,1... | collective-permute-start | bytes 1622024 | tf_op jit(solution)/shard_map/ppermute | solution.py:167
  442.9 28.9 %collective-permute-start.37 = (f32[256,1536]{1,0:T(8,128)}, f32[256,1536]{1,0:T(8,128)}, u32[]{:S(2)}, u32[]{:S(2)}) collective-permute-start(f32[256,1536]{1,0:T(8,128)} %fusion.47), channel_id=1, source_target_pairs={{0,4},{4,0},{8,12},{12,8},{16,20},{20,16},{24,28},{28,24},{1,5},{5... | collective-permute-start | bytes 4718600 | tf_op jit(solution)/shard_map/ppermute | solution.py:27
  464.0 66.0 %collective-permute-start.36 = (f32[256,2048]{1,0:T(8,128)}, f32[256,2048]{1,0:T(8,128)}, u32[]{:S(2)}, u32[]{:S(2)}) collective-permute-start(f32[256,2048]{1,0:T(8,128)} %fusion.2), channel_id=1, source_target_pairs={{0,4},{4,0},{8,12},{12,8},{16,20},{20,16},{24,28},{28,24},{1,5},{5... | collective-permute-start | bytes 6291464 | tf_op jit(solution)/shard_map/ppermute | solution.py:27
  471.6 25.8 %collective-permute-start.35 = (f32[256,512]{1,0:T(8,128)S(1)}, f32[256,512]{1,0:T(8,128)S(1)}, u32[]{:S(2)}, u32[]{:S(2)}) collective-permute-start(f32[256,512]{1,0:T(8,128)S(1)} %get-tuple-element.327), channel_id=1, source_target_pairs={{0,2},{1,3},{2,0},{3,1},{4,6},{5,7},{6,4},{7,5},{8,10},{9,11},{10,... | collective-permute-start | bytes 1572872 | tf_op jit(solution)/shard_map/ppermute | solution.py:27
  499.3 32.8 %collective-permute-start.38 = (f32[256,512]{1,0:T(8,128)}, f32[256,512]{1,0:T(8,128)}, u32[]{:S(2)}, u32[]{:S(2)}) collective-permute-start(f32[256,512]{1,0:T(8,128)} %get-tuple-element.326), channel_id=1, source_target_pairs={{0,1},{1,0},{2,3},{3,2},{4,5},{5,4},{6,7},{7,6},{8,9},{9,8},{10,11... | collective-permute-start | bytes 1572872 | tf_op jit(solution)/shard_map/ppermute | solution.py:27
  499.3 32.8 %collective-permute-start.39 = (f32[256,512]{1,0:T(8,128)}, f32[256,512]{1,0:T(8,128)}, u32[]{:S(2)}, u32[]{:S(2)}) collective-permute-start(f32[256,512]{1,0:T(8,128)} %get-tuple-element.325), channel_id=1, source_target_pairs={{0,3},{1,2},{2,1},{3,0},{4,7},{5,6},{6,5},{7,4},{8,11},{9,10},{10,... | collective-permute-start | bytes 1572872 | tf_op jit(solution)/shard_map/ppermute | solution.py:27
  533.2 37.2 %collective-permute-start.41 = (f32[128,1536]{1,0:T(8,128)}, f32[128,1536]{1,0:T(8,128)}, u32[]{:S(2)}, u32[]{:S(2)}) collective-permute-start(f32[128,1536]{1,0:T(8,128)} %constant_dynamic-slice_fusion.6), channel_id=1, source_target_pairs={{0,16},{4,20},{8,24},{12,28},{16,0},{20,4},{24,8},{28,12},{1,17},{... | collective-permute-start | bytes 2359304 | tf_op jit(solution)/shard_map/ppermute | solution.py:27
  535.6 36.3 %collective-permute-start.40 = (f32[128,2048]{1,0:T(8,128)}, f32[128,2048]{1,0:T(8,128)}, u32[]{:S(2)}, u32[]{:S(2)}) collective-permute-start(f32[128,2048]{1,0:T(8,128)} %constant_dynamic-slice_fusion.7), channel_id=1, source_target_pairs={{0,8},{4,12},{8,0},{12,4},{16,24},{20,28},{24,16},{28,20},{1,9},{5... | collective-permute-start | bytes 3145736 | tf_op jit(solution)/shard_map/ppermute | solution.py:27
  574.4 25.3 %collective-permute-start.42 = (f32[64,2048]{1,0:T(8,128)S(1)}, f32[64,2048]{1,0:T(8,128)S(1)}, u32[]{:S(2)}, u32[]{:S(2)}) collective-permute-start(f32[64,2048]{1,0:T(8,128)S(1)} %constant_dynamic-slice_fusion.5), channel_id=1, source_target_pairs={{0,16},{4,20},{8,24},{12,28},{16,0},{20,4},{24,8},{28,12},{1,17},{... | collective-permute-start | bytes 1572872 | tf_op jit(solution)/shard_map/ppermute | solution.py:27
  647.5 46.4 %collective-permute-start.55 = (f32[264,512]{1,0:T(8,128)}, f32[264,512]{1,0:T(8,128)}, u32[]{:S(2)}, u32[]{:S(2)}) collective-permute-start(f32[264,512]{1,0:T(8,128)} %pad_maximum_fusion.25), channel_id=1, source_target_pairs={{3,0},{1,1},{7,2},{5,3},{2,4},{0,5},{6,6},{4,7},{11,8},{9,9},{15,1... | collective-permute-start | bytes 1622024 | tf_op jit(solution)/shard_map/ppermute | solution.py:167
  651.4 42.5 %collective-permute-start.54 = (f32[264,512]{1,0:T(8,128)S(1)}, f32[264,512]{1,0:T(8,128)S(1)}, u32[]{:S(2)}, u32[]{:S(2)}) collective-permute-start(f32[264,512]{1,0:T(8,128)S(1)} %pad_maximum_fusion.24), channel_id=1, source_target_pairs={{1,0},{3,1},{5,2},{7,3},{0,4},{2,5},{4,6},{6,7},{9,8},{11,9},{13,1... | collective-permute-start | bytes 1622024 | tf_op jit(solution)/shard_map/ppermute | solution.py:167
  656.9 25.0 %collective-permute-start.59 = (f32[128,1536]{1,0:T(8,128)}, f32[128,1536]{1,0:T(8,128)S(1)}, u32[]{:S(2)}, u32[]{:S(2)}) collective-permute-start(f32[128,1536]{1,0:T(8,128)} %constant_dynamic-update-slice_fusion.6), channel_id=1, source_target_pairs={{0,16},{4,20},{8,24},{12,28},{16,0},{20,4},{24,8},{28,12},{1,17},{... | collective-permute-start | bytes 2359304 | tf_op jit(solution)/shard_map/ppermute | solution.py:27
  660.5 32.3 %collective-permute-start.57 = (f32[128,2048]{1,0:T(8,128)}, f32[128,2048]{1,0:T(8,128)S(1)}, u32[]{:S(2)}, u32[]{:S(2)}) collective-permute-start(f32[128,2048]{1,0:T(8,128)} %constant_dynamic-update-slice_fusion.10), channel_id=1, source_target_pairs={{0,8},{4,12},{8,0},{12,4},{16,24},{20,28},{24,16},{28,20},{1,9},{5... | collective-permute-start | bytes 3145736 | tf_op jit(solution)/shard_map/ppermute | solution.py:27
  662.3 31.7 %collective-permute-start.53 = (f32[264,512]{1,0:T(8,128)S(1)}, f32[264,512]{1,0:T(8,128)S(1)}, u32[]{:S(2)}, u32[]{:S(2)}) collective-permute-start(f32[264,512]{1,0:T(8,128)S(1)} %pad_maximum_fusion.23), channel_id=1, source_target_pairs={{2,0},{0,1},{6,2},{4,3},{3,4},{1,5},{7,6},{5,7},{10,8},{8,9},{14,1... | collective-permute-start | bytes 1622024 | tf_op jit(solution)/shard_map/ppermute | solution.py:167
  (220 other events, 1665.1 us)
Sparse Core Ops, SparseCore 0:
  337.0 125.6 all-reduce.31
  570.4 151.9 all-reduce.29

commit v4 on v3

--- a/solution.py
+++ b/solution.py
@@ -162,6 +162,8 @@
                     row, few = self.piece(rows, u * self.micro, self.micro), self.piece(more, u * self.micro, self.micro, 1)
                 message = row
                 if more.shape[0]:
+                    message = row
+                if more.shape[0]:
                     message = jnp.concatenate([row, jnp.pad(few, ((0, 0), (0, wide - few.shape[1])))], axis=0)
                 if self.paired:
                     messages.append(lax.ppermute(message, ("dp", "ep"), self.route(group, u, True)))
@@ -436,7 +438,7 @@
     inner[...] = summed(normed, grad_pre)
 
 
-def expert_weight_grads(kept):
+def expert_weight_grads(kept, brief):
     normed, active, grad_result, grad_pre = zip(*kept)
     rows, width = normed[0].shape
     inner = active[0].shape[1]
@@ -454,7 +456,7 @@
             jax.ShapeDtypeStruct((inner, width), jnp.float32),
         ],
         compiler_params=pltpu.CompilerParams(vmem_limit_bytes=48 * 1024 * 1024),
-        cost_estimate=pl.CostEstimate(
+        cost_estimate=BRIEF if brief else pl.CostEstimate(
             flops=12 * count * rows * width * inner, bytes_accessed=16 * count * rows * inner, transcendentals=0
         ),
         name="weights",
@@ -812,7 +814,7 @@
     sums, router_one = add_up(small)
     gain_three, shift_three, gain_four, shift_four = (sums[k] for k in range(4))
     kept, _ = lax.optimization_barrier((kept, back[:-2]))
-    expert_one = lax.psum(expert_weight_grads(kept), "dp")
+    expert_one = lax.psum(expert_weight_grads(kept, False), "dp")
     grad_third = pick(work[1][1], jnp.concatenate(back, axis=0))
     project_grad = product(swished.T, grad_third)
     grad_shaped = product(grad_third, project_weight.T) * swish_slope(shaped)
@@ -905,17 +907,27 @@
         small.append((sums, product(normed.T, grad_logits[:, :experts])))
     sums, router_zero = add_up(small)
     gain_zero, shift_zero = sums[0], sums[1]
-    expert_zero = lax.psum(expert_weight_grads(kept), "dp")
-    sources = dense.step(sources, 2 * over_ep + 1)
-    frame_messages = layout.expert_to_home(sources)
+    expert_zero = expert_weight_grads(kept, True)
+    sources, dense.parts = after((sources, dense.parts), *expert_zero)
+    expert_zero = lax.psum(expert_zero, "dp")
+    logit_slots = jnp.concatenate(layout.expert_to_home([(more.T, more[:0]) for _, more in sources]), axis=0).T
+    logit_zero = pick_columns(logit_slots[:experts], home[0][0])
+    router_zero = router_zero + product(logit_zero, home_rows).T
+    late = jnp.concatenate([gain_zero[None], shift_zero[None], router_zero.T, early], axis=0)
+    ahead = 2 * over_ep + 1
+    for step in bits_of("ep") + bits_of("dp"):
+        late = late + swap(late, *step)
+        if ahead:
+            late = dense.step(late)
+            ahead -= 1
+    frame_rows, late = dense.step(([v for v, _ in sources], late), ahead) if ahead else lax.optimization_barrier(
+        ([v for v, _ in sources], late)
+    )
+    frame_messages = layout.expert_to_home([(v, jnp.zeros((0, v.shape[0]), v.dtype)) for v in frame_rows])
     wholes = [lax.pad(one[None], 0.0, ((1, 0, 0), (0, 0, 0), (0, 0, 0))) for one in expert_one]
     frame_messages, wholes = dense.step((frame_messages, wholes), over_dp - 1)
-    rows_back, logit_slots = layout.opened(frame_messages)
-    logit_zero = pick_columns(logit_slots[:experts], home[0][0])
-    router_zero = router_zero + product(logit_zero, home_rows).T
-    frames_grad = pick(home[0][1], rows_back).reshape(micro, rows, width)
-    late = jnp.concatenate([gain_zero[None], shift_zero[None], router_zero.T, early], axis=0)
-    late = butterfly(dense.step(late), bits_of("ep") + bits_of("dp"))
+    frames_grad = pick(home[0][1], jnp.concatenate(frame_messages, axis=0)).reshape(micro, rows, width)
+    late = dense.step(late)
     late, early = late[: 2 + experts], late[2 + experts :]
     packed_grad, project_grad = dense.parts[0][:, : 3 * width], dense.parts[0][:, 3 * width :]
     mixing_grad, point_grad = dense.parts[1][:, :width], dense.parts[1][:, width:]

time: 771 us -> 797 us (1.034)
  waiting for transfers between devices: 155 us -> 186 us
  local copies, waits for them, and re-layouts: 158 us -> 147 us
    ppermute x49, waiting for transfers between devices: 146 us -> 167 us  [swap(): return lax.ppermute(values, axis, [(i, i ^ bit) for i in range(count)])]
    slice x38 -> x42, local copies, waits for them, and re-layouts: 23.7 us -> 28.6 us  [piece(): lax.slice_in_dim(values, at * self.capacity, (at + count) * self.capacity...]
    unnamed x381 -> x351, local copies, waits for them, and re-layouts: 24.8 us -> 20.6 us
    ppermute x8 -> x12, starting transfers between devices: 18 us -> 20.8 us  [expert_to_home(): lax.ppermute(message, ('dp', 'ep'), self.route(group, u, True))]
  transfers between devices with their start and end apart: 69 -> 73, of which waited for: 21 -> 26; matrix products, arithmetic and copies ran while one was open for 32% -> 28% of each run, Pallas kernels for 21% -> 21%
where the time goes in v4:
time: 797 us; the launch traced here: 789 us
  waiting for transfers between devices  186 us (23%)
  Pallas kernels  163 us (20%)
  local copies, waits for them, and re-layouts  147 us (18%)
  starting transfers between devices  136 us (17%)
  other arithmetic  79.9 us (10%)
  matrix products  59.7 us (7%)
  between operations  17.5 us (2%)
    ppermute x49, waiting for transfers between devices, swap(): return lax.ppermute(values, axis, [(i, i ^ bit) for i in range(count)])  167 us
    pallas_call x6, Pallas kernels, expert_call(): pl.pallas_call(functools.partial(kernel, experts), grid=(rows // block,),...  87.8 us
    ppermute x49, starting transfers between devices, swap(): return lax.ppermute(values, axis, [(i, i ^ bit) for i in range(count)])  73.8 us
    dot_general x20, matrix products, product(): return jnp.matmul(left, right, precision=HIGH)  38.7 us
    ppermute x8, starting transfers between devices, home_to_expert(): got.append(lax.ppermute(message, ('dp', 'ep'), self.route(group, u, False)))  36 us
    pallas_call x2, Pallas kernels, expert_weight_grads(): pl.pallas_call(functools.partial(weight_kernel, count), grid=(inner // wi...  35.1 us
    slice x42, local copies, waits for them, and re-layouts, piece(): lax.slice_in_dim(values, at * self.capacity, (at + count) * self.capacity...  28.6 us
    pallas_call x1, Pallas kernels, attend_back(): pl.pallas_call(functools.partial(attend_back_kernel, chunk, (width // slo...  26.4 us
  transfers between devices with their start and end apart: 73, of which 26 were waited for; matrix products, arithmetic and copies ran while one was open for 28% of the time, Pallas kernels for 21%

profile of v4, /device:TPU:0, one launch (start us, length us, event | category | flops | bytes accessed | tf_op | source)
XLA Modules:
  0.0 788.5 jit_solution(17022896269502302798)
XLA Ops:
  22.5 5.0 collective-permute-start.1
  39.1 6.7 collective-permute-start.5
  45.8 5.5 collective-permute-start.6
  57.0 9.4 %forward.2 = (f32[512,512]{1,0:T(8,128)S(1)}, f32[512,512]{1,0:T(8,128)S(1)}, f32[512,2048]{1,0:T(8,128)}) custom-call(f32[512,512]{1,0:T(8,128)S(1)} %pad_maximum_fusion.8.hidden, f32[512,128]{1,0:T(8,128)S(1)} %pad.75.extra, f32[1,128]{1,0:T(1,128)S(1)} %compare_convert_fusion.2.own, f32[2,512]{1,0:T(2,128)S(1)} %get-tuple-element.513.norm, ...), custom_call_target="tpu_custom_call" | custom-call | flops 1 | bytes 1 | tf_op jit(solution)/shard_map/forward/pallas_call | solution.py:408
  71.4 10.4 %forward.3 = (f32[512,512]{1,0:T(8,128)S(1)}, f32[512,512]{1,0:T(8,128)S(1)}, f32[512,2048]{1,0:T(8,128)}) custom-call(f32[512,512]{1,0:T(8,128)S(1)} %pad_maximum_fusion.9.hidden, f32[512,128]{1,0:T(8,128)S(1)} %pad.79.extra, f32[1,128]{1,0:T(1,128)S(1)} %compare_convert_fusion.2.own, f32[2,512]{1,0:T(2,128)S(1)} %get-tuple-element.513.norm, ...), custom_call_target="tpu_custom_call" | custom-call | flops 1 | bytes 1 | tf_op jit(solution)/shard_map/forward/pallas_call | solution.py:408
  81.9 18.2 %collective-permute-start.7 = (f32[256,512]{1,0:T(8,128)S(1)}, f32[256,512]{1,0:T(8,128)S(1)}, u32[]{:S(2)}, u32[]{:S(2)}) collective-permute-start(f32[256,512]{1,0:T(8,128)S(1)} %get-tuple-element.379), channel_id=1, source_target_pairs={{0,1},{1,0},{2,3},{3,2},{4,5},{5,4},{6,7},{7,6},{8,9},{9,8},{10,11... | collective-permute-start | bytes 1572872 | tf_op jit(solution)/shard_map/ppermute | solution.py:27
  103.8 18.6 %collective-permute-done.7 = f32[256,512]{1,0:T(8,128)S(1)} collective-permute-done((f32[256,512]{1,0:T(8,128)S(1)}, f32[256,512]{1,0:T(8,128)S(1)}, u32[]{:S(2)}, u32[]{:S(2)}) %collective-permute-start.7) | collective-permute-done | bytes 524320 | tf_op jit(solution)/shard_map/ppermute | solution.py:27
  131.3 5.8 collective-permute-start.16
  143.6 8.6 %collective-permute-done.17 = f32[264,512]{1,0:T(8,128)} collective-permute-done((f32[264,512]{1,0:T(8,128)}, f32[264,512]{1,0:T(8,128)}, u32[]{:S(2)}, u32[]{:S(2)}) %collective-permute-start.17) | collective-permute-done | bytes 540704 | tf_op jit(solution)/shard_map/ppermute | solution.py:140
  152.3 5.6 collective-permute-start.20
  157.9 6.4 collective-permute-start.21
  170.9 13.4 %attend.1 = (f32[512,512]{1,0:T(8,128)S(1)}, f32[4,8,512]{2,1,0:T(8,128)S(1)}) custom-call(f32[8]{0:T(128)S(1)} %copy-done.32, f32[1024,512]{1,0:T(8,128)S(1)} %convert_select_fusion.dist, f32[512,1536]{1,0:T(8,128)S(1)} %copy-done.6, f32[1024,1024]{1,0:T(8,128)S(1)} %pad_maximum_fusion.k_ref.v_ref, f32[1024,1024]{1,0:T(8,128)S(1)} %pad_maximum_fusion.k_ref.v_ref), custom_call_target="tpu_custom_call" | custom-call | flops 1 | bytes 1 | tf_op jit(solution)/shard_map/attend/pallas_call | solution.py:620
  224.8 18.2 %collective-permute-done.15 = f32[256,512]{1,0:T(8,128)S(1)} collective-permute-done((f32[256,512]{1,0:T(8,128)S(1)}, f32[256,512]{1,0:T(8,128)S(1)}, u32[]{:S(2)}, u32[]{:S(2)}) %collective-permute-start.15) | collective-permute-done | bytes 524320 | tf_op jit(solution)/shard_map/ppermute | solution.py:27
  245.8 19.6 %both.2 = (f32[512,512]{1,0:T(8,128)S(1)}, f32[512,512]{1,0:T(8,128)S(1)}, f32[512,128]{1,0:T(8,128)S(1)}, f32[512,512]{1,0:T(8,128)S(1)}, f32[512,2048]{1,0:T(8...) custom-call(f32[512,512]{1,0:T(8,128)S(1)} %pad_maximum_fusion.10.hidden, ...), custom_call_target="tpu_custom_call" | custom-call | flops 1 | bytes 1 | tf_op jit(solution)/shard_map/both/pallas_call | solution.py:408
  277.5 19.5 %both.3 = (f32[512,512]{1,0:T(8,128)S(1)}, f32[512,512]{1,0:T(8,128)S(1)}, f32[512,128]{1,0:T(8,128)S(1)}, f32[512,512]{1,0:T(8,128)S(1)}, f32[512,2048]{1,0:T(8...) custom-call(f32[512,512]{1,0:T(8,128)S(1)} %pad_maximum_fusion.12.hidden, ...), custom_call_target="tpu_custom_call" | custom-call | flops 1 | bytes 1 | tf_op jit(solution)/shard_map/both/pallas_call | solution.py:408
  299.7 17.7 %weights.2 = (f32[512,2048]{1,0:T(8,128)}, f32[2048,512]{1,0:T(8,128)}) custom-call(f32[512,512]{1,0:T(8,128)S(1)} %copy-done.21, f32[512,512]{1,0:T(8,128)S(1)} %get-tuple-element.173.refs_1_, f32[512,512]{1,0:T(8,128)S(1)} %copy-done.34, f32[512,512]{1,0:T(8,128)S(1)} %get-tuple-element.175.refs_3_, f32[512,2048]{1,0:T(8,128)} %get-tuple-element.176.refs_4_, ...), custom_call_target="tpu_custom_call" | custom-call | flops 12884901888 | bytes 33554432 | tf_op jit(solution)/shard_map/weights/pallas_call | solution.py:449
  343.3 9.0 %multiply_reduce_fusion = (f32[512]{0:T(512)}, f32[512]{0:T(512)}, f32[512]{0:T(512)}, f32[512]{0:T(512)}, f32[512]{0:T(512)}, /*index=5*/f32[512]{0:T(512)}, f32[512]{0:T(512)}, f32[512]{0:T(512)}, f32[512,512]{1,0:T(8,128)S(1)}) fusion(f32[7,512]{1,0:T(8,128)S(1)} %get-tuple-element.477, f32[512,512]{1,0:T(8,128)} %copy-done.46, ...), kind=kLoop, calls=%fused_computation.204 | loop fusion | flops 8122368 | bytes 4237316 | tf_op jit(solution)/shard_map/reduce_sum | solution.py:845
  353.4 5.9 collective-permute-start.29
  370.4 10.5 %fusion.58 = (f32[512,512]{1,0:T(8,128)S(1)}, f32[512,512]{1,0:T(8,128)S(1)}) fusion(f32[512,1024]{1,0:T(8,128)} %copy-done.42, f32[512]{0:T(512)S(1)} %copy-done.92, f32[512,512]{1,0:T(8,128)} %copy-done.51, f32[7,512]{1,0:T(8,128)S(1)} %get-tuple-element.459, f32[512]{0:T(512)} %bitcast.311, f32[512]{0:T(512)} %bitcast.313, f32[512]{0:T(512)} %bitcast.287, ...), kind=kLoop, calls=%fused_computation.124 | loop fusion | flops 13369344 | bytes 5304320 | tf_op jit(solution)/shard_map/transpose(jvp())/mul | solution.py:770
  394.8 26.4 %attend_back.1 = (f32[512,512]{1,0:T(8,128)S(1)}, f32[2,1024,512]{2,1,0:T(8,128)S(1)}, f32[4,8,512]{2,1,0:T(8,128)S(1)}) custom-call(f32[8]{0:T(128)S(1)} %copy-done.32, f32[1024,512]{1,0:T(8,128)S(1)} %copy-done.9, f32[512,1536]{1,0:T(8,128)S(1)} %copy-done.7, f32[1024,1024]{1,0:T(8,128)} %copy-done.2, f32[1024,1024]{1,0:T(8,128)} %copy-done.2, ...), custom_call_target="tpu_custom_call" | custom-call | flops 1 | bytes 1 | tf_op jit(solution)/shard_map/attend_back/pallas_call | solution.py:646
  481.1 20.6 %collective-permute-done.35 = f32[256,512]{1,0:T(8,128)S(1)} collective-permute-done((f32[256,512]{1,0:T(8,128)S(1)}, f32[256,512]{1,0:T(8,128)S(1)}, u32[]{:S(2)}, u32[]{:S(2)}) %collective-permute-start.35) | collective-permute-done | bytes 524320 | tf_op jit(solution)/shard_map/ppermute | solution.py:27
  506.9 14.5 %backward.2 = (f32[512,512]{1,0:T(8,128)S(1)}, f32[512,128]{1,0:T(8,128)S(1)}, f32[512,512]{1,0:T(8,128)S(1)}, f32[512,2048]{1,0:T(8,128)}, f32[512,512]{1,0:T(8...) custom-call(f32[512,512]{1,0:T(8,128)S(1)} %copy-done.11, f32[512,128]{1,0:T(8,128)S(1)} %copy-done.17, ...), custom_call_target="tpu_custom_call" | custom-call | flops 1 | bytes 1 | tf_op jit(solution)/shard_map/backward/pallas_call | solution.py:408
  533.8 14.4 %backward.3 = (f32[512,512]{1,0:T(8,128)S(1)}, f32[512,128]{1,0:T(8,128)S(1)}, f32[512,512]{1,0:T(8,128)S(1)}, f32[512,2048]{1,0:T(8,128)}, f32[512,512]{1,0:T(8...) custom-call(f32[512,512]{1,0:T(8,128)S(1)} %copy-done.13, f32[512,128]{1,0:T(8,128)S(1)} %pad.79.extra, ...), custom_call_target="tpu_custom_call" | custom-call | flops 1 | bytes 1 | tf_op jit(solution)/shard_map/backward/pallas_call | solution.py:408
  548.8 17.3 %weights.3 = (f32[512,2048]{1,0:T(8,128)}, f32[2048,512]{1,0:T(8,128)}) custom-call(f32[512,512]{1,0:T(8,128)S(1)} %get-tuple-element.201.refs_0_, f32[512,512]{1,0:T(8,128)S(1)} %get-tuple-element.202.refs_1_, f32[512,512]{1,0:T(8,128)S(1)} %get-tuple-element.203.refs_2_, f32[512,512]{1,0:T(8,128)S(1)} %get-tuple-element.204.refs_3_, ...), custom_call_target="tpu_custom_call" | custom-call | flops 1 | bytes 1 | tf_op jit(solution)/shard_map/weights/pallas_call | solution.py:449
  617.0 16.6 %collective-permute-done.49 = f32[36,512]{1,0:T(8,128)S(1)} collective-permute-done((f32[36,512]{1,0:T(8,128)S(1)}, f32[36,512]{1,0:T(8,128)S(1)}, u32[]{:S(2)}, u32[]{:S(2)}) %collective-permute-start.49) | collective-permute-done | bytes 73760 | tf_op jit(solution)/shard_map/ppermute | solution.py:27
  633.7 5.2 collective-permute-done.50
  662.3 8.3 %collective-permute-done.60 = f32[32,1536]{1,0:T(8,128)S(1)} collective-permute-done((f32[32,1536]{1,0:T(8,128)S(1)}, f32[32,1536]{1,0:T(8,128)S(1)}, u32[]{:S(2)}, u32[]{:S(2)}) %collective-permute-start.60) | collective-permute-done | bytes 196640 | tf_op jit(solution)/shard_map/ppermute | solution.py:27
  680.4 10.7 %collective-permute-done.67 = f32[64,1536]{1,0:T(8,128)S(1)} collective-permute-done((f32[64,1536]{1,0:T(8,128)S(1)}, f32[64,1536]{1,0:T(8,128)S(1)}, u32[]{:S(2)}, u32[]{:S(2)}) %collective-permute-start.67) | collective-permute-done | bytes 393248 | tf_op jit(solution)/shard_map/ppermute | solution.py:27
  693.2 8.8 %collective-permute-done.65 = f32[64,2048]{1,0:T(8,128)S(1)} collective-permute-done((f32[64,2048]{1,0:T(8,128)S(1)}, f32[64,2048]{1,0:T(8,128)S(1)}, u32[]{:S(2)}, u32[]{:S(2)}) %collective-permute-start.65) | collective-permute-done | bytes 524320 | tf_op jit(solution)/shard_map/ppermute | solution.py:27
  702.6 21.2 %collective-permute-done.68 = f32[128,1536]{1,0:T(8,128)S(1)} collective-permute-done((f32[128,1536]{1,0:T(8,128)S(1)}, f32[128,1536]{1,0:T(8,128)S(1)}, u32[]{:S(2)}, u32[]{:S(2)}) %collective-permute-start.68) | collective-permute-done | bytes 786464 | tf_op jit(solution)/shard_map/ppermute | solution.py:27
  727.4 6.6 collective-permute-done.66
  747.0 7.8 all-reduce.26.cloned.1.call-done
  (782 shorter events, 378.8 us)
Async XLA Ops:
  7.2 498.6 %all-reduce.28.cloned.1.call-start = ((), (), s32[]{:S(2)}) async-start(), calls=%async_computation.1 | async-start | bytes 16777216 | tf_op jit(solution)/shard_map/psum | solution.py:817
  39.1 28.3 %collective-permute-start.5 = (f32[264,512]{1,0:T(8,128)}, f32[264,512]{1,0:T(8,128)}, u32[]{:S(2)}, u32[]{:S(2)}) collective-permute-start(f32[264,512]{1,0:T(8,128)} %get-tuple-element.135), channel_id=1, source_target_pairs={{0,1},{1,3},{2,5},{3,7},{4,0},{5,2},{6,4},{7,6},{8,9},{9,11},{10,1... | collective-permute-start | bytes 1622024 | tf_op jit(solution)/shard_map/ppermute | solution.py:140
  67.4 36.3 %collective-permute-start.4 = (f32[256,512]{1,0:T(8,128)S(1)}, f32[256,512]{1,0:T(8,128)}, u32[]{:S(2)}, u32[]{:S(2)}) collective-permute-start(f32[256,512]{1,0:T(8,128)S(1)} %get-tuple-element.378), channel_id=1, source_target_pairs={{0,2},{1,3},{2,0},{3,1},{4,6},{5,7},{6,4},{7,5},{8,10},{9,11},{10,... | collective-permute-start | bytes 1572872 | tf_op jit(solution)/shard_map/ppermute | solution.py:27
  81.9 40.5 %collective-permute-start.7 = (f32[256,512]{1,0:T(8,128)S(1)}, f32[256,512]{1,0:T(8,128)S(1)}, u32[]{:S(2)}, u32[]{:S(2)}) collective-permute-start(f32[256,512]{1,0:T(8,128)S(1)} %get-tuple-element.379), channel_id=1, source_target_pairs={{0,1},{1,0},{2,3},{3,2},{4,5},{5,4},{6,7},{7,6},{8,9},{9,8},{10,11... | collective-permute-start | bytes 1572872 | tf_op jit(solution)/shard_map/ppermute | solution.py:27
  130.2 37.6 %collective-permute-start.9 = (f32[512,1024]{1,0:T(8,128)}, f32[512,1024]{1,0:T(8,128)}, u32[]{:S(2)}, u32[]{:S(2)}) collective-permute-start(f32[512,1024]{1,0:T(8,128)} %slice_bitcast_fusion), channel_id=1, source_target_pairs={{0,4},{4,0},{8,12},{12,8},{16,20},{20,16},{24,28},{28,24},{1,5},{5... | collective-permute-start | bytes 6291464 | tf_op jit(solution)/shard_map/ppermute | solution.py:27
  152.3 47.2 %collective-permute-start.20 = (f32[264,512]{1,0:T(8,128)}, f32[264,512]{1,0:T(8,128)}, u32[]{:S(2)}, u32[]{:S(2)}) collective-permute-start(f32[264,512]{1,0:T(8,128)} %select_maximum_fusion.1), channel_id=1, source_target_pairs={{0,1},{1,3},{2,5},{3,7},{4,0},{5,2},{6,4},{7,6},{8,9},{9,11},{10,1... | collective-permute-start | bytes 1622024 | tf_op jit(solution)/shard_map/ppermute | solution.py:140
  157.9 46.0 %collective-permute-start.21 = (f32[264,512]{1,0:T(8,128)}, f32[264,512]{1,0:T(8,128)}, u32[]{:S(2)}, u32[]{:S(2)}) collective-permute-start(f32[264,512]{1,0:T(8,128)} %select_maximum_fusion), channel_id=1, source_target_pairs={{0,3},{1,1},{2,7},{3,5},{4,2},{5,0},{6,6},{7,4},{8,11},{9,9},{10,1... | collective-permute-start | bytes 1622024 | tf_op jit(solution)/shard_map/ppermute | solution.py:140
  244.1 30.8 %collective-permute-start.18 = (f32[256,512]{1,0:T(8,128)}, f32[256,512]{1,0:T(8,128)}, u32[]{:S(2)}, u32[]{:S(2)}) collective-permute-start(f32[256,512]{1,0:T(8,128)} %get-tuple-element.374), channel_id=1, source_target_pairs={{0,1},{1,0},{2,3},{3,2},{4,5},{5,4},{6,7},{7,6},{8,9},{9,8},{10,11... | collective-permute-start | bytes 1572872 | tf_op jit(solution)/shard_map/ppermute | solution.py:27
  244.1 30.8 %collective-permute-start.19 = (f32[256,512]{1,0:T(8,128)}, f32[256,512]{1,0:T(8,128)}, u32[]{:S(2)}, u32[]{:S(2)}) collective-permute-start(f32[256,512]{1,0:T(8,128)} %get-tuple-element.373), channel_id=1, source_target_pairs={{0,3},{1,2},{2,1},{3,0},{4,7},{5,6},{6,5},{7,4},{8,11},{9,10},{10,... | collective-permute-start | bytes 1572872 | tf_op jit(solution)/shard_map/ppermute | solution.py:27
  269.5 30.2 %collective-permute-start.22 = (f32[256,512]{1,0:T(8,128)}, f32[256,512]{1,0:T(8,128)}, u32[]{:S(2)}, u32[]{:S(2)}) collective-permute-start(f32[256,512]{1,0:T(8,128)} %get-tuple-element.370), channel_id=1, source_target_pairs={{0,2},{1,3},{2,0},{3,1},{4,6},{5,7},{6,4},{7,5},{8,10},{9,11},{10,... | collective-permute-start | bytes 1572872 | tf_op jit(solution)/shard_map/ppermute | solution.py:27
  298.1 24.3 %collective-permute-start.24 = (f32[256,512]{1,0:T(8,128)S(1)}, f32[256,512]{1,0:T(8,128)S(1)}, u32[]{:S(2)}, u32[]{:S(2)}) collective-permute-start(f32[256,512]{1,0:T(8,128)S(1)} %get-tuple-element.372), channel_id=1, source_target_pairs={{0,3},{1,2},{2,1},{3,0},{4,7},{5,6},{6,5},{7,4},{8,11},{9,10},{10,... | collective-permute-start | bytes 1572872 | tf_op jit(solution)/shard_map/ppermute | solution.py:27
  334.5 420.3 %all-reduce.26.cloned.1.call-start = ((), (), s32[]{:S(2)}) async-start(), calls=%async_computation | async-start | bytes 16777216 | tf_op jit(solution)/shard_map/psum | solution.py:912
  353.4 87.9 %collective-permute-start.29 = (f32[264,512]{1,0:T(8,128)}, f32[264,512]{1,0:T(8,128)}, u32[]{:S(2)}, u32[]{:S(2)}) collective-permute-start(f32[264,512]{1,0:T(8,128)} %pad_maximum_fusion.18), channel_id=1, source_target_pairs={{0,0},{2,1},{4,2},{6,3},{1,4},{3,5},{5,6},{7,7},{8,8},{10,9},{12,1... | collective-permute-start | bytes 1622024 | tf_op jit(solution)/shard_map/ppermute | solution.py:169
  360.1 83.9 %collective-permute-start.30 = (f32[264,512]{1,0:T(8,128)}, f32[264,512]{1,0:T(8,128)}, u32[]{:S(2)}, u32[]{:S(2)}) collective-permute-start(f32[264,512]{1,0:T(8,128)} %pad_maximum_fusion.19), channel_id=1, source_target_pairs={{2,0},{0,1},{6,2},{4,3},{3,4},{1,5},{7,6},{5,7},{10,8},{8,9},{14,1... | collective-permute-start | bytes 1622024 | tf_op jit(solution)/shard_map/ppermute | solution.py:169
  366.6 80.1 %collective-permute-start.31 = (f32[264,512]{1,0:T(8,128)}, f32[264,512]{1,0:T(8,128)}, u32[]{:S(2)}, u32[]{:S(2)}) collective-permute-start(f32[264,512]{1,0:T(8,128)} %pad_maximum_fusion.20), channel_id=1, source_target_pairs={{1,0},{3,1},{5,2},{7,3},{0,4},{2,5},{4,6},{6,7},{9,8},{11,9},{13,1... | collective-permute-start | bytes 1622024 | tf_op jit(solution)/shard_map/ppermute | solution.py:169
  425.4 27.5 %collective-permute-start.34 = (f32[2,512,512]{2,1,0:T(8,128)}, f32[2,512,512]{2,1,0:T(8,128)}, u32[]{:S(2)}, u32[]{:S(2)}) collective-permute-start(f32[2,512,512]{2,1,0:T(8,128)} %slice.934), channel_id=1, source_target_pairs={{0,4},{4,0},{8,12},{12,8},{16,20},{20,16},{24,28},{28,24},{1,5},{5... | collective-permute-start | bytes 6291464 | tf_op jit(solution)/shard_map/ppermute | solution.py:27
  441.2 37.1 %collective-permute-start.37 = (f32[256,1536]{1,0:T(8,128)}, f32[256,1536]{1,0:T(8,128)}, u32[]{:S(2)}, u32[]{:S(2)}) collective-permute-start(f32[256,1536]{1,0:T(8,128)} %fusion.47), channel_id=1, source_target_pairs={{0,4},{4,0},{8,12},{12,8},{16,20},{20,16},{24,28},{28,24},{1,5},{5... | collective-permute-start | bytes 4718600 | tf_op jit(solution)/shard_map/ppermute | solution.py:27
  469.5 52.4 %collective-permute-start.36 = (f32[256,2048]{1,0:T(8,128)}, f32[256,2048]{1,0:T(8,128)}, u32[]{:S(2)}, u32[]{:S(2)}) collective-permute-start(f32[256,2048]{1,0:T(8,128)} %fusion.2), channel_id=1, source_target_pairs={{0,4},{4,0},{8,12},{12,8},{16,20},{20,16},{24,28},{28,24},{1,5},{5... | collective-permute-start | bytes 6291464 | tf_op jit(solution)/shard_map/ppermute | solution.py:27
  473.6 28.1 %collective-permute-start.35 = (f32[256,512]{1,0:T(8,128)S(1)}, f32[256,512]{1,0:T(8,128)S(1)}, u32[]{:S(2)}, u32[]{:S(2)}) collective-permute-start(f32[256,512]{1,0:T(8,128)S(1)} %get-tuple-element.359), channel_id=1, source_target_pairs={{0,2},{1,3},{2,0},{3,1},{4,6},{5,7},{6,4},{7,5},{8,10},{9,11},{10,... | collective-permute-start | bytes 1572872 | tf_op jit(solution)/shard_map/ppermute | solution.py:27
  503.5 25.8 %collective-permute-start.39 = (f32[256,512]{1,0:T(8,128)}, f32[256,512]{1,0:T(8,128)}, u32[]{:S(2)}, u32[]{:S(2)}) collective-permute-start(f32[256,512]{1,0:T(8,128)} %get-tuple-element.357), channel_id=1, source_target_pairs={{0,3},{1,2},{2,1},{3,0},{4,7},{5,6},{6,5},{7,4},{8,11},{9,10},{10,... | collective-permute-start | bytes 1572872 | tf_op jit(solution)/shard_map/ppermute | solution.py:27
  529.4 37.8 %collective-permute-start.41 = (f32[128,1536]{1,0:T(8,128)S(1)}, f32[128,1536]{1,0:T(8,128)}, u32[]{:S(2)}, u32[]{:S(2)}) collective-permute-start(f32[128,1536]{1,0:T(8,128)S(1)} %constant_dynamic-slice_fusion.6), channel_id=1, source_target_pairs={{0,16},{4,20},{8,24},{12,28},{16,0},{20,4},{24,8},{28,12},{1,17},{... | collective-permute-start | bytes 2359304 | tf_op jit(solution)/shard_map/ppermute | solution.py:27
  531.1 37.4 %collective-permute-start.40 = (f32[128,2048]{1,0:T(8,128)S(1)}, f32[128,2048]{1,0:T(8,128)S(1)}, u32[]{:S(2)}, u32[]{:S(2)}) collective-permute-start(f32[128,2048]{1,0:T(8,128)S(1)} %constant_dynamic-slice_fusion.7), channel_id=1, source_target_pairs={{0,8},{4,12},{8,0},{12,4},{16,24},{20,28},{24,16},{28,20},{1,9},{5... | collective-permute-start | bytes 3145736 | tf_op jit(solution)/shard_map/ppermute | solution.py:27
  570.4 39.0 %collective-permute-start.48 = (f32[64,1536]{1,0:T(8,128)}, f32[64,1536]{1,0:T(8,128)}, u32[]{:S(2)}, u32[]{:S(2)}) collective-permute-start(f32[64,1536]{1,0:T(8,128)} %constant_dynamic-slice_fusion.4), channel_id=1, source_target_pairs={{0,8},{4,12},{8,0},{12,4},{16,24},{20,28},{24,16},{28,20},{1,9},{5... | collective-permute-start | bytes 1179656 | tf_op jit(solution)/shard_map/ppermute | solution.py:27
  614.6 24.2 %collective-permute-start.50 = (f32[32,2048]{1,0:T(8,128)S(1)}, f32[32,2048]{1,0:T(8,128)S(1)}, u32[]{:S(2)}, u32[]{:S(2)}) collective-permute-start(f32[32,2048]{1,0:T(8,128)S(1)} %constant_dynamic-slice_fusion.3), channel_id=1, source_target_pairs={{0,2},{1,3},{2,0},{3,1},{4,6},{5,7},{6,4},{7,5},{8,10},{9,11},{10,... | collective-permute-start | bytes 786440 | tf_op jit(solution)/shard_map/ppermute | solution.py:27
  676.5 25.5 %collective-permute-start.65 = (f32[64,2048]{1,0:T(8,128)S(1)}, f32[64,2048]{1,0:T(8,128)S(1)}, u32[]{:S(2)}, u32[]{:S(2)}) collective-permute-start(f32[64,2048]{1,0:T(8,128)S(1)} %constant_dynamic-update-slice_fusion.14), channel_id=1, source_target_pairs={{0,16},{4,20},{8,24},{12,28},{16,0},{20,4},{24,8},{28,12},{1,17},{... | collective-permute-start | bytes 1572872 | tf_op jit(solution)/shard_map/ppermute | solution.py:27
  678.2 56.8 %collective-permute-start.64 = (f32[256,512]{1,0:T(8,128)S(1)}, f32[256,512]{1,0:T(8,128)S(1)}, u32[]{:S(2)}, u32[]{:S(2)}) collective-permute-start(f32[256,512]{1,0:T(8,128)S(1)} %pad_maximum_fusion.25), channel_id=1, source_target_pairs={{3,0},{1,1},{7,2},{5,3},{2,4},{0,5},{6,6},{4,7},{11,8},{9,9},{15,1... | collective-permute-start | bytes 1572872 | tf_op jit(solution)/shard_map/ppermute | solution.py:169
  680.2 54.9 %collective-permute-start.63 = (f32[256,512]{1,0:T(8,128)S(1)}, f32[256,512]{1,0:T(8,128)S(1)}, u32[]{:S(2)}, u32[]{:S(2)}) collective-permute-start(f32[256,512]{1,0:T(8,128)S(1)} %pad_maximum_fusion.24), channel_id=1, source_target_pairs={{1,0},{3,1},{5,2},{7,3},{0,4},{2,5},{4,6},{6,7},{9,8},{11,9},{13,1... | collective-permute-start | bytes 1572872 | tf_op jit(solution)/shard_map/ppermute | solution.py:169
  691.1 32.7 %collective-permute-start.68 = (f32[128,1536]{1,0:T(8,128)S(1)}, f32[128,1536]{1,0:T(8,128)S(1)}, u32[]{:S(2)}, u32[]{:S(2)}) collective-permute-start(f32[128,1536]{1,0:T(8,128)S(1)} %constant_dynamic-update-slice_fusion.6), channel_id=1, source_target_pairs={{0,16},{4,20},{8,24},{12,28},{16,0},{20,4},{24,8},{28,12},{1,17},{... | collective-permute-start | bytes 2359304 | tf_op jit(solution)/shard_map/ppermute | solution.py:27
  702.0 31.9 %collective-permute-start.66 = (f32[128,2048]{1,0:T(8,128)S(1)}, f32[128,2048]{1,0:T(8,128)S(1)}, u32[]{:S(2)}, u32[]{:S(2)}) collective-permute-start(f32[128,2048]{1,0:T(8,128)S(1)} %constant_dynamic-update-slice_fusion.10), channel_id=1, source_target_pairs={{0,8},{4,12},{8,0},{12,4},{16,24},{20,28},{24,16},{28,20},{1,9},{5... | collective-permute-start | bytes 3145736 | tf_op jit(solution)/shard_map/ppermute | solution.py:27
  702.2 32.8 %collective-permute-start.62 = (f32[256,512]{1,0:T(8,128)S(1)}, f32[256,512]{1,0:T(8,128)S(1)}, u32[]{:S(2)}, u32[]{:S(2)}) collective-permute-start(f32[256,512]{1,0:T(8,128)S(1)} %pad_maximum_fusion.23), channel_id=1, source_target_pairs={{2,0},{0,1},{6,2},{4,3},{3,4},{1,5},{7,6},{5,7},{10,8},{8,9},{14,1... | collective-permute-start | bytes 1572872 | tf_op jit(solution)/shard_map/ppermute | solution.py:169
  735.0 26.9 %collective-permute-start.70 = (f32[256,1536]{1,0:T(8,128)S(1)}, f32[256,1536]{1,0:T(8,128)S(1)}, u32[]{:S(2)}, u32[]{:S(2)}) collective-permute-start(f32[256,1536]{1,0:T(8,128)S(1)} %constant_dynamic-update-slice_fusion.4), channel_id=1, source_target_pairs={{0,4},{4,0},{8,12},{12,8},{16,20},{20,16},{24,28},{28,24},{1,5},{5... | collective-permute-start | bytes 4718600 | tf_op jit(solution)/shard_map/ppermute | solution.py:27
  735.1 28.0 %collective-permute-start.69 = (f32[256,2048]{1,0:T(8,128)}, f32[256,2048]{1,0:T(8,128)}, u32[]{:S(2)}, u32[]{:S(2)}) collective-permute-start(f32[256,2048]{1,0:T(8,128)} %constant_dynamic-update-slice_fusion.8), channel_id=1, source_target_pairs={{0,4},{4,0},{8,12},{12,8},{16,20},{20,16},{24,28},{28,24},{1,5},{5... | collective-permute-start | bytes 6291464 | tf_op jit(solution)/shard_map/ppermute | solution.py:27
  (206 other events, 2000.1 us)
Sparse Core Ops, SparseCore 0:
  334.6 125.6 all-reduce.27
  608.5 146.2 all-reduce.25

commit v5 on v3

--- a/solution.py
+++ b/solution.py
@@ -882,7 +882,9 @@
         arrived = tuple(grad)
         grad = after(grad, *last)
         if group == 0:
-            grad, expert_one = lax.optimization_barrier((grad, expert_one))
+            grad, expert_one = lax.optimization_barrier((dense.step(grad), expert_one))
+        if group == 1:
+            grad = dense.step(grad)
         (hidden, extra), saved, fixed = kept_first[group]
         new, grad_logits, normed, active, grad_result, grad_pre, sums = expert_call(
             backward_kernel,
@@ -896,9 +898,9 @@
             2,
         )
         if group == 0:
-            new = dense.step(new)
+            new = dense.step(new, over_dp - 2)
         if group == 1:
-            new = dense.step(new, over_dp - 2)
+            new = dense.step(new, over_ep - 1)
         last = (new,)
         sources.append((new, grad_logits[:, : experts + (-experts % 8)].T))
         kept.append((normed, active, grad_result, grad_pre))
@@ -906,7 +908,7 @@
     sums, router_zero = add_up(small)
     gain_zero, shift_zero = sums[0], sums[1]
     expert_zero = lax.psum(expert_weight_grads(kept), "dp")
-    sources = dense.step(sources, 2 * over_ep + 1)
+    sources = dense.step(sources, over_ep + 1)
     frame_messages = layout.expert_to_home(sources)
     wholes = [lax.pad(one[None], 0.0, ((1, 0, 0), (0, 0, 0), (0, 0, 0))) for one in expert_one]
     frame_messages, wholes = dense.step((frame_messages, wholes), over_dp - 1)

time: 771 us -> 761 us (0.987)
    ppermute x49, waiting for transfers between devices: 146 us -> 127 us  [swap(): return lax.ppermute(values, axis, [(i, i ^ bit) for i in range(count)])]
    psum x1, waiting for transfers between devices: 0.01 us -> 15.4 us  [body(): expert_zero = lax.psum(expert_weight_grads(kept), 'dp')]
    unnamed x381 -> x379, local copies, waits for them, and re-layouts: 24.8 us -> 23.9 us
  transfers between devices with their start and end apart: 69 -> 69, of which waited for: 21 -> 23; matrix products, arithmetic and copies ran while one was open for 32% -> 31% of each run, Pallas kernels for 21% -> 22%
where the time goes in v5:
time: 761 us; the launch traced here: 752 us
  Pallas kernels  163 us (21%)
  local copies, waits for them, and re-layouts  154 us (20%)
  waiting for transfers between devices  151 us (20%)
  starting transfers between devices  132 us (17%)
  other arithmetic  79.8 us (10%)
  matrix products  55 us (7%)
  between operations  17.6 us (2%)
    ppermute x49, waiting for transfers between devices, swap(): return lax.ppermute(values, axis, [(i, i ^ bit) for i in range(count)])  127 us
    pallas_call x6, Pallas kernels, expert_call(): pl.pallas_call(functools.partial(kernel, experts), grid=(rows // block,),...  87.8 us
    ppermute x49, starting transfers between devices, swap(): return lax.ppermute(values, axis, [(i, i ^ bit) for i in range(count)])  75.1 us
    dot_general x20, matrix products, product(): return jnp.matmul(left, right, precision=HIGH)  36.7 us
    ppermute x8, starting transfers between devices, home_to_expert(): got.append(lax.ppermute(message, ('dp', 'ep'), self.route(group, u, False)))  36.1 us
    pallas_call x2, Pallas kernels, expert_weight_grads(): pl.pallas_call(functools.partial(weight_kernel, count), grid=(inner // wi...  35.2 us
    pallas_call x1, Pallas kernels, attend_back(): pl.pallas_call(functools.partial(attend_back_kernel, chunk, (width // slo...  26.4 us
    unnamed x379, local copies, waits for them, and re-layouts  23.9 us
  transfers between devices with their start and end apart: 69, of which 23 were waited for; matrix products, arithmetic and copies ran while one was open for 31% of the time, Pallas kernels for 22%

profile of v5, /device:TPU:0, one launch (start us, length us, event | category | flops | bytes accessed | tf_op | source)
XLA Modules:
  0.0 752.4 jit_solution(8257682851836755832)
XLA Ops:
  15.8 5.8 collective-permute-start.2
  23.3 5.0 collective-permute-start.1
  40.4 7.1 collective-permute-start.5
  47.4 5.3 collective-permute-start.6
  58.4 9.4 %forward.2 = (f32[512,512]{1,0:T(8,128)S(1)}, f32[512,512]{1,0:T(8,128)S(1)}, f32[512,2048]{1,0:T(8,128)}) custom-call(f32[512,512]{1,0:T(8,128)S(1)} %pad_maximum_fusion.8.hidden, f32[512,128]{1,0:T(8,128)S(1)} %pad.87.extra, f32[1,128]{1,0:T(1,128)S(1)} %compare_convert_fusion.2.own, f32[2,512]{1,0:T(2,128)S(1)} %get-tuple-element.497.norm, ...), custom_call_target="tpu_custom_call" | custom-call | flops 1 | bytes 1 | tf_op jit(solution)/shard_map/forward/pallas_call | solution.py:406
  72.7 10.0 %forward.3 = (f32[512,512]{1,0:T(8,128)S(1)}, f32[512,512]{1,0:T(8,128)S(1)}, f32[512,2048]{1,0:T(8,128)}) custom-call(f32[512,512]{1,0:T(8,128)S(1)} %pad_maximum_fusion.9.hidden, f32[512,128]{1,0:T(8,128)S(1)} %pad.91.extra, f32[1,128]{1,0:T(1,128)S(1)} %compare_convert_fusion.2.own, f32[2,512]{1,0:T(2,128)S(1)} %get-tuple-element.497.norm, ...), custom_call_target="tpu_custom_call" | custom-call | flops 1 | bytes 1 | tf_op jit(solution)/shard_map/forward/pallas_call | solution.py:406
  82.8 18.3 %collective-permute-start.7 = (f32[256,512]{1,0:T(8,128)S(1)}, f32[256,512]{1,0:T(8,128)S(1)}, u32[]{:S(2)}, u32[]{:S(2)}) collective-permute-start(f32[256,512]{1,0:T(8,128)S(1)} %get-tuple-element.363), channel_id=1, source_target_pairs={{0,1},{1,0},{2,3},{3,2},{4,5},{5,4},{6,7},{7,6},{8,9},{9,8},{10,11... | collective-permute-start | bytes 1572872 | tf_op jit(solution)/shard_map/ppermute | solution.py:27
  104.9 18.6 %collective-permute-done.7 = f32[256,512]{1,0:T(8,128)S(1)} collective-permute-done((f32[256,512]{1,0:T(8,128)S(1)}, f32[256,512]{1,0:T(8,128)S(1)}, u32[]{:S(2)}, u32[]{:S(2)}) %collective-permute-start.7) | collective-permute-done | bytes 524320 | tf_op jit(solution)/shard_map/ppermute | solution.py:27
  132.4 5.8 collective-permute-start.16
  144.7 8.6 %collective-permute-done.17 = f32[264,512]{1,0:T(8,128)} collective-permute-done((f32[264,512]{1,0:T(8,128)}, f32[264,512]{1,0:T(8,128)}, u32[]{:S(2)}, u32[]{:S(2)}) %collective-permute-start.17) | collective-permute-done | bytes 540704 | tf_op jit(solution)/shard_map/ppermute | solution.py:140
  153.3 5.6 collective-permute-start.20
  158.9 6.4 collective-permute-start.21
  172.0 13.5 %attend.1 = (f32[512,512]{1,0:T(8,128)S(1)}, f32[4,8,512]{2,1,0:T(8,128)S(1)}) custom-call(f32[8]{0:T(128)S(1)} %copy-done.33, f32[1024,512]{1,0:T(8,128)S(1)} %convert_select_fusion.dist, f32[512,1536]{1,0:T(8,128)S(1)} %copy-done.6, f32[1024,1024]{1,0:T(8,128)S(1)} %pad_maximum_fusion.k_ref.v_ref, f32[1024,1024]{1,0:T(8,128)S(1)} %pad_maximum_fusion.k_ref.v_ref), custom_call_target="tpu_custom_call" | custom-call | flops 1 | bytes 1 | tf_op jit(solution)/shard_map/attend/pallas_call | solution.py:618
  226.0 18.2 %collective-permute-done.15 = f32[256,512]{1,0:T(8,128)S(1)} collective-permute-done((f32[256,512]{1,0:T(8,128)S(1)}, f32[256,512]{1,0:T(8,128)S(1)}, u32[]{:S(2)}, u32[]{:S(2)}) %collective-permute-start.15) | collective-permute-done | bytes 524320 | tf_op jit(solution)/shard_map/ppermute | solution.py:27
  247.0 19.8 %both.2 = (f32[512,512]{1,0:T(8,128)S(1)}, f32[512,512]{1,0:T(8,128)S(1)}, f32[512,128]{1,0:T(8,128)S(1)}, f32[512,512]{1,0:T(8,128)S(1)}, f32[512,2048]{1,0:T(8...) custom-call(f32[512,512]{1,0:T(8,128)S(1)} %pad_maximum_fusion.10.hidden, ...), custom_call_target="tpu_custom_call" | custom-call | flops 1 | bytes 1 | tf_op jit(solution)/shard_map/both/pallas_call | solution.py:406
  278.8 19.5 %both.3 = (f32[512,512]{1,0:T(8,128)S(1)}, f32[512,512]{1,0:T(8,128)S(1)}, f32[512,128]{1,0:T(8,128)S(1)}, f32[512,512]{1,0:T(8,128)S(1)}, f32[512,2048]{1,0:T(8...) custom-call(f32[512,512]{1,0:T(8,128)S(1)} %pad_maximum_fusion.12.hidden, ...), custom_call_target="tpu_custom_call" | custom-call | flops 1 | bytes 1 | tf_op jit(solution)/shard_map/both/pallas_call | solution.py:406
  302.0 17.7 %weights.2 = (f32[512,2048]{1,0:T(8,128)}, f32[2048,512]{1,0:T(8,128)}) custom-call(f32[512,512]{1,0:T(8,128)S(1)} %copy-done.21, f32[512,512]{1,0:T(8,128)S(1)} %get-tuple-element.165.refs_1_, f32[512,512]{1,0:T(8,128)S(1)} %copy-done.37, f32[512,512]{1,0:T(8,128)S(1)} %get-tuple-element.167.refs_3_, f32[512,2048]{1,0:T(8,128)} %get-tuple-element.168.refs_4_, ...), custom_call_target="tpu_custom_call" | custom-call | flops 12884901888 | bytes 33554432 | tf_op jit(solution)/shard_map/weights/pallas_call | solution.py:447
  319.8 4.8 collective-permute-done.24
  345.5 8.5 %multiply_reduce_fusion = (f32[512]{0:T(512)}, f32[512]{0:T(512)}, f32[512]{0:T(512)}, f32[512]{0:T(512)}, f32[512]{0:T(512)}, /*index=5*/f32[512]{0:T(512)}, f32[512]{0:T(512)}, f32[512]{0:T(512)}, f32[512,512]{1,0:T(8,128)S(1)}) fusion(f32[7,512]{1,0:T(8,128)S(1)} %get-tuple-element.461, f32[512,512]{1,0:T(8,128)} %copy-done.49, ...), kind=kLoop, calls=%fused_computation.204 | loop fusion | flops 8122368 | bytes 4237316 | tf_op jit(solution)/shard_map/reduce_sum | solution.py:843
  355.2 5.9 collective-permute-start.29
  365.1 10.7 %fusion.58 = (f32[512,512]{1,0:T(8,128)S(1)}, f32[512,512]{1,0:T(8,128)S(1)}) fusion(f32[512,1024]{1,0:T(8,128)} %copy-done.45, f32[512]{0:T(512)S(1)} %copy-done.100, f32[512,512]{1,0:T(8,128)} %copy-done.54, f32[7,512]{1,0:T(8,128)S(1)} %get-tuple-element.443, f32[512]{0:T(512)} %bitcast.305, f32[512]{0:T(512)} %bitcast.307, f32[512]{0:T(512)} %bitcast.281, ...), kind=kLoop, calls=%fused_computation.124 | loop fusion | flops 13369344 | bytes 5304320 | tf_op jit(solution)/shard_map/transpose(jvp())/mul | solution.py:768
  390.2 26.4 %attend_back.1 = (f32[512,512]{1,0:T(8,128)S(1)}, f32[2,1024,512]{2,1,0:T(8,128)S(1)}, f32[4,8,512]{2,1,0:T(8,128)S(1)}) custom-call(f32[8]{0:T(128)S(1)} %copy-done.33, f32[1024,512]{1,0:T(8,128)S(1)} %copy-done.9, f32[512,1536]{1,0:T(8,128)S(1)} %copy-done.7, f32[1024,1024]{1,0:T(8,128)} %copy-done.2, f32[1024,1024]{1,0:T(8,128)} %copy-done.2, ...), custom_call_target="tpu_custom_call" | custom-call | flops 1 | bytes 1 | tf_op jit(solution)/shard_map/attend_back/pallas_call | solution.py:644
  429.0 5.4 multiply_reduce_fusion.8
  471.0 23.3 %collective-permute-done.35 = f32[256,512]{1,0:T(8,128)S(1)} collective-permute-done((f32[256,512]{1,0:T(8,128)S(1)}, f32[256,512]{1,0:T(8,128)S(1)}, u32[]{:S(2)}, u32[]{:S(2)}) %collective-permute-start.35) | collective-permute-done | bytes 524320 | tf_op jit(solution)/shard_map/ppermute | solution.py:27
  504.4 14.3 %backward.2 = (f32[512,512]{1,0:T(8,128)S(1)}, f32[512,128]{1,0:T(8,128)S(1)}, f32[512,512]{1,0:T(8,128)S(1)}, f32[512,2048]{1,0:T(8,128)}, f32[512,512]{1,0:T(8...) custom-call(f32[512,512]{1,0:T(8,128)S(1)} %copy-done.13, f32[512,128]{1,0:T(8,128)S(1)} %copy-done.17, ...), custom_call_target="tpu_custom_call" | custom-call | flops 1 | bytes 1 | tf_op jit(solution)/shard_map/backward/pallas_call | solution.py:406
  545.6 14.7 %backward.3 = (f32[512,512]{1,0:T(8,128)S(1)}, f32[512,128]{1,0:T(8,128)S(1)}, f32[512,512]{1,0:T(8,128)S(1)}, f32[512,2048]{1,0:T(8,128)}, f32[512,512]{1,0:T(8...) custom-call(f32[512,512]{1,0:T(8,128)S(1)} %copy-done.11, f32[512,128]{1,0:T(8,128)S(1)} %pad.91.extra, ...), custom_call_target="tpu_custom_call" | custom-call | flops 1 | bytes 1 | tf_op jit(solution)/shard_map/backward/pallas_call | solution.py:406
  560.3 17.6 %weights.3 = (f32[512,2048]{1,0:T(8,128)}, f32[2048,512]{1,0:T(8,128)}) custom-call(f32[512,512]{1,0:T(8,128)S(1)} %get-tuple-element.213.refs_0_, f32[512,512]{1,0:T(8,128)S(1)} %get-tuple-element.214.refs_1_, f32[512,512]{1,0:T(8,128)S(1)} %copy-done.35, f32[512,512]{1,0:T(8,128)S(1)} %get-tuple-element.225.refs_3_, ...), custom_call_target="tpu_custom_call" | custom-call | flops 12884901888 | bytes 33554432 | tf_op jit(solution)/shard_map/weights/pallas_call | solution.py:447
  596.0 9.4 %collective-permute-done.51 = f32[32,1536]{1,0:T(8,128)S(1)} collective-permute-done((f32[32,1536]{1,0:T(8,128)S(1)}, f32[32,1536]{1,0:T(8,128)S(1)}, u32[]{:S(2)}, u32[]{:S(2)}) %collective-permute-start.51) | collective-permute-done | bytes 196640 | tf_op jit(solution)/shard_map/ppermute | solution.py:27
  636.4 20.5 %collective-permute-done.59 = f32[128,1536]{1,0:T(8,128)S(1)} collective-permute-done((f32[128,1536]{1,0:T(8,128)}, f32[128,1536]{1,0:T(8,128)S(1)}, u32[]{:S(2)}, u32[]{:S(2)}) %collective-permute-start.59) | collective-permute-done | bytes 786464 | tf_op jit(solution)/shard_map/ppermute | solution.py:27
  685.2 8.3 %collective-permute-start.62 = (f32[36,512]{1,0:T(8,128)S(1)}, f32[36,512]{1,0:T(8,128)S(1)}, u32[]{:S(2)}, u32[]{:S(2)}) collective-permute-start(f32[36,512]{1,0:T(8,128)S(1)} %concatenate.252), channel_id=1, source_target_pairs={{0,1},{1,0},{2,3},{3,2},{4,5},{5,4},{6,7},{7,6},{8,9},{9,8},{10,11... | collective-permute-start | bytes 221192 | tf_op jit(solution)/shard_map/ppermute | solution.py:27
  708.1 15.4 %all-reduce.30.cloned.1.call-done = (f32[1,1,512,2048]{3,2,1,0:T(8,128)}, f32[1,1,2048,512]{3,2,1,0:T(8,128)}) async-done(((f32[1,1,512,2048]{3,2,1,0:T(8,128)}, f32[1,1,2048,512]{3,2,1,0:T(8,128)}), (f32[1,1,512,2048]{3,2,1,0:T(8,128)}, f32[1,1,2048,512]{3,2,1,0:T(8,128)})) %all-reduce.30.cloned.1.call-update) | async-done | bytes 8388624 | tf_op jit(solution)/shard_map/psum | solution.py:910
  723.6 4.8 bitcast_dynamic-update-slice_fusion
  (807 shorter events, 350.3 us)
Async XLA Ops:
  7.2 497.1 %all-reduce.32.cloned.1.call-start = ((), (), s32[]{:S(2)}) async-start(), calls=%async_computation.1 | async-start | bytes 16777216 | tf_op jit(solution)/shard_map/psum | solution.py:815
  15.8 24.6 %collective-permute-start.2 = (f32[264,512]{1,0:T(8,128)}, f32[264,512]{1,0:T(8,128)}, u32[]{:S(2)}, u32[]{:S(2)}) collective-permute-start(f32[264,512]{1,0:T(8,128)} %pad_maximum_fusion.16), channel_id=1, source_target_pairs={{0,0},{1,2},{2,4},{3,6},{4,1},{5,3},{6,5},{7,7},{8,8},{9,10},{10,1... | collective-permute-start | bytes 1622024 | tf_op jit(solution)/shard_map/ppermute | solution.py:140
  40.4 28.4 %collective-permute-start.5 = (f32[264,512]{1,0:T(8,128)}, f32[264,512]{1,0:T(8,128)}, u32[]{:S(2)}, u32[]{:S(2)}) collective-permute-start(f32[264,512]{1,0:T(8,128)} %get-tuple-element.125), channel_id=1, source_target_pairs={{0,1},{1,3},{2,5},{3,7},{4,0},{5,2},{6,4},{7,6},{8,9},{9,11},{10,1... | collective-permute-start | bytes 1622024 | tf_op jit(solution)/shard_map/ppermute | solution.py:140
  68.8 36.1 %collective-permute-start.4 = (f32[256,512]{1,0:T(8,128)S(1)}, f32[256,512]{1,0:T(8,128)}, u32[]{:S(2)}, u32[]{:S(2)}) collective-permute-start(f32[256,512]{1,0:T(8,128)S(1)} %get-tuple-element.362), channel_id=1, source_target_pairs={{0,2},{1,3},{2,0},{3,1},{4,6},{5,7},{6,4},{7,5},{8,10},{9,11},{10,... | collective-permute-start | bytes 1572872 | tf_op jit(solution)/shard_map/ppermute | solution.py:27
  82.8 40.7 %collective-permute-start.7 = (f32[256,512]{1,0:T(8,128)S(1)}, f32[256,512]{1,0:T(8,128)S(1)}, u32[]{:S(2)}, u32[]{:S(2)}) collective-permute-start(f32[256,512]{1,0:T(8,128)S(1)} %get-tuple-element.363), channel_id=1, source_target_pairs={{0,1},{1,0},{2,3},{3,2},{4,5},{5,4},{6,7},{7,6},{8,9},{9,8},{10,11... | collective-permute-start | bytes 1572872 | tf_op jit(solution)/shard_map/ppermute | solution.py:27
  131.3 37.5 %collective-permute-start.9 = (f32[512,1024]{1,0:T(8,128)}, f32[512,1024]{1,0:T(8,128)}, u32[]{:S(2)}, u32[]{:S(2)}) collective-permute-start(f32[512,1024]{1,0:T(8,128)} %slice_bitcast_fusion), channel_id=1, source_target_pairs={{0,4},{4,0},{8,12},{12,8},{16,20},{20,16},{24,28},{28,24},{1,5},{5... | collective-permute-start | bytes 6291464 | tf_op jit(solution)/shard_map/ppermute | solution.py:27
  153.3 47.3 %collective-permute-start.20 = (f32[264,512]{1,0:T(8,128)}, f32[264,512]{1,0:T(8,128)}, u32[]{:S(2)}, u32[]{:S(2)}) collective-permute-start(f32[264,512]{1,0:T(8,128)} %select_maximum_fusion.1), channel_id=1, source_target_pairs={{0,1},{1,3},{2,5},{3,7},{4,0},{5,2},{6,4},{7,6},{8,9},{9,11},{10,1... | collective-permute-start | bytes 1622024 | tf_op jit(solution)/shard_map/ppermute | solution.py:140
  158.9 46.0 %collective-permute-start.21 = (f32[264,512]{1,0:T(8,128)}, f32[264,512]{1,0:T(8,128)}, u32[]{:S(2)}, u32[]{:S(2)}) collective-permute-start(f32[264,512]{1,0:T(8,128)} %select_maximum_fusion), channel_id=1, source_target_pairs={{0,3},{1,1},{2,7},{3,5},{4,2},{5,0},{6,6},{7,4},{8,11},{9,9},{10,1... | collective-permute-start | bytes 1622024 | tf_op jit(solution)/shard_map/ppermute | solution.py:140
  220.5 23.7 %collective-permute-start.15 = (f32[256,512]{1,0:T(8,128)S(1)}, f32[256,512]{1,0:T(8,128)S(1)}, u32[]{:S(2)}, u32[]{:S(2)}) collective-permute-start(f32[256,512]{1,0:T(8,128)S(1)} %get-tuple-element.359), channel_id=1, source_target_pairs={{0,2},{1,3},{2,0},{3,1},{4,6},{5,7},{6,4},{7,5},{8,10},{9,11},{10,... | collective-permute-start | bytes 1572872 | tf_op jit(solution)/shard_map/ppermute | solution.py:27
  245.3 30.9 %collective-permute-start.18 = (f32[256,512]{1,0:T(8,128)}, f32[256,512]{1,0:T(8,128)}, u32[]{:S(2)}, u32[]{:S(2)}) collective-permute-start(f32[256,512]{1,0:T(8,128)} %get-tuple-element.358), channel_id=1, source_target_pairs={{0,1},{1,0},{2,3},{3,2},{4,5},{5,4},{6,7},{7,6},{8,9},{9,8},{10,11... | collective-permute-start | bytes 1572872 | tf_op jit(solution)/shard_map/ppermute | solution.py:27
  245.3 30.9 %collective-permute-start.19 = (f32[256,512]{1,0:T(8,128)}, f32[256,512]{1,0:T(8,128)}, u32[]{:S(2)}, u32[]{:S(2)}) collective-permute-start(f32[256,512]{1,0:T(8,128)} %get-tuple-element.357), channel_id=1, source_target_pairs={{0,3},{1,2},{2,1},{3,0},{4,7},{5,6},{6,5},{7,4},{8,11},{9,10},{10,... | collective-permute-start | bytes 1572872 | tf_op jit(solution)/shard_map/ppermute | solution.py:27
  270.8 31.2 %collective-permute-start.22 = (f32[256,512]{1,0:T(8,128)}, f32[256,512]{1,0:T(8,128)}, u32[]{:S(2)}, u32[]{:S(2)}) collective-permute-start(f32[256,512]{1,0:T(8,128)} %get-tuple-element.354), channel_id=1, source_target_pairs={{0,2},{1,3},{2,0},{3,1},{4,6},{5,7},{6,4},{7,5},{8,10},{9,11},{10,... | collective-permute-start | bytes 1572872 | tf_op jit(solution)/shard_map/ppermute | solution.py:27
  300.4 24.2 %collective-permute-start.24 = (f32[256,512]{1,0:T(8,128)S(1)}, f32[256,512]{1,0:T(8,128)S(1)}, u32[]{:S(2)}, u32[]{:S(2)}) collective-permute-start(f32[256,512]{1,0:T(8,128)S(1)} %get-tuple-element.356), channel_id=1, source_target_pairs={{0,3},{1,2},{2,1},{3,0},{4,7},{5,6},{6,5},{7,4},{8,11},{9,10},{10,... | collective-permute-start | bytes 1572872 | tf_op jit(solution)/shard_map/ppermute | solution.py:27
  336.8 386.7 %all-reduce.30.cloned.1.call-start = ((), (), s32[]{:S(2)}) async-start(), calls=%async_computation | async-start | bytes 16777216 | tf_op jit(solution)/shard_map/psum | solution.py:910
  355.2 87.4 %collective-permute-start.29 = (f32[264,512]{1,0:T(8,128)}, f32[264,512]{1,0:T(8,128)}, u32[]{:S(2)}, u32[]{:S(2)}) collective-permute-start(f32[264,512]{1,0:T(8,128)} %pad_maximum_fusion.18), channel_id=1, source_target_pairs={{0,0},{2,1},{4,2},{6,3},{1,4},{3,5},{5,6},{7,7},{8,8},{10,9},{12,1... | collective-permute-start | bytes 1622024 | tf_op jit(solution)/shard_map/ppermute | solution.py:167
  361.9 82.4 %collective-permute-start.30 = (f32[264,512]{1,0:T(8,128)}, f32[264,512]{1,0:T(8,128)}, u32[]{:S(2)}, u32[]{:S(2)}) collective-permute-start(f32[264,512]{1,0:T(8,128)} %pad_maximum_fusion.19), channel_id=1, source_target_pairs={{2,0},{0,1},{6,2},{4,3},{3,4},{1,5},{7,6},{5,7},{10,8},{8,9},{14,1... | collective-permute-start | bytes 1622024 | tf_op jit(solution)/shard_map/ppermute | solution.py:167
  420.2 26.3 %collective-permute-start.34 = (f32[2,512,512]{2,1,0:T(8,128)}, f32[2,512,512]{2,1,0:T(8,128)}, u32[]{:S(2)}, u32[]{:S(2)}) collective-permute-start(f32[2,512,512]{2,1,0:T(8,128)} %slice.958), channel_id=1, source_target_pairs={{0,4},{4,0},{8,12},{12,8},{16,20},{20,16},{24,28},{28,24},{1,5},{5... | collective-permute-start | bytes 6291464 | tf_op jit(solution)/shard_map/ppermute | solution.py:27
  421.9 23.1 %collective-permute-start.31 = (f32[264,512]{1,0:T(8,128)}, f32[264,512]{1,0:T(8,128)}, u32[]{:S(2)}, u32[]{:S(2)}) collective-permute-start(f32[264,512]{1,0:T(8,128)} %pad_maximum_fusion.20), channel_id=1, source_target_pairs={{1,0},{3,1},{5,2},{7,3},{0,4},{2,5},{4,6},{6,7},{9,8},{11,9},{13,1... | collective-permute-start | bytes 1622024 | tf_op jit(solution)/shard_map/ppermute | solution.py:167
  442.5 25.8 %collective-permute-start.37 = (f32[256,1536]{1,0:T(8,128)}, f32[256,1536]{1,0:T(8,128)}, u32[]{:S(2)}, u32[]{:S(2)}) collective-permute-start(f32[256,1536]{1,0:T(8,128)} %fusion.47), channel_id=1, source_target_pairs={{0,4},{4,0},{8,12},{12,8},{16,20},{20,16},{24,28},{28,24},{1,5},{5... | collective-permute-start | bytes 4718600 | tf_op jit(solution)/shard_map/ppermute | solution.py:27
  455.6 38.7 %collective-permute-start.36 = (f32[256,2048]{1,0:T(8,128)}, f32[256,2048]{1,0:T(8,128)}, u32[]{:S(2)}, u32[]{:S(2)}) collective-permute-start(f32[256,2048]{1,0:T(8,128)} %fusion.2), channel_id=1, source_target_pairs={{0,4},{4,0},{8,12},{12,8},{16,20},{20,16},{24,28},{28,24},{1,5},{5... | collective-permute-start | bytes 6291464 | tf_op jit(solution)/shard_map/ppermute | solution.py:27
  468.1 26.2 %collective-permute-start.35 = (f32[256,512]{1,0:T(8,128)S(1)}, f32[256,512]{1,0:T(8,128)S(1)}, u32[]{:S(2)}, u32[]{:S(2)}) collective-permute-start(f32[256,512]{1,0:T(8,128)S(1)} %get-tuple-element.343), channel_id=1, source_target_pairs={{0,2},{1,3},{2,0},{3,1},{4,6},{5,7},{6,4},{7,5},{8,10},{9,11},{10,... | collective-permute-start | bytes 1572872 | tf_op jit(solution)/shard_map/ppermute | solution.py:27
  497.5 23.4 %collective-permute-start.39 = (f32[128,1536]{1,0:T(8,128)}, f32[128,1536]{1,0:T(8,128)}, u32[]{:S(2)}, u32[]{:S(2)}) collective-permute-start(f32[128,1536]{1,0:T(8,128)} %constant_dynamic-slice_fusion.6), channel_id=1, source_target_pairs={{0,16},{4,20},{8,24},{12,28},{16,0},{20,4},{24,8},{28,12},{1,17},{... | collective-permute-start | bytes 2359304 | tf_op jit(solution)/shard_map/ppermute | solution.py:27
  500.0 25.1 %collective-permute-start.38 = (f32[128,2048]{1,0:T(8,128)}, f32[128,2048]{1,0:T(8,128)}, u32[]{:S(2)}, u32[]{:S(2)}) collective-permute-start(f32[128,2048]{1,0:T(8,128)} %constant_dynamic-slice_fusion.7), channel_id=1, source_target_pairs={{0,8},{4,12},{8,0},{12,4},{16,24},{20,28},{24,16},{28,20},{1,9},{5... | collective-permute-start | bytes 3145736 | tf_op jit(solution)/shard_map/ppermute | solution.py:27
  503.1 34.4 %collective-permute-start.40 = (f32[256,512]{1,0:T(8,128)}, f32[256,512]{1,0:T(8,128)}, u32[]{:S(2)}, u32[]{:S(2)}) collective-permute-start(f32[256,512]{1,0:T(8,128)} %get-tuple-element.342), channel_id=1, source_target_pairs={{0,1},{1,0},{2,3},{3,2},{4,5},{5,4},{6,7},{7,6},{8,9},{9,8},{10,11... | collective-permute-start | bytes 1572872 | tf_op jit(solution)/shard_map/ppermute | solution.py:27
  503.1 34.4 %collective-permute-start.41 = (f32[256,512]{1,0:T(8,128)}, f32[256,512]{1,0:T(8,128)}, u32[]{:S(2)}, u32[]{:S(2)}) collective-permute-start(f32[256,512]{1,0:T(8,128)} %get-tuple-element.341), channel_id=1, source_target_pairs={{0,3},{1,2},{2,1},{3,0},{4,7},{5,6},{6,5},{7,4},{8,11},{9,10},{10,... | collective-permute-start | bytes 1572872 | tf_op jit(solution)/shard_map/ppermute | solution.py:27
  540.5 37.4 %collective-permute-start.45 = (f32[32,1536]{1,0:T(8,128)S(1)}, f32[32,1536]{1,0:T(8,128)}, u32[]{:S(2)}, u32[]{:S(2)}) collective-permute-start(f32[32,1536]{1,0:T(8,128)S(1)} %constant_dynamic-slice_fusion.2), channel_id=1, source_target_pairs={{0,2},{1,3},{2,0},{3,1},{4,6},{5,7},{6,4},{7,5},{8,10},{9,11},{10,... | collective-permute-start | bytes 589832 | tf_op jit(solution)/shard_map/ppermute | solution.py:27
  541.4 37.7 %collective-permute-start.44 = (f32[32,2048]{1,0:T(8,128)}, f32[32,2048]{1,0:T(8,128)}, u32[]{:S(2)}, u32[]{:S(2)}) collective-permute-start(f32[32,2048]{1,0:T(8,128)} %constant_dynamic-slice_fusion.3), channel_id=1, source_target_pairs={{0,2},{1,3},{2,0},{3,1},{4,6},{5,7},{6,4},{7,5},{8,10},{9,11},{10,... | collective-permute-start | bytes 786440 | tf_op jit(solution)/shard_map/ppermute | solution.py:27
  618.2 48.4 %collective-permute-start.55 = (f32[264,512]{1,0:T(8,128)}, f32[264,512]{1,0:T(8,128)}, u32[]{:S(2)}, u32[]{:S(2)}) collective-permute-start(f32[264,512]{1,0:T(8,128)} %pad_maximum_fusion.25), channel_id=1, source_target_pairs={{3,0},{1,1},{7,2},{5,3},{2,4},{0,5},{6,6},{4,7},{11,8},{9,9},{15,1... | collective-permute-start | bytes 1622024 | tf_op jit(solution)/shard_map/ppermute | solution.py:167
  622.1 44.5 %collective-permute-start.54 = (f32[264,512]{1,0:T(8,128)S(1)}, f32[264,512]{1,0:T(8,128)S(1)}, u32[]{:S(2)}, u32[]{:S(2)}) collective-permute-start(f32[264,512]{1,0:T(8,128)S(1)} %pad_maximum_fusion.24), channel_id=1, source_target_pairs={{1,0},{3,1},{5,2},{7,3},{0,4},{2,5},{4,6},{6,7},{9,8},{11,9},{13,1... | collective-permute-start | bytes 1622024 | tf_op jit(solution)/shard_map/ppermute | solution.py:167
  626.9 29.9 %collective-permute-start.59 = (f32[128,1536]{1,0:T(8,128)}, f32[128,1536]{1,0:T(8,128)S(1)}, u32[]{:S(2)}, u32[]{:S(2)}) collective-permute-start(f32[128,1536]{1,0:T(8,128)} %constant_dynamic-update-slice_fusion.6), channel_id=1, source_target_pairs={{0,16},{4,20},{8,24},{12,28},{16,0},{20,4},{24,8},{28,12},{1,17},{... | collective-permute-start | bytes 2359304 | tf_op jit(solution)/shard_map/ppermute | solution.py:27
  630.3 35.2 %collective-permute-start.57 = (f32[128,2048]{1,0:T(8,128)}, f32[128,2048]{1,0:T(8,128)S(1)}, u32[]{:S(2)}, u32[]{:S(2)}) collective-permute-start(f32[128,2048]{1,0:T(8,128)} %constant_dynamic-update-slice_fusion.10), channel_id=1, source_target_pairs={{0,8},{4,12},{8,0},{12,4},{16,24},{20,28},{24,16},{28,20},{1,9},{5... | collective-permute-start | bytes 3145736 | tf_op jit(solution)/shard_map/ppermute | solution.py:27
  631.4 35.2 %collective-permute-start.53 = (f32[264,512]{1,0:T(8,128)S(1)}, f32[264,512]{1,0:T(8,128)S(1)}, u32[]{:S(2)}, u32[]{:S(2)}) collective-permute-start(f32[264,512]{1,0:T(8,128)S(1)} %pad_maximum_fusion.23), channel_id=1, source_target_pairs={{2,0},{0,1},{6,2},{4,3},{3,4},{1,5},{7,6},{5,7},{10,8},{8,9},{14,1... | collective-permute-start | bytes 1622024 | tf_op jit(solution)/shard_map/ppermute | solution.py:167
  (219 other events, 1707.1 us)
Sparse Core Ops, SparseCore 0:
  337.0 125.6 all-reduce.31
  578.0 145.5 all-reduce.29

commit v6 on v5

--- a/solution.py
+++ b/solution.py
@@ -917,10 +917,13 @@
     router_zero = router_zero + product(logit_zero, home_rows).T
     frames_grad = pick(home[0][1], rows_back).reshape(micro, rows, width)
     late = jnp.concatenate([gain_zero[None], shift_zero[None], router_zero.T, early], axis=0)
-    late = butterfly(dense.step(late), bits_of("ep") + bits_of("dp"))
+    one, two = dense.parts
+    pieces = [one[:, : 3 * width], one[:, 3 * width :], two[:, :width], two[:, width:]]
+    pieces = [join(piece, bits_of("dp")[0]) for piece in pieces]
+    late, pieces = lax.optimization_barrier((late, pieces))
+    packed_grad, project_grad, mixing_grad, point_grad = pieces
+    late = butterfly(late, bits_of("ep") + bits_of("dp"))
     late, early = late[: 2 + experts], late[2 + experts :]
-    packed_grad, project_grad = dense.parts[0][:, : 3 * width], dense.parts[0][:, 3 * width :]
-    mixing_grad, point_grad = dense.parts[1][:, :width], dense.parts[1][:, width:]
     expert_grads = []
     for zero, whole in zip(expert_zero, wholes):
         expert_grads.append(lax.dynamic_update_slice(whole, zero[None], (0, 0, 0))[:, None])

time: 761 us -> 754 us (level)
  local copies, waits for them, and re-layouts: 154 us -> 142 us
    ppermute x49 -> x51, starting transfers between devices: 75.1 us -> 81.1 us  [swap(): return lax.ppermute(values, axis, [(i, i ^ bit) for i in range(count)])]
    ppermute x49 -> x51, waiting for transfers between devices: 127 us -> 129 us  [swap(): return lax.ppermute(values, axis, [(i, i ^ bit) for i in range(count)])]
    unnamed x379 -> x409, local copies, waits for them, and re-layouts: 23.9 us -> 22.5 us
  transfers between devices with their start and end apart: 69 -> 71, of which waited for: 23 -> 26; matrix products, arithmetic and copies ran while one was open for 31% -> 29% of each run, Pallas kernels for 22% -> 22%
where the time goes in v6:
time: 754 us; the launch traced here: 746 us
  Pallas kernels  165 us (22%)
  waiting for transfers between devices  155 us (21%)
  local copies, waits for them, and re-layouts  142 us (19%)
  starting transfers between devices  137 us (18%)
  other arithmetic  73.8 us (10%)
  matrix products  55.3 us (7%)
  between operations  17.7 us (2%)
    ppermute x51, waiting for transfers between devices, swap(): return lax.ppermute(values, axis, [(i, i ^ bit) for i in range(count)])  129 us
    pallas_call x6, Pallas kernels, expert_call(): pl.pallas_call(functools.partial(kernel, experts), grid=(rows // block,),...  88 us
    ppermute x51, starting transfers between devices, swap(): return lax.ppermute(values, axis, [(i, i ^ bit) for i in range(count)])  81.1 us
    dot_general x20, matrix products, product(): return jnp.matmul(left, right, precision=HIGH)  36.7 us
    pallas_call x2, Pallas kernels, expert_weight_grads(): pl.pallas_call(functools.partial(weight_kernel, count), grid=(inner // wi...  35.7 us
    ppermute x8, starting transfers between devices, home_to_expert(): got.append(lax.ppermute(message, ('dp', 'ep'), self.route(group, u, False)))  35.6 us
    pallas_call x1, Pallas kernels, attend_back(): pl.pallas_call(functools.partial(attend_back_kernel, chunk, (width // slo...  27.1 us
    slice x38, local copies, waits for them, and re-layouts, piece(): lax.slice_in_dim(values, at * self.capacity, (at + count) * self.capacity...  26.4 us
  transfers between devices with their start and end apart: 71, of which 26 were waited for; matrix products, arithmetic and copies ran while one was open for 29% of the time, Pallas kernels for 22%

profile of v6, /device:TPU:0, one launch (start us, length us, event | category | flops | bytes accessed | tf_op | source)
XLA Modules:
  0.0 745.9 jit_solution(4477821576793648865)
XLA Ops:
  16.5 5.8 collective-permute-start.2
  24.0 5.0 collective-permute-start.1
  41.1 6.5 collective-permute-start.5
  47.6 5.3 collective-permute-start.6
  58.6 9.5 %forward.2 = (f32[512,512]{1,0:T(8,128)S(1)}, f32[512,512]{1,0:T(8,128)S(1)}, f32[512,2048]{1,0:T(8,128)}) custom-call(f32[512,512]{1,0:T(8,128)S(1)} %pad_maximum_fusion.8.hidden, f32[512,128]{1,0:T(8,128)S(1)} %pad.87.extra, f32[1,128]{1,0:T(1,128)S(1)} %compare_convert_fusion.2.own, f32[2,512]{1,0:T(2,128)S(1)} %get-tuple-element.509.norm, ...), custom_call_target="tpu_custom_call" | custom-call | flops 1 | bytes 1 | tf_op jit(solution)/shard_map/forward/pallas_call | solution.py:406
  73.8 9.7 %forward.3 = (f32[512,512]{1,0:T(8,128)S(1)}, f32[512,512]{1,0:T(8,128)S(1)}, f32[512,2048]{1,0:T(8,128)}) custom-call(f32[512,512]{1,0:T(8,128)S(1)} %pad_maximum_fusion.9.hidden, f32[512,128]{1,0:T(8,128)S(1)} %pad.91.extra, f32[1,128]{1,0:T(1,128)S(1)} %compare_convert_fusion.2.own, f32[2,512]{1,0:T(2,128)S(1)} %get-tuple-element.509.norm, ...), custom_call_target="tpu_custom_call" | custom-call | flops 1 | bytes 1 | tf_op jit(solution)/shard_map/forward/pallas_call | solution.py:406
  83.6 17.9 %collective-permute-start.7 = (f32[256,512]{1,0:T(8,128)S(1)}, f32[256,512]{1,0:T(8,128)S(1)}, u32[]{:S(2)}, u32[]{:S(2)}) collective-permute-start(f32[256,512]{1,0:T(8,128)S(1)} %get-tuple-element.375), channel_id=1, source_target_pairs={{0,1},{1,0},{2,3},{3,2},{4,5},{5,4},{6,7},{7,6},{8,9},{9,8},{10,11... | collective-permute-start | bytes 1572872 | tf_op jit(solution)/shard_map/ppermute | solution.py:27
  105.2 18.6 %collective-permute-done.7 = f32[256,512]{1,0:T(8,128)S(1)} collective-permute-done((f32[256,512]{1,0:T(8,128)S(1)}, f32[256,512]{1,0:T(8,128)S(1)}, u32[]{:S(2)}, u32[]{:S(2)}) %collective-permute-start.7) | collective-permute-done | bytes 524320 | tf_op jit(solution)/shard_map/ppermute | solution.py:27
  132.6 5.8 collective-permute-start.16
  144.9 8.6 %collective-permute-done.17 = f32[264,512]{1,0:T(8,128)} collective-permute-done((f32[264,512]{1,0:T(8,128)}, f32[264,512]{1,0:T(8,128)}, u32[]{:S(2)}, u32[]{:S(2)}) %collective-permute-start.17) | collective-permute-done | bytes 540704 | tf_op jit(solution)/shard_map/ppermute | solution.py:140
  153.5 5.6 collective-permute-start.20
  159.1 6.4 collective-permute-start.21
  172.2 13.9 %attend.1 = (f32[512,512]{1,0:T(8,128)S(1)}, f32[4,8,512]{2,1,0:T(8,128)S(1)}) custom-call(f32[8]{0:T(128)S(1)} %copy-done.34, f32[1024,512]{1,0:T(8,128)S(1)} %convert_select_fusion.dist, f32[512,1536]{1,0:T(8,128)S(1)} %copy-done.6, f32[1024,1024]{1,0:T(8,128)S(1)} %pad_maximum_fusion.k_ref.v_ref, f32[1024,1024]{1,0:T(8,128)S(1)} %pad_maximum_fusion.k_ref.v_ref), custom_call_target="tpu_custom_call" | custom-call | flops 1 | bytes 1 | tf_op jit(solution)/shard_map/attend/pallas_call | solution.py:618
  226.7 18.2 %collective-permute-done.15 = f32[256,512]{1,0:T(8,128)S(1)} collective-permute-done((f32[256,512]{1,0:T(8,128)S(1)}, f32[256,512]{1,0:T(8,128)S(1)}, u32[]{:S(2)}, u32[]{:S(2)}) %collective-permute-start.15) | collective-permute-done | bytes 524320 | tf_op jit(solution)/shard_map/ppermute | solution.py:27
  247.6 19.9 %both.2 = (f32[512,512]{1,0:T(8,128)S(1)}, f32[512,512]{1,0:T(8,128)S(1)}, f32[512,128]{1,0:T(8,128)S(1)}, f32[512,512]{1,0:T(8,128)S(1)}, f32[512,2048]{1,0:T(8...) custom-call(f32[512,512]{1,0:T(8,128)S(1)} %pad_maximum_fusion.10.hidden, ...), custom_call_target="tpu_custom_call" | custom-call | flops 1 | bytes 1 | tf_op jit(solution)/shard_map/both/pallas_call | solution.py:406
  279.6 19.5 %both.3 = (f32[512,512]{1,0:T(8,128)S(1)}, f32[512,512]{1,0:T(8,128)S(1)}, f32[512,128]{1,0:T(8,128)S(1)}, f32[512,512]{1,0:T(8,128)S(1)}, f32[512,2048]{1,0:T(8...) custom-call(f32[512,512]{1,0:T(8,128)S(1)} %pad_maximum_fusion.12.hidden, ...), custom_call_target="tpu_custom_call" | custom-call | flops 1 | bytes 1 | tf_op jit(solution)/shard_map/both/pallas_call | solution.py:406
  301.8 18.0 %weights.2 = (f32[512,2048]{1,0:T(8,128)}, f32[2048,512]{1,0:T(8,128)}) custom-call(f32[512,512]{1,0:T(8,128)S(1)} %copy-done.21, f32[512,512]{1,0:T(8,128)S(1)} %get-tuple-element.167.refs_1_, f32[512,512]{1,0:T(8,128)S(1)} %copy-done.38, f32[512,512]{1,0:T(8,128)S(1)} %get-tuple-element.169.refs_3_, f32[512,2048]{1,0:T(8,128)} %get-tuple-element.170.refs_4_, ...), custom_call_target="tpu_custom_call" | custom-call | flops 12884901888 | bytes 33554432 | tf_op jit(solution)/shard_map/weights/pallas_call | solution.py:447
  345.3 8.5 %multiply_reduce_fusion = (f32[512]{0:T(512)}, f32[512]{0:T(512)}, f32[512]{0:T(512)}, f32[512]{0:T(512)}, f32[512]{0:T(512)}, /*index=5*/f32[512]{0:T(512)}, f32[512]{0:T(512)}, f32[512]{0:T(512)}, f32[512,512]{1,0:T(8,128)S(1)}) fusion(f32[7,512]{1,0:T(8,128)S(1)} %get-tuple-element.473, f32[512,512]{1,0:T(8,128)} %copy-done.51, ...), kind=kLoop, calls=%fused_computation.204 | loop fusion | flops 8122368 | bytes 4237316 | tf_op jit(solution)/shard_map/reduce_sum | solution.py:843
  355.0 5.9 collective-permute-start.29
  372.1 10.9 %fusion.58 = (f32[512,512]{1,0:T(8,128)S(1)}, f32[512,512]{1,0:T(8,128)S(1)}) fusion(f32[512,1024]{1,0:T(8,128)} %copy-done.47, f32[512]{0:T(512)S(1)} %copy-done.111, f32[512,512]{1,0:T(8,128)} %copy-done.56, f32[7,512]{1,0:T(8,128)S(1)} %get-tuple-element.455, f32[512]{0:T(512)} %bitcast.305, f32[512]{0:T(512)} %bitcast.307, f32[512]{0:T(512)} %bitcast.281, ...), kind=kLoop, calls=%fused_computation.124 | loop fusion | flops 13369344 | bytes 5304320 | tf_op jit(solution)/shard_map/transpose(jvp())/mul | solution.py:768
  396.9 27.1 %attend_back.1 = (f32[512,512]{1,0:T(8,128)S(1)}, f32[2,1024,512]{2,1,0:T(8,128)S(1)}, f32[4,8,512]{2,1,0:T(8,128)S(1)}) custom-call(f32[8]{0:T(128)S(1)} %copy-done.34, f32[1024,512]{1,0:T(8,128)S(1)} %copy-done.9, f32[512,1536]{1,0:T(8,128)S(1)} %copy-done.7, f32[1024,1024]{1,0:T(8,128)} %copy-done.2, f32[1024,1024]{1,0:T(8,128)} %copy-done.2, ...), custom_call_target="tpu_custom_call" | custom-call | flops 1 | bytes 1 | tf_op jit(solution)/shard_map/attend_back/pallas_call | solution.py:644
  429.1 4.8 collective-permute-start.32
  472.4 21.7 %collective-permute-done.35 = f32[256,512]{1,0:T(8,128)S(1)} collective-permute-done((f32[256,512]{1,0:T(8,128)S(1)}, f32[256,512]{1,0:T(8,128)S(1)}, u32[]{:S(2)}, u32[]{:S(2)}) %collective-permute-start.35) | collective-permute-done | bytes 524320 | tf_op jit(solution)/shard_map/ppermute | solution.py:27
  505.6 14.5 %backward.2 = (f32[512,512]{1,0:T(8,128)S(1)}, f32[512,128]{1,0:T(8,128)S(1)}, f32[512,512]{1,0:T(8,128)S(1)}, f32[512,2048]{1,0:T(8,128)}, f32[512,512]{1,0:T(8...) custom-call(f32[512,512]{1,0:T(8,128)S(1)} %copy-done.13, f32[512,128]{1,0:T(8,128)S(1)} %copy-done.17, ...), custom_call_target="tpu_custom_call" | custom-call | flops 1 | bytes 1 | tf_op jit(solution)/shard_map/backward/pallas_call | solution.py:406
  546.0 14.9 %backward.3 = (f32[512,512]{1,0:T(8,128)S(1)}, f32[512,128]{1,0:T(8,128)S(1)}, f32[512,512]{1,0:T(8,128)S(1)}, f32[512,2048]{1,0:T(8,128)}, f32[512,512]{1,0:T(8...) custom-call(f32[512,512]{1,0:T(8,128)S(1)} %copy-done.11, f32[512,128]{1,0:T(8,128)S(1)} %pad.91.extra, ...), custom_call_target="tpu_custom_call" | custom-call | flops 1 | bytes 1 | tf_op jit(solution)/shard_map/backward/pallas_call | solution.py:406
  561.4 17.7 %weights.3 = (f32[512,2048]{1,0:T(8,128)}, f32[2048,512]{1,0:T(8,128)}) custom-call(f32[512,512]{1,0:T(8,128)S(1)} %get-tuple-element.215.refs_0_, f32[512,512]{1,0:T(8,128)S(1)} %get-tuple-element.216.refs_1_, f32[512,512]{1,0:T(8,128)S(1)} %copy-done.36, f32[512,512]{1,0:T(8,128)S(1)} %get-tuple-element.229.refs_3_, ...), custom_call_target="tpu_custom_call" | custom-call | flops 12884901888 | bytes 33554432 | tf_op jit(solution)/shard_map/weights/pallas_call | solution.py:447
  600.2 7.2 collective-permute-done.51
  621.1 6.8 collective-permute-done.58
  637.2 21.5 %collective-permute-done.59 = f32[128,1536]{1,0:T(8,128)S(1)} collective-permute-done((f32[128,1536]{1,0:T(8,128)S(1)}, f32[128,1536]{1,0:T(8,128)S(1)}, u32[]{:S(2)}, u32[]{:S(2)}) %collective-permute-start.59) | collective-permute-done | bytes 786464 | tf_op jit(solution)/shard_map/ppermute | solution.py:27
  661.2 6.5 collective-permute-done.57
  686.2 7.8 %collective-permute-start.64 = (f32[36,512]{1,0:T(8,128)S(1)}, f32[36,512]{1,0:T(8,128)S(1)}, u32[]{:S(2)}, u32[]{:S(2)}) collective-permute-start(f32[36,512]{1,0:T(8,128)S(1)} %concatenate.252), channel_id=1, source_target_pairs={{0,1},{1,0},{2,3},{3,2},{4,5},{5,4},{6,7},{7,6},{8,9},{9,8},{10,11... | collective-permute-start | bytes 221192 | tf_op jit(solution)/shard_map/ppermute | solution.py:27
  709.8 16.1 %all-reduce.30.cloned.1.call-done = (f32[1,1,512,2048]{3,2,1,0:T(8,128)}, f32[1,1,2048,512]{3,2,1,0:T(8,128)}) async-done(((f32[1,1,512,2048]{3,2,1,0:T(8,128)}, f32[1,1,2048,512]{3,2,1,0:T(8,128)}), (f32[1,1,512,2048]{3,2,1,0:T(8,128)}, f32[1,1,2048,512]{3,2,1,0:T(8,128)})) %all-reduce.30.cloned.1.call-update) | async-done | bytes 8388624 | tf_op jit(solution)/shard_map/psum | solution.py:910
  (843 shorter events, 342.1 us)
Async XLA Ops:
  7.2 498.2 %all-reduce.32.cloned.1.call-start = ((), (), s32[]{:S(2)}) async-start(), calls=%async_computation.1 | async-start | bytes 16777216 | tf_op jit(solution)/shard_map/psum | solution.py:815
  16.5 24.6 %collective-permute-start.2 = (f32[264,512]{1,0:T(8,128)}, f32[264,512]{1,0:T(8,128)}, u32[]{:S(2)}, u32[]{:S(2)}) collective-permute-start(f32[264,512]{1,0:T(8,128)} %pad_maximum_fusion.16), channel_id=1, source_target_pairs={{0,0},{1,2},{2,4},{3,6},{4,1},{5,3},{6,5},{7,7},{8,8},{9,10},{10,1... | collective-permute-start | bytes 1622024 | tf_op jit(solution)/shard_map/ppermute | solution.py:140
  41.1 28.3 %collective-permute-start.5 = (f32[264,512]{1,0:T(8,128)}, f32[264,512]{1,0:T(8,128)}, u32[]{:S(2)}, u32[]{:S(2)}) collective-permute-start(f32[264,512]{1,0:T(8,128)} %get-tuple-element.127), channel_id=1, source_target_pairs={{0,1},{1,3},{2,5},{3,7},{4,0},{5,2},{6,4},{7,6},{8,9},{9,11},{10,1... | collective-permute-start | bytes 1622024 | tf_op jit(solution)/shard_map/ppermute | solution.py:140
  69.4 35.8 %collective-permute-start.4 = (f32[256,512]{1,0:T(8,128)}, f32[256,512]{1,0:T(8,128)}, u32[]{:S(2)}, u32[]{:S(2)}) collective-permute-start(f32[256,512]{1,0:T(8,128)} %get-tuple-element.374), channel_id=1, source_target_pairs={{0,2},{1,3},{2,0},{3,1},{4,6},{5,7},{6,4},{7,5},{8,10},{9,11},{10,... | collective-permute-start | bytes 1572872 | tf_op jit(solution)/shard_map/ppermute | solution.py:27
  83.6 40.3 %collective-permute-start.7 = (f32[256,512]{1,0:T(8,128)S(1)}, f32[256,512]{1,0:T(8,128)S(1)}, u32[]{:S(2)}, u32[]{:S(2)}) collective-permute-start(f32[256,512]{1,0:T(8,128)S(1)} %get-tuple-element.375), channel_id=1, source_target_pairs={{0,1},{1,0},{2,3},{3,2},{4,5},{5,4},{6,7},{7,6},{8,9},{9,8},{10,11... | collective-permute-start | bytes 1572872 | tf_op jit(solution)/shard_map/ppermute | solution.py:27
  131.5 37.5 %collective-permute-start.9 = (f32[512,1024]{1,0:T(8,128)}, f32[512,1024]{1,0:T(8,128)}, u32[]{:S(2)}, u32[]{:S(2)}) collective-permute-start(f32[512,1024]{1,0:T(8,128)} %slice_bitcast_fusion), channel_id=1, source_target_pairs={{0,4},{4,0},{8,12},{12,8},{16,20},{20,16},{24,28},{28,24},{1,5},{5... | collective-permute-start | bytes 6291464 | tf_op jit(solution)/shard_map/ppermute | solution.py:27
  153.5 47.7 %collective-permute-start.20 = (f32[264,512]{1,0:T(8,128)}, f32[264,512]{1,0:T(8,128)}, u32[]{:S(2)}, u32[]{:S(2)}) collective-permute-start(f32[264,512]{1,0:T(8,128)} %select_maximum_fusion.1), channel_id=1, source_target_pairs={{0,1},{1,3},{2,5},{3,7},{4,0},{5,2},{6,4},{7,6},{8,9},{9,11},{10,1... | collective-permute-start | bytes 1622024 | tf_op jit(solution)/shard_map/ppermute | solution.py:140
  159.1 46.5 %collective-permute-start.21 = (f32[264,512]{1,0:T(8,128)}, f32[264,512]{1,0:T(8,128)}, u32[]{:S(2)}, u32[]{:S(2)}) collective-permute-start(f32[264,512]{1,0:T(8,128)} %select_maximum_fusion), channel_id=1, source_target_pairs={{0,3},{1,1},{2,7},{3,5},{4,2},{5,0},{6,6},{7,4},{8,11},{9,9},{10,1... | collective-permute-start | bytes 1622024 | tf_op jit(solution)/shard_map/ppermute | solution.py:140
  221.1 23.9 %collective-permute-start.15 = (f32[256,512]{1,0:T(8,128)S(1)}, f32[256,512]{1,0:T(8,128)S(1)}, u32[]{:S(2)}, u32[]{:S(2)}) collective-permute-start(f32[256,512]{1,0:T(8,128)S(1)} %get-tuple-element.371), channel_id=1, source_target_pairs={{0,2},{1,3},{2,0},{3,1},{4,6},{5,7},{6,4},{7,5},{8,10},{9,11},{10,... | collective-permute-start | bytes 1572872 | tf_op jit(solution)/shard_map/ppermute | solution.py:27
  246.0 31.0 %collective-permute-start.18 = (f32[256,512]{1,0:T(8,128)}, f32[256,512]{1,0:T(8,128)}, u32[]{:S(2)}, u32[]{:S(2)}) collective-permute-start(f32[256,512]{1,0:T(8,128)} %get-tuple-element.370), channel_id=1, source_target_pairs={{0,1},{1,0},{2,3},{3,2},{4,5},{5,4},{6,7},{7,6},{8,9},{9,8},{10,11... | collective-permute-start | bytes 1572872 | tf_op jit(solution)/shard_map/ppermute | solution.py:27
  246.0 31.0 %collective-permute-start.19 = (f32[256,512]{1,0:T(8,128)}, f32[256,512]{1,0:T(8,128)}, u32[]{:S(2)}, u32[]{:S(2)}) collective-permute-start(f32[256,512]{1,0:T(8,128)} %get-tuple-element.369), channel_id=1, source_target_pairs={{0,3},{1,2},{2,1},{3,0},{4,7},{5,6},{6,5},{7,4},{8,11},{9,10},{10,... | collective-permute-start | bytes 1572872 | tf_op jit(solution)/shard_map/ppermute | solution.py:27
  271.6 30.2 %collective-permute-start.22 = (f32[256,512]{1,0:T(8,128)}, f32[256,512]{1,0:T(8,128)}, u32[]{:S(2)}, u32[]{:S(2)}) collective-permute-start(f32[256,512]{1,0:T(8,128)} %get-tuple-element.366), channel_id=1, source_target_pairs={{0,2},{1,3},{2,0},{3,1},{4,6},{5,7},{6,4},{7,5},{8,10},{9,11},{10,... | collective-permute-start | bytes 1572872 | tf_op jit(solution)/shard_map/ppermute | solution.py:27
  300.2 24.2 %collective-permute-start.24 = (f32[256,512]{1,0:T(8,128)S(1)}, f32[256,512]{1,0:T(8,128)S(1)}, u32[]{:S(2)}, u32[]{:S(2)}) collective-permute-start(f32[256,512]{1,0:T(8,128)S(1)} %get-tuple-element.368), channel_id=1, source_target_pairs={{0,3},{1,2},{2,1},{3,0},{4,7},{5,6},{6,5},{7,4},{8,11},{9,10},{10,... | collective-permute-start | bytes 1572872 | tf_op jit(solution)/shard_map/ppermute | solution.py:27
  336.6 389.3 %all-reduce.30.cloned.1.call-start = ((), (), s32[]{:S(2)}) async-start(), calls=%async_computation | async-start | bytes 16777216 | tf_op jit(solution)/shard_map/psum | solution.py:910
  355.0 88.9 %collective-permute-start.29 = (f32[264,512]{1,0:T(8,128)}, f32[264,512]{1,0:T(8,128)}, u32[]{:S(2)}, u32[]{:S(2)}) collective-permute-start(f32[264,512]{1,0:T(8,128)} %pad_maximum_fusion.18), channel_id=1, source_target_pairs={{0,0},{2,1},{4,2},{6,3},{1,4},{3,5},{5,6},{7,7},{8,8},{10,9},{12,1... | collective-permute-start | bytes 1622024 | tf_op jit(solution)/shard_map/ppermute | solution.py:167
  361.7 84.0 %collective-permute-start.30 = (f32[264,512]{1,0:T(8,128)}, f32[264,512]{1,0:T(8,128)}, u32[]{:S(2)}, u32[]{:S(2)}) collective-permute-start(f32[264,512]{1,0:T(8,128)} %pad_maximum_fusion.19), channel_id=1, source_target_pairs={{2,0},{0,1},{6,2},{4,3},{3,4},{1,5},{7,6},{5,7},{10,8},{8,9},{14,1... | collective-permute-start | bytes 1622024 | tf_op jit(solution)/shard_map/ppermute | solution.py:167
  368.3 78.1 %collective-permute-start.31 = (f32[264,512]{1,0:T(8,128)}, f32[264,512]{1,0:T(8,128)}, u32[]{:S(2)}, u32[]{:S(2)}) collective-permute-start(f32[264,512]{1,0:T(8,128)} %pad_maximum_fusion.20), channel_id=1, source_target_pairs={{1,0},{3,1},{5,2},{7,3},{0,4},{2,5},{4,6},{6,7},{9,8},{11,9},{13,1... | collective-permute-start | bytes 1622024 | tf_op jit(solution)/shard_map/ppermute | solution.py:167
  443.9 26.8 %collective-permute-start.37 = (f32[256,1536]{1,0:T(8,128)}, f32[256,1536]{1,0:T(8,128)}, u32[]{:S(2)}, u32[]{:S(2)}) collective-permute-start(f32[256,1536]{1,0:T(8,128)} %fusion.47), channel_id=1, source_target_pairs={{0,4},{4,0},{8,12},{12,8},{16,20},{20,16},{24,28},{28,24},{1,5},{5... | collective-permute-start | bytes 4718600 | tf_op jit(solution)/shard_map/ppermute | solution.py:27
  458.6 36.2 %collective-permute-start.36 = (f32[256,2048]{1,0:T(8,128)}, f32[256,2048]{1,0:T(8,128)}, u32[]{:S(2)}, u32[]{:S(2)}) collective-permute-start(f32[256,2048]{1,0:T(8,128)} %fusion.2), channel_id=1, source_target_pairs={{0,4},{4,0},{8,12},{12,8},{16,20},{20,16},{24,28},{28,24},{1,5},{5... | collective-permute-start | bytes 6291464 | tf_op jit(solution)/shard_map/ppermute | solution.py:27
  467.2 26.8 %collective-permute-start.35 = (f32[256,512]{1,0:T(8,128)S(1)}, f32[256,512]{1,0:T(8,128)S(1)}, u32[]{:S(2)}, u32[]{:S(2)}) collective-permute-start(f32[256,512]{1,0:T(8,128)S(1)} %get-tuple-element.355), channel_id=1, source_target_pairs={{0,2},{1,3},{2,0},{3,1},{4,6},{5,7},{6,4},{7,5},{8,10},{9,11},{10,... | collective-permute-start | bytes 1572872 | tf_op jit(solution)/shard_map/ppermute | solution.py:27
  497.9 24.7 %collective-permute-start.39 = (f32[128,1536]{1,0:T(8,128)}, f32[128,1536]{1,0:T(8,128)}, u32[]{:S(2)}, u32[]{:S(2)}) collective-permute-start(f32[128,1536]{1,0:T(8,128)} %constant_dynamic-slice_fusion.6), channel_id=1, source_target_pairs={{0,16},{4,20},{8,24},{12,28},{16,0},{20,4},{24,8},{28,12},{1,17},{... | collective-permute-start | bytes 2359304 | tf_op jit(solution)/shard_map/ppermute | solution.py:27
  500.4 24.6 %collective-permute-start.38 = (f32[128,2048]{1,0:T(8,128)}, f32[128,2048]{1,0:T(8,128)}, u32[]{:S(2)}, u32[]{:S(2)}) collective-permute-start(f32[128,2048]{1,0:T(8,128)} %constant_dynamic-slice_fusion.7), channel_id=1, source_target_pairs={{0,8},{4,12},{8,0},{12,4},{16,24},{20,28},{24,16},{28,20},{1,9},{5... | collective-permute-start | bytes 3145736 | tf_op jit(solution)/shard_map/ppermute | solution.py:27
  503.0 34.5 %collective-permute-start.40 = (f32[256,512]{1,0:T(8,128)}, f32[256,512]{1,0:T(8,128)}, u32[]{:S(2)}, u32[]{:S(2)}) collective-permute-start(f32[256,512]{1,0:T(8,128)} %get-tuple-element.354), channel_id=1, source_target_pairs={{0,1},{1,0},{2,3},{3,2},{4,5},{5,4},{6,7},{7,6},{8,9},{9,8},{10,11... | collective-permute-start | bytes 1572872 | tf_op jit(solution)/shard_map/ppermute | solution.py:27
  503.0 34.5 %collective-permute-start.41 = (f32[256,512]{1,0:T(8,128)}, f32[256,512]{1,0:T(8,128)}, u32[]{:S(2)}, u32[]{:S(2)}) collective-permute-start(f32[256,512]{1,0:T(8,128)} %get-tuple-element.353), channel_id=1, source_target_pairs={{0,3},{1,2},{2,1},{3,0},{4,7},{5,6},{6,5},{7,4},{8,11},{9,10},{10,... | collective-permute-start | bytes 1572872 | tf_op jit(solution)/shard_map/ppermute | solution.py:27
  541.1 38.1 %collective-permute-start.45 = (f32[32,1536]{1,0:T(8,128)}, f32[32,1536]{1,0:T(8,128)}, u32[]{:S(2)}, u32[]{:S(2)}) collective-permute-start(f32[32,1536]{1,0:T(8,128)} %constant_dynamic-slice_fusion.2), channel_id=1, source_target_pairs={{0,2},{1,3},{2,0},{3,1},{4,6},{5,7},{6,4},{7,5},{8,10},{9,11},{10,... | collective-permute-start | bytes 589832 | tf_op jit(solution)/shard_map/ppermute | solution.py:27
  541.8 39.2 %collective-permute-start.44 = (f32[32,2048]{1,0:T(8,128)}, f32[32,2048]{1,0:T(8,128)}, u32[]{:S(2)}, u32[]{:S(2)}) collective-permute-start(f32[32,2048]{1,0:T(8,128)} %constant_dynamic-slice_fusion.3), channel_id=1, source_target_pairs={{0,2},{1,3},{2,0},{3,1},{4,6},{5,7},{6,4},{7,5},{8,10},{9,11},{10,... | collective-permute-start | bytes 786440 | tf_op jit(solution)/shard_map/ppermute | solution.py:27
  617.8 50.0 %collective-permute-start.55 = (f32[264,512]{1,0:T(8,128)}, f32[264,512]{1,0:T(8,128)}, u32[]{:S(2)}, u32[]{:S(2)}) collective-permute-start(f32[264,512]{1,0:T(8,128)} %pad_maximum_fusion.25), channel_id=1, source_target_pairs={{3,0},{1,1},{7,2},{5,3},{2,4},{0,5},{6,6},{4,7},{11,8},{9,9},{15,1... | collective-permute-start | bytes 1622024 | tf_op jit(solution)/shard_map/ppermute | solution.py:167
  620.7 47.1 %collective-permute-start.54 = (f32[264,512]{1,0:T(8,128)S(1)}, f32[264,512]{1,0:T(8,128)S(1)}, u32[]{:S(2)}, u32[]{:S(2)}) collective-permute-start(f32[264,512]{1,0:T(8,128)S(1)} %pad_maximum_fusion.24), channel_id=1, source_target_pairs={{1,0},{3,1},{5,2},{7,3},{0,4},{2,5},{4,6},{6,7},{9,8},{11,9},{13,1... | collective-permute-start | bytes 1622024 | tf_op jit(solution)/shard_map/ppermute | solution.py:167
  628.9 29.8 %collective-permute-start.59 = (f32[128,1536]{1,0:T(8,128)S(1)}, f32[128,1536]{1,0:T(8,128)S(1)}, u32[]{:S(2)}, u32[]{:S(2)}) collective-permute-start(f32[128,1536]{1,0:T(8,128)S(1)} %constant_dynamic-update-slice_fusion.10), channel_id=1, source_target_pairs={{0,16},{4,20},{8,24},{12,28},{16,0},{20,4},{24,8},{28,12},{1,17},{... | collective-permute-start | bytes 2359304 | tf_op jit(solution)/shard_map/ppermute | solution.py:27
  633.4 34.3 %collective-permute-start.57 = (f32[128,2048]{1,0:T(8,128)}, f32[128,2048]{1,0:T(8,128)S(1)}, u32[]{:S(2)}, u32[]{:S(2)}) collective-permute-start(f32[128,2048]{1,0:T(8,128)} %constant_dynamic-update-slice_fusion.14), channel_id=1, source_target_pairs={{0,8},{4,12},{8,0},{12,4},{16,24},{20,28},{24,16},{28,20},{1,9},{5... | collective-permute-start | bytes 3145736 | tf_op jit(solution)/shard_map/ppermute | solution.py:27
  635.7 32.1 %collective-permute-start.53 = (f32[264,512]{1,0:T(8,128)S(1)}, f32[264,512]{1,0:T(8,128)S(1)}, u32[]{:S(2)}, u32[]{:S(2)}) collective-permute-start(f32[264,512]{1,0:T(8,128)S(1)} %pad_maximum_fusion.23), channel_id=1, source_target_pairs={{2,0},{0,1},{6,2},{4,3},{3,4},{1,5},{7,6},{5,7},{10,8},{8,9},{14,1... | collective-permute-start | bytes 1622024 | tf_op jit(solution)/shard_map/ppermute | solution.py:167
  708.2 22.5 %collective-permute-start.67 = (f32[36,512]{1,0:T(8,128)S(1)}, f32[36,512]{1,0:T(8,128)S(1)}, u32[]{:S(2)}, u32[]{:S(2)}) collective-permute-start(f32[36,512]{1,0:T(8,128)S(1)} %add.882), channel_id=1, source_target_pairs={{0,8},{4,12},{8,0},{12,4},{16,24},{20,28},{24,16},{28,20},{1,9},{5... | collective-permute-start | bytes 221192 | tf_op jit(solution)/shard_map/ppermute | solution.py:27
  (236 other events, 1885.7 us)
Sparse Core Ops, SparseCore 0:
  336.7 125.7 all-reduce.31
  579.2 146.6 all-reduce.29
